TPU v7x, 32 devices: a whole 2x2x4 slice. The times are simulated.
32 devices in a mesh: ctx: 8 (over z, y), wt: 4 (over x, core).
Axes of the slice: x: 2, y: 2, z: 4, core: 2. Of those that a mesh axis runs over, the one named last changes fastest.
Arguments:
- tokens: bfloat16 [5, 1024, 1024], P(None, 'ctx'), may hold values from -6 to 6
- segments: int32 [5, 1024], P(None, 'ctx'), may hold values from 0 to 1023, as said below
- attn_gain: bfloat16 [1024], replicated, may hold values from 0.099609375 to 1.8984375
- w_query: bfloat16 [1024, 1024], P(None, 'wt'), may hold values from -0.1875 to 0.1875
- key_matrix: bfloat16 [1024, 512], P(None, 'wt'), may hold values from -0.1875 to 0.1875
- value_matrix: bfloat16 [1024, 512], P(None, 'wt'), may hold values from -0.1875 to 0.1875
- q_gain: bfloat16 [64], replicated, may hold values from 0.099609375 to 1.8984375
- k_gain: bfloat16 [64], replicated, may hold values from 0.099609375 to 1.8984375
- w_out: bfloat16 [1024, 1024], P(None, 'wt'), may hold values from -0.75 to 0.75
- ffn_gain: bfloat16 [1024], replicated, may hold values from 0.099609375 to 1.8984375
- w_gate: bfloat16 [1024, 4608], P(None, 'wt'), may hold values from -0.1875 to 0.1875
- w_up: bfloat16 [1024, 4608], P(None, 'wt'), may hold values from -0.1875 to 0.1875
- w_down: bfloat16 [1024, 4608], P(None, 'wt'), may hold values from -0.09375 to 0.09375
- cotangent: bfloat16 [5, 1024, 1024], P(None, 'ctx'), may hold values from -6 to 6
Outputs:
- output: bfloat16 [5, 1024, 1024], P(None, 'ctx')
- tokens_grad: bfloat16 [5, 1024, 1024], P(None, 'ctx')
- attn_gain_grad: float32 [1024], replicated
- w_query_grad: float32 [1024, 1024], P('ctx', 'wt')
- w_key_grad: float32 [1024, 512], P('ctx', 'wt')
- w_value_grad: float32 [1024, 512], P('ctx', 'wt')
- q_gain_grad: float32 [64], replicated
- k_gain_grad: float32 [64], replicated
- w_out_grad: float32 [1024, 1024], P('ctx', 'wt')
- ffn_gain_grad: float32 [1024], replicated
- w_gate_grad: float32 [1024, 4608], P('ctx', 'wt')
- w_up_grad: float32 [1024, 4608], P('ctx', 'wt')
- w_down_grad: float32 [1024, 4608], P('ctx', 'wt')
Inputs may be any that keep to these rules, and one draw needn't show every extreme that they name: `segments`: segment numbers are 0 or more and never fall along a sequence; the last document of each sequence is numbered 1024 - 1.
All inputs are finite; a program needn't handle non-finite values.
Results may differ from a plain program's by a relative error of at most 0.03.
Values may be sent and summed in bfloat16 or wider, within the bound.
A program may use at most 192 MiB of HBM per device.

v0:
```python
from functools import partial
import math

import jax
import jax.numpy as jnp
from jax import lax
from jax.sharding import PartitionSpec as P

EPS = 1e-05
THETA = 1000000.0
NEG = -1e30


def carried_in(value, axis, join, neutral):
    count, mine = (lax.axis_size(axis), lax.axis_index(axis))
    pieces = jax.tree.map(lambda part: lax.all_gather(part, axis), value)
    running = jax.tree.map(
        lambda part, zero: jnp.full_like(part, 0) + jnp.asarray(zero, part.dtype), value, neutral
    )

    def step(position, running):
        longer = join(running, jax.tree.map(lambda part: part[position], pieces))
        return jax.tree.map(lambda new, old: jnp.where(position < mine, new, old), longer, running)

    return lax.fori_loop(0, count - 1, step, running)


def product(left, right):
    return jnp.dot(left, right, preferred_element_type=jnp.float32)


def by_transpose(left, right):
    return lax.dot_general(
        left, right, (((1,), (1,)), ((), ())), preferred_element_type=jnp.float32
    )


def transpose_by(left, right):
    return lax.dot_general(
        left, right, (((0,), (0,)), ((), ())), preferred_element_type=jnp.float32
    )


def norm_rows(values, gain):
    inverse = lax.rsqrt(jnp.mean(values * values, axis=-1, keepdims=True) + EPS)
    unit_rows = values * inverse
    return (unit_rows * gain, unit_rows, inverse)


def norm_back(grads, unit_rows, inverse, gain):
    scaled = grads * gain
    return inverse * (scaled - unit_rows * jnp.mean(scaled * unit_rows, axis=-1, keepdims=True))


def rotate(values, cosine_table, sine_table, direction):
    half_dim = values.shape[-1] // 2
    first_half = values[..., :half_dim]
    second_half = values[..., half_dim:]
    return jnp.concatenate(
        [
            first_half * cosine_table - direction * second_half * sine_table,
            second_half * cosine_table + direction * first_half * sine_table,
        ],
        axis=-1,
    )


def chain_starts(earlier, later):
    earlier_seg, prior_start = earlier
    later_seg, later_start = later
    joined = jnp.where(earlier_seg == later_seg, jnp.minimum(prior_start, later_start), later_start)
    return (
        jnp.where(later_seg < 0, earlier_seg, later_seg),
        jnp.where(later_seg < 0, prior_start, joined),
    )


def doc_positions(segments, places):
    same_doc = segments[:, :, None] == segments[:, None, :]
    first_place = jnp.min(jnp.where(same_doc, places[None, None, :], 1 << 30), axis=2)
    identity = (
        jnp.full(segments.shape[:1], -1, jnp.int32),
        jnp.full(segments.shape[:1], 1 << 30, jnp.int32),
    )
    before_seg, before_start = carried_in(
        (segments[:, -1], first_place[:, -1]), "ctx", chain_starts, identity
    )
    starts = jnp.where(
        segments == before_seg[:, None],
        jnp.minimum(first_place, before_start[:, None]),
        first_place,
    )
    return places[None, :] - starts


def split_blocks(array, block_len):
    shaped = array.reshape(
        (array.shape[0], array.shape[1] // block_len, block_len) + array.shape[2:]
    )
    return jnp.moveaxis(shaped, 1, 0)


def attend_piece(folded, pieces, first_row, queries, query_places, query_segs, score_scale):
    key_piece, value_piece, seg_piece = pieces
    sequences, piece_rows = seg_piece.shape
    kv_local = queries.shape[2]
    head_dim = queries.shape[4]
    block_len = math.gcd(piece_rows, 512)
    key_blocks = split_blocks(
        key_piece.reshape(sequences, piece_rows, kv_local, head_dim), block_len
    )
    value_tiles = split_blocks(
        value_piece.reshape(sequences, piece_rows, kv_local, head_dim), block_len
    )
    seg_blocks = split_blocks(seg_piece, block_len)
    offsets = block_len * jnp.arange(piece_rows // block_len, dtype=jnp.int32)

    def attend_block_step(running, block_item):
        row_max, row_sum, weighted = running
        key_block, value_block, seg_block, offset = block_item
        key_places = offset + jnp.arange(block_len, dtype=jnp.int32)
        allowed = (key_places[None, None, :] <= query_places[None, :, None]) & (
            query_segs[:, :, None] == seg_block[:, None, :]
        )
        allowed = allowed[:, None, None]
        scores = (
            jnp.einsum("sqgrd,skgd->sgrqk", queries, key_block, preferred_element_type=jnp.float32)
            * score_scale
        )
        scores = jnp.where(allowed, scores, NEG)
        new_max = jnp.maximum(row_max, jnp.max(scores, axis=-1))
        weights = jnp.where(allowed, jnp.exp(scores - new_max[..., None]), 0.0)
        fading = jnp.exp(row_max - new_max)
        row_sum = row_sum * fading + jnp.sum(weights, axis=-1)
        fade_rows = jnp.transpose(fading, (0, 3, 1, 2))[..., None]
        weighted = weighted * fade_rows + jnp.einsum(
            "sgrqk,skgd->sqgrd",
            weights.astype(jnp.bfloat16),
            value_block,
            preferred_element_type=jnp.float32,
        )
        return ((new_max, row_sum, weighted), None)

    folded, unused = lax.scan(
        attend_block_step, folded, (key_blocks, value_tiles, seg_blocks, offsets)
    )
    return folded


def query_grad_piece(
    folded,
    pieces,
    first_row,
    queries,
    grad_heads,
    log_total,
    row_delta,
    query_places,
    query_segs,
    score_scale,
):
    key_piece, value_piece, seg_piece = pieces
    sequences, piece_rows = seg_piece.shape
    kv_local = queries.shape[2]
    head_dim = queries.shape[4]
    block_len = math.gcd(piece_rows, 512)
    key_blocks = split_blocks(
        key_piece.reshape(sequences, piece_rows, kv_local, head_dim), block_len
    )
    value_tiles = split_blocks(
        value_piece.reshape(sequences, piece_rows, kv_local, head_dim), block_len
    )
    seg_blocks = split_blocks(seg_piece, block_len)
    offsets = block_len * jnp.arange(piece_rows // block_len, dtype=jnp.int32)

    def query_block_step(running, block_item):
        key_block, value_block, seg_block, offset = block_item
        key_places = offset + jnp.arange(block_len, dtype=jnp.int32)
        allowed = (key_places[None, None, :] <= query_places[None, :, None]) & (
            query_segs[:, :, None] == seg_block[:, None, :]
        )
        allowed = allowed[:, None, None]
        scores = (
            jnp.einsum("sqgrd,skgd->sgrqk", queries, key_block, preferred_element_type=jnp.float32)
            * score_scale
        )
        probs = jnp.where(allowed, jnp.exp(scores - log_total[..., None]), 0.0)
        grad_probs = jnp.einsum(
            "sqgrd,skgd->sgrqk", grad_heads, value_block, preferred_element_type=jnp.float32
        )
        grad_scores = (probs * (grad_probs - row_delta[..., None])).astype(jnp.bfloat16)
        running = running + jnp.einsum(
            "sgrqk,skgd->sqgrd", grad_scores, key_block, preferred_element_type=jnp.float32
        )
        return (running, None)

    folded, unused = lax.scan(
        query_block_step, folded, (key_blocks, value_tiles, seg_blocks, offsets)
    )
    return folded


def key_grad_piece(
    folded, pieces, first_row, keys_here, values_here, key_places, key_segs, score_scale
):
    query_piece, grad_piece, total_piece, delta_piece, seg_piece = pieces
    sequences, piece_rows = seg_piece.shape
    kv_local = keys_here.shape[2]
    head_dim = keys_here.shape[3]
    per_group = query_piece.shape[2] // (kv_local * head_dim)
    block_len = math.gcd(piece_rows, 512)
    query_blocks = split_blocks(
        query_piece.reshape(sequences, piece_rows, kv_local, per_group, head_dim), block_len
    )
    grad_blocks = split_blocks(
        grad_piece.reshape(sequences, piece_rows, kv_local, per_group, head_dim), block_len
    )
    total_blocks = split_blocks(
        total_piece.reshape(sequences, piece_rows, kv_local, per_group), block_len
    )
    delta_blocks = split_blocks(
        delta_piece.reshape(sequences, piece_rows, kv_local, per_group), block_len
    )
    seg_blocks = split_blocks(seg_piece, block_len)
    offsets = block_len * jnp.arange(piece_rows // block_len, dtype=jnp.int32)

    def key_block_step(running, block_item):
        grad_keys, grad_values = running
        query_block, grad_block, total_block, delta_block, seg_block, offset = block_item
        query_rows = offset + jnp.arange(block_len, dtype=jnp.int32)
        allowed = (key_places[None, None, :] <= query_rows[None, :, None]) & (
            seg_block[:, :, None] == key_segs[:, None, :]
        )
        allowed = allowed[:, None, None]
        scores = (
            jnp.einsum(
                "sqgrd,skgd->sgrqk", query_block, keys_here, preferred_element_type=jnp.float32
            )
            * score_scale
        )
        total_cols = jnp.transpose(total_block, (0, 2, 3, 1))
        delta_cols = jnp.transpose(delta_block, (0, 2, 3, 1))
        probs = jnp.where(allowed, jnp.exp(scores - total_cols[..., None]), 0.0)
        grad_probs = jnp.einsum(
            "sqgrd,skgd->sgrqk", grad_block, values_here, preferred_element_type=jnp.float32
        )
        grad_scores = (probs * (grad_probs - delta_cols[..., None])).astype(jnp.bfloat16)
        grad_values = grad_values + jnp.einsum(
            "sgrqk,sqgrd->skgd",
            probs.astype(jnp.bfloat16),
            grad_block,
            preferred_element_type=jnp.float32,
        )
        grad_keys = grad_keys + jnp.einsum(
            "sgrqk,sqgrd->skgd", grad_scores, query_block, preferred_element_type=jnp.float32
        )
        return ((grad_keys, grad_values), None)

    folded, unused = lax.scan(
        key_block_step,
        folded,
        (query_blocks, grad_blocks, total_blocks, delta_blocks, seg_blocks, offsets),
    )
    return folded


def on_device(
    tokens,
    segments,
    attn_gain,
    w_query,
    key_matrix,
    value_matrix,
    q_gain,
    k_gain,
    w_out,
    ffn_gain,
    w_gate,
    w_up,
    w_down,
    cotangent,
):
    sequences, seq_rows, model_width = tokens.shape
    head_dim = q_gain.shape[0]
    q_local = w_query.shape[1] // head_dim
    kv_local = key_matrix.shape[1] // head_dim
    per_group = q_local // kv_local
    score_scale = 1.0 / math.sqrt(head_dim)
    all_rows = sequences * seq_rows
    places = lax.axis_index("ctx") * seq_rows + jnp.arange(seq_rows, dtype=jnp.int32)
    positions = doc_positions(segments, places)
    frequency = THETA ** (-jnp.arange(0, head_dim, 2, dtype=jnp.float32) / head_dim)
    angles = positions.astype(jnp.float32)[:, :, None] * frequency
    cosine_table = jnp.cos(angles)[:, :, None, :]
    sine_table = jnp.sin(angles)[:, :, None, :]
    inputs = tokens.astype(jnp.float32).reshape(all_rows, model_width)
    normed, attn_unit, attn_inverse = norm_rows(inputs, attn_gain)
    normed_low = normed.astype(jnp.bfloat16)
    query_raw = product(normed_low, w_query).reshape(sequences, seq_rows, q_local, head_dim)
    key_raw = product(normed_low, key_matrix).reshape(sequences, seq_rows, kv_local, head_dim)
    value_low = (
        product(normed_low, value_matrix)
        .astype(jnp.bfloat16)
        .reshape(sequences, seq_rows, kv_local * head_dim)
    )
    query_normed, query_unit, query_inverse = norm_rows(query_raw, q_gain)
    key_normed, key_unit, key_inverse = norm_rows(key_raw, k_gain)
    query_low = rotate(query_normed, cosine_table, sine_table, 1.0).astype(jnp.bfloat16)
    key_low = rotate(key_normed, cosine_table, sine_table, 1.0).astype(jnp.bfloat16)
    key_flat = key_low.reshape(sequences, seq_rows, kv_local * head_dim)
    query_groups = query_low.reshape(sequences, seq_rows, kv_local, per_group, head_dim)
    attend = partial(
        attend_piece,
        queries=query_groups,
        query_places=places,
        query_segs=segments,
        score_scale=score_scale,
    )
    start_state = (
        jnp.full((sequences, kv_local, per_group, seq_rows), NEG, jnp.float32),
        jnp.zeros((sequences, kv_local, per_group, seq_rows), jnp.float32),
        jnp.zeros((sequences, seq_rows, kv_local, per_group, head_dim), jnp.float32),
    )
    row_max, row_sum, weighted = attend(
        start_state,
        (
            lax.all_gather(key_flat, "ctx", axis=1, tiled=True),
            lax.all_gather(value_low, "ctx", axis=1, tiled=True),
            lax.all_gather(segments, "ctx", axis=1, tiled=True),
        ),
        jnp.int32(0),
    )
    mixed_heads = weighted / jnp.transpose(row_sum, (0, 3, 1, 2))[..., None]
    mixed_low = mixed_heads.astype(jnp.bfloat16).reshape(all_rows, q_local * head_dim)
    attn_term = by_transpose(mixed_low, w_out)
    residual = inputs + lax.psum(attn_term.astype(jnp.bfloat16), "wt").astype(jnp.float32)
    normed_ffn, ffn_unit, ffn_inverse = norm_rows(residual, ffn_gain)
    normed_ffn_low = normed_ffn.astype(jnp.bfloat16)
    gate_proj = product(normed_ffn_low, w_gate)
    up_proj = product(normed_ffn_low, w_up)
    gate_sigmoid = jax.nn.sigmoid(gate_proj)
    gate_silu = gate_proj * gate_sigmoid
    hidden_low = (gate_silu * up_proj).astype(jnp.bfloat16)
    mlp_term = by_transpose(hidden_low, w_down)
    output_rows = (
        residual + lax.psum(mlp_term.astype(jnp.bfloat16), "wt").astype(jnp.float32)
    ).astype(jnp.bfloat16)
    row_max, row_sum, weighted = attend(
        start_state,
        (
            lax.all_gather(key_flat, "ctx", axis=1, tiled=True),
            lax.all_gather(value_low, "ctx", axis=1, tiled=True),
            lax.all_gather(segments, "ctx", axis=1, tiled=True),
        ),
        jnp.int32(0),
    )
    mixed_heads = weighted / jnp.transpose(row_sum, (0, 3, 1, 2))[..., None]
    mixed_low = mixed_heads.astype(jnp.bfloat16).reshape(all_rows, q_local * head_dim)
    log_total = row_max + jnp.log(row_sum)
    grad_rows = cotangent.reshape(all_rows, model_width)
    w_down_grad = transpose_by(grad_rows, hidden_low)
    grad_hidden = product(grad_rows, w_down)
    grad_gate = (
        grad_hidden * up_proj * gate_sigmoid * (1.0 + gate_proj * (1.0 - gate_sigmoid))
    ).astype(jnp.bfloat16)
    grad_up = (grad_hidden * gate_silu).astype(jnp.bfloat16)
    w_gate_grad = transpose_by(normed_ffn_low, grad_gate)
    w_up_grad = transpose_by(normed_ffn_low, grad_up)
    grad_normed_ffn = by_transpose(grad_gate, w_gate) + by_transpose(grad_up, w_up)
    ffn_gain_part = jnp.sum(grad_normed_ffn * ffn_unit, axis=0)
    grad_normed_ffn = lax.psum(grad_normed_ffn.astype(jnp.bfloat16), "wt").astype(jnp.float32)
    grad_residual = grad_rows.astype(jnp.float32) + norm_back(
        grad_normed_ffn, ffn_unit, ffn_inverse, ffn_gain
    )
    grad_residual_low = grad_residual.astype(jnp.bfloat16)
    w_out_grad = transpose_by(grad_residual_low, mixed_low)
    grad_heads_low = product(grad_residual_low, w_out).astype(jnp.bfloat16)
    grad_groups = grad_heads_low.reshape(sequences, seq_rows, kv_local, per_group, head_dim)
    delta_rows = jnp.sum(grad_groups.astype(jnp.float32) * mixed_heads, axis=-1)
    delta_cols = jnp.transpose(delta_rows, (0, 2, 3, 1))
    query_grad_fn = partial(
        query_grad_piece,
        queries=query_groups,
        grad_heads=grad_groups,
        log_total=log_total,
        row_delta=delta_cols,
        query_places=places,
        query_segs=segments,
        score_scale=score_scale,
    )
    grad_query = query_grad_fn(
        jnp.zeros((sequences, seq_rows, kv_local, per_group, head_dim), jnp.float32),
        (
            lax.all_gather(key_flat, "ctx", axis=1, tiled=True),
            lax.all_gather(value_low, "ctx", axis=1, tiled=True),
            lax.all_gather(segments, "ctx", axis=1, tiled=True),
        ),
        jnp.int32(0),
    )
    key_grad_fn = partial(
        key_grad_piece,
        keys_here=key_low,
        values_here=value_low.reshape(sequences, seq_rows, kv_local, head_dim),
        key_places=places,
        key_segs=segments,
        score_scale=score_scale,
    )
    total_rows = jnp.transpose(log_total, (0, 3, 1, 2)).reshape(sequences, seq_rows, q_local)
    zero_keys = jnp.zeros((sequences, seq_rows, kv_local, head_dim), jnp.float32)
    grad_key, grad_value = key_grad_fn(
        (zero_keys, zero_keys),
        (
            lax.all_gather(
                query_low.reshape(sequences, seq_rows, q_local * head_dim),
                "ctx",
                axis=1,
                tiled=True,
            ),
            lax.all_gather(
                grad_heads_low.reshape(sequences, seq_rows, q_local * head_dim),
                "ctx",
                axis=1,
                tiled=True,
            ),
            lax.all_gather(total_rows.astype(jnp.bfloat16), "ctx", axis=1, tiled=True).astype(
                jnp.float32
            ),
            lax.all_gather(
                delta_rows.reshape(sequences, seq_rows, q_local).astype(jnp.bfloat16),
                "ctx",
                axis=1,
                tiled=True,
            ).astype(jnp.float32),
            lax.all_gather(segments, "ctx", axis=1, tiled=True),
        ),
        jnp.int32(0),
    )
    grad_query = rotate(
        grad_query.reshape(sequences, seq_rows, q_local, head_dim) * score_scale,
        cosine_table,
        sine_table,
        -1.0,
    )
    grad_key = rotate(grad_key * score_scale, cosine_table, sine_table, -1.0)
    q_gain_part = jnp.sum(grad_query * query_unit, axis=(0, 1, 2))
    k_gain_part = jnp.sum(grad_key * key_unit, axis=(0, 1, 2))
    grad_query_low = (
        norm_back(grad_query, query_unit, query_inverse, q_gain)
        .astype(jnp.bfloat16)
        .reshape(all_rows, q_local * head_dim)
    )
    grad_key_low = (
        norm_back(grad_key, key_unit, key_inverse, k_gain)
        .astype(jnp.bfloat16)
        .reshape(all_rows, kv_local * head_dim)
    )
    grad_value_low = grad_value.astype(jnp.bfloat16).reshape(all_rows, kv_local * head_dim)
    w_query_grad = transpose_by(normed_low, grad_query_low)
    w_key_grad = transpose_by(normed_low, grad_key_low)
    w_value_grad = transpose_by(normed_low, grad_value_low)
    grad_normed = (
        by_transpose(grad_query_low, w_query)
        + by_transpose(grad_key_low, key_matrix)
        + by_transpose(grad_value_low, value_matrix)
    )
    attn_gain_part = jnp.sum(grad_normed * attn_unit, axis=0)
    grad_normed = lax.psum(grad_normed.astype(jnp.bfloat16), "wt").astype(jnp.float32)
    tokens_rows = (
        grad_residual + norm_back(grad_normed, attn_unit, attn_inverse, attn_gain)
    ).astype(jnp.bfloat16)
    output = output_rows.reshape(sequences, seq_rows, model_width)
    tokens_grad = tokens_rows.reshape(sequences, seq_rows, model_width)
    w_query_grad, w_key_grad, w_value_grad, w_out_grad, w_gate_grad, w_up_grad, w_down_grad = (
        lax.psum_scatter(w_query_grad, "ctx", scatter_dimension=0, tiled=True),
        lax.psum_scatter(w_key_grad, "ctx", scatter_dimension=0, tiled=True),
        lax.psum_scatter(w_value_grad, "ctx", scatter_dimension=0, tiled=True),
        lax.psum_scatter(w_out_grad, "ctx", scatter_dimension=0, tiled=True),
        lax.psum_scatter(w_gate_grad, "ctx", scatter_dimension=0, tiled=True),
        lax.psum_scatter(w_up_grad, "ctx", scatter_dimension=0, tiled=True),
        lax.psum_scatter(w_down_grad, "ctx", scatter_dimension=0, tiled=True),
    )
    attn_gain_grad, q_gain_grad, k_gain_grad, ffn_gain_grad = lax.psum(
        (attn_gain_part, q_gain_part, k_gain_part, ffn_gain_part), ("ctx", "wt")
    )
    return (
        output,
        tokens_grad,
        attn_gain_grad,
        w_query_grad,
        w_key_grad,
        w_value_grad,
        q_gain_grad,
        k_gain_grad,
        w_out_grad,
        ffn_gain_grad,
        w_gate_grad,
        w_up_grad,
        w_down_grad,
    )


def solution(mesh):
    in_specs = (
        P(None, "ctx", None),
        P(None, "ctx"),
        P(),
        P(None, "wt"),
        P(None, "wt"),
        P(None, "wt"),
        P(),
        P(),
        P(None, "wt"),
        P(),
        P(None, "wt"),
        P(None, "wt"),
        P(None, "wt"),
        P(None, "ctx", None),
    )
    out_specs = (
        P(None, "ctx", None),
        P(None, "ctx", None),
        P(),
        P("ctx", "wt"),
        P("ctx", "wt"),
        P("ctx", "wt"),
        P(),
        P(),
        P("ctx", "wt"),
        P(),
        P("ctx", "wt"),
        P("ctx", "wt"),
        P("ctx", "wt"),
    )
    return jax.shard_map(
        on_device, mesh=mesh, in_specs=in_specs, out_specs=out_specs, check_vma=False
    )
```

profile of v0, /device:TPU:0, one launch (start us, length us, event | category | flops | bytes accessed | tf_op | source)
XLA Modules:
  0.0 1050.5 jit_solution(4892683801340686765)
XLA Ops:
  11.9 13.1 %all-reduce.2 = (s32[40]{0:T(128)S(1)}, s32[40]{0:T(128)S(1)}) all-reduce(s32[40]{0:T(128)S(1)} %dynamic-update-slice, s32[40]{0:T(128)S(1)} %dynamic-update-slice.1), channel_id=2, replica_groups=mesh['ctx'=8,'wt'=4] {'ctx'}, use_global_device_ids=true, to_apply=%add | all-reduce | flops 80 | bytes 640
  39.5 30.8 %all_gather.34 = s32[5,1024]{1,0:T(8,128)S(1)} all-gather(s32[5,128]{1,0:T(8,128)S(1)} %copy-done.22), channel_id=1, replica_groups=mesh['ctx'=8,'wt'=4] {'ctx'}, dimensions={1}, use_global_device_ids=true | all-gather | bytes 23040 | tf_op jit(solution)/shard_map/all_gather | solution.py:329
  76.1 4.4 reshape_reshape.27
  83.1 35.6 %all-gather.9.cloned.1.call-done = bf16[5,1024,128]{1,2,0:T(8,128)(2,1)} async-done(((bf16[5,128,128]{1,2,0:T(8,128)(2,1)}), bf16[5,1024,128]{1,2,0:T(8,128)(2,1)}) %all-gather.9.cloned.1.call-update) | async-done | bytes 1310736 | tf_op jit(solution)/shard_map/all_gather | solution.py:328
  118.7 4.4 reshape_reshape.28
  125.7 25.6 %while.62 = (s32[]{:T(128)}, f32[5,2,2,128]{3,2,1,0:T(2,128)S(1)}, f32[5,2,2,128]{3,2,1,0:T(2,128)S(1)}, f32[5,128,2,2,64]{1,4,3,2,0:T(8,128)}, s32[2]{0:T(128)S...) while((s32[]{:T(128)}, f32[5,2,2,128]{3,2,1,0:T(2,128)S(1)}, ...), condition=%wide.region_9.10_spmd.clone, body=%wide.region_6.9_spmd.clone.sunk | while | flops 353812096 | bytes 41294520 | solution.py:144
  127.7 4.4 fusion.239
  132.1 5.0 fusion.243
  140.4 4.4 fusion.239
  144.9 5.1 fusion.243
  157.4 37.1 %all-reduce.9.cloned.1.call-done = bf16[640,1024]{1,0:T(8,128)(2,1)} async-done(((bf16[640,1024]{1,0:T(8,128)(2,1)}), bf16[640,1024]{1,0:T(8,128)(2,1)}) %all-reduce.9.cloned.1.call-update) | async-done | bytes 1310736 | tf_op jit(solution)/shard_map/psum | solution.py:336
  202.6 3.6 multiply_convert_fusion
  208.1 3.8 fusion.169
  216.1 20.9 %all_gather.40 = bf16[5,1024,4]{1,2,0:T(4,128)(2,1)S(1)} all-gather(bf16[5,128,4]{1,2,0:T(4,128)(2,1)S(1)} %bitcast.469), channel_id=1, replica_groups=mesh['ctx'=8,'wt'=4] {'ctx'}, dimensions={1}, use_global_device_ids=true | all-gather | bytes 46080 | tf_op jit(solution)/shard_map/all_gather | solution.py:425
  237.7 4.5 convolution_convert_fusion.1
  242.2 9.0 all-reduce.11.cloned.1.call-done
  251.2 4.0 multiply_reduce_fusion
  262.3 26.1 %while.63 = (s32[]{:T(128)}, f32[5,128,2,2,64]{1,4,3,2,0:T(8,128)}, bf16[2,5,512,2,64]{2,4,3,1,0:T(8,128)(2,1)}, s32[2]{0:T(128)}, s32[5,128]{1,0:T(8,128)S(1)},...) while((s32[]{:T(128)}, f32[5,128,2,2,64]{1,4,3,2,0:T(8,128)}, ...), condition=%wide.region_17.18_spmd.clone, body=%wide.region_16.17_spmd.clone.sunk | while | flops 512230016 | bytes 20589848 | solution.py:197
  265.0 4.4 fusion.250
  269.4 5.1 fusion.251
  277.9 4.4 fusion.250
  282.3 5.2 fusion.251
  291.9 21.1 %all_gather.42 = bf16[5,1024,4]{1,2,0:T(4,128)(2,1)S(1)} all-gather(bf16[5,128,4]{1,2,0:T(4,128)(2,1)S(1)} %copy.132), channel_id=1, replica_groups=mesh['ctx'=8,'wt'=4] {'ctx'}, dimensions={1}, use_global_device_ids=true | all-gather | bytes 46080 | tf_op jit(solution)/shard_map/all_gather | solution.py:428
  313.7 5.5 reshape_reshape.29
  319.2 3.9 copy.133
  323.1 45.5 %all-gather.13.cloned.1.call-done = bf16[5,1024,256]{1,2,0:T(8,128)(2,1)} async-done(((bf16[5,128,256]{1,2,0:T(8,128)(2,1)}), bf16[5,1024,256]{1,2,0:T(8,128)(2,1)}) %all-gather.13.cloned.1.call-update) | async-done | bytes 2621456 | tf_op jit(solution)/shard_map/all_gather | solution.py:419
  368.6 5.5 reshape_reshape.31
  374.1 3.9 copy.135
  378.1 38.3 %while.64 = (s32[]{:T(128)}, f32[5,128,2,64]{1,3,2,0:T(8,128)}, f32[5,128,2,64]{1,3,2,0:T(8,128)}, bf16[2,5,512,2,2,64]{2,5,4,3,1,0:T(8,128)(2,1)}, s32[2]{0:T(1...) while((s32[]{:T(128)}, f32[5,128,2,64]{1,3,2,0:T(8,128)}, ...), condition=%wide.region_20.21_spmd.clone, body=%wide.region_19.20_spmd.clone.sunk | while | flops 685245056 | bytes 24870636 | solution.py:259
  380.0 4.7 fusion.260
  384.8 7.7 fusion.261
  392.6 4.6 fusion.262
  399.1 4.7 fusion.260
  404.0 7.7 fusion.261
  411.7 4.7 fusion.262
  423.0 5.9 convolution_bitcast_fusion
  441.4 6.2 fusion.174
  447.6 6.2 fusion.175
  453.8 27.6 %all-reduce.13.cloned.1.call-done = (bf16[640,1024]{1,0:T(8,128)(2,1)}, bf16[640,1024]{1,0:T(8,128)(2,1)}) async-done(((bf16[640,1024]{1,0:T(8,128)(2,1)}, bf16[640,1024]{1,0:T(8,128)(2,1)}), (bf16[640,1024]{1,0:T(8,128)(2,1)}, bf16[640,1024]{1,0:T(8,128)(2,1)})) %all-reduce.13.cloned.1.call-update) | async-done | bytes 2621456 | tf_op jit(solution)/shard_map/psum | solution.py:346
  484.4 42.1 %all-reduce.3 = (f32[1024]{0:T(1024)}, f32[64]{0:T(128)}, f32[64]{0:T(128)}, f32[1024]{0:T(1024)}) all-reduce(f32[1024]{0:T(1024)S(1)} %get-tuple-element.713, f32[64]{0:T(128)S(1)} %copy-done.59, f32[64]{0:T(128)S(1)} %get-tuple-element.715, f32[1024]{0:T(1024)S(1)} %get-tuple-element.709), channel_id=1, replica_groups=mesh['ctx'=8,'wt'=4] {'ctx','wt'}, use_global_device_ids=true, to_apply=%region_25.26 | all-reduce | flops 2176 | bytes 17408 | tf_op jit(solution)/shard_map/psum | solution.py:482
  526.5 6.2 fusion.129
  532.7 49.3 %reduce-scatter.20.cloned.1.call-done = f32[128,1152]{0,1:T(8,128)} async-done(((f32[1024,1152]{0,1:T(8,128)}), f32[128,1152]{0,1:T(8,128)}) %reduce-scatter.20.cloned.1.call-update) | async-done | bytes 589840 | tf_op jit(solution)/shard_map/reduce_scatter | solution.py:480
  584.1 65.2 %reduce-scatter.8.cloned.1.call-done = f32[128,256]{1,0:T(8,128)} async-done(((f32[1024,256]{1,0:T(8,128)}), f32[128,256]{1,0:T(8,128)}) %reduce-scatter.8.cloned.1.call-update) | async-done | bytes 131088 | tf_op jit(solution)/shard_map/reduce_scatter | solution.py:474
  649.3 66.8 %reduce-scatter.14.cloned.1.call-done = f32[128,256]{1,0:T(8,128)} async-done(((f32[1024,256]{1,0:T(8,128)}), f32[128,256]{1,0:T(8,128)}) %reduce-scatter.14.cloned.1.call-update) | async-done | bytes 131088 | tf_op jit(solution)/shard_map/reduce_scatter | solution.py:477
  716.1 64.8 %reduce-scatter.10.cloned.1.call-done = f32[128,128]{1,0:T(8,128)} async-done(((f32[1024,128]{1,0:T(8,128)}), f32[128,128]{1,0:T(8,128)}) %reduce-scatter.10.cloned.1.call-update) | async-done | bytes 65552 | tf_op jit(solution)/shard_map/reduce_scatter | solution.py:475
  780.9 65.1 %reduce-scatter.12.cloned.1.call-done = f32[128,128]{1,0:T(8,128)} async-done(((f32[1024,128]{1,0:T(8,128)}), f32[128,128]{1,0:T(8,128)}) %reduce-scatter.12.cloned.1.call-update) | async-done | bytes 65552 | tf_op jit(solution)/shard_map/reduce_scatter | solution.py:476
  846.0 98.5 %reduce-scatter.16.cloned.1.call-done = f32[128,1152]{1,0:T(8,128)} async-done(((f32[1024,1152]{1,0:T(8,128)}), f32[128,1152]{1,0:T(8,128)}) %reduce-scatter.16.cloned.1.call-update) | async-done | bytes 589840 | tf_op jit(solution)/shard_map/reduce_scatter | solution.py:478
  944.6 99.1 %reduce-scatter.18.cloned.1.call-done = f32[128,1152]{1,0:T(8,128)} async-done(((f32[1024,1152]{1,0:T(8,128)}), f32[128,1152]{1,0:T(8,128)}) %reduce-scatter.18.cloned.1.call-update) | async-done | bytes 589840 | tf_op jit(solution)/shard_map/reduce_scatter | solution.py:479
  (337 shorter events, 102.5 us)
Async XLA Ops:
  7.2 195.4 %copy-start = (bf16[1024,1152]{1,0:T(8,128)(2,1)S(1)}, bf16[1024,1152]{1,0:T(8,128)(2,1)}, u32[]{:S(2)}) copy-start(bf16[1024,1152]{1,0:T(8,128)(2,1)} %param.34) | copy-start | bytes 7077892
  7.2 68.9 %all-gather.7.cloned.1.call-start = ((), (), s32[]{:S(2)}) async-start(), calls=%async_computation.7 | async-start | bytes 1474560 | tf_op jit(solution)/shard_map/all_gather | solution.py:327
  26.1 8.3 copy-start.43
  27.7 4.6 copy-start.63
  27.8 4.6 copy-start.22
  27.8 6.6 copy-start.47
  33.5 39.2 %copy-start.20 = (f32[5,128,32]{1,2,0:T(8,128)}, f32[5,128,32]{1,2,0:T(8,128)S(1)}, u32[]{:S(2)}) copy-start(f32[5,128,32]{1,2,0:T(8,128)S(1)} %get-tuple-element.834) | copy-start | bytes 245764
  33.6 4.9 copy-start.17
  34.4 84.3 %all-gather.9.cloned.1.call-start = ((), (), s32[]{:S(2)}) async-start(), calls=%async_computation.8 | async-start | bytes 1474560 | tf_op jit(solution)/shard_map/all_gather | solution.py:328
  34.4 5.1 copy-start.64
  38.4 156.1 %all-reduce.9.cloned.1.call-start = ((), (), s32[]{:S(2)}) async-start(), calls=%async_computation.9 | async-start | bytes 2621440 | tf_op jit(solution)/shard_map/psum | solution.py:336
  39.5 33.8 %copy-start.55 = (f32[64]{0:T(128)}, f32[64]{0:T(128)S(1)}, u32[]{:S(2)}) copy-start(f32[64]{0:T(128)S(1)} %convert_element_type.154) | copy-start | bytes 772
  72.8 10.3 copy-start.23
  72.8 10.3 copy-start.25
  132.1 5.0 copy-start.2
  144.9 5.1 copy-start.2
  151.4 6.0 copy-start.60
  156.8 94.3 %all-reduce.11.cloned.1.call-start = ((), (), s32[]{:S(2)}) async-start(), calls=%async_computation.10 | async-start | bytes 2621440 | tf_op jit(solution)/shard_map/psum | solution.py:371
  157.4 40.1 %copy-start.49 = (f32[1024]{0:T(1024)}, f32[1024]{0:T(1024)S(1)}, u32[]{:S(2)}) copy-start(f32[1024]{0:T(1024)S(1)} %convert_element_type.160) | copy-start | bytes 12292
  212.0 101.7 %all-gather.11.cloned.1.call-start = ((), (), s32[]{:S(2)}) async-start(), calls=%async_computation.11 | async-start | bytes 2949120 | tf_op jit(solution)/shard_map/all_gather | solution.py:413
  212.8 155.7 %all-gather.13.cloned.1.call-start = ((), (), s32[]{:S(2)}) async-start(), calls=%async_computation.12 | async-start | bytes 2949120 | tf_op jit(solution)/shard_map/all_gather | solution.py:419
  237.7 13.4 %copy-start.50 = (f32[1024]{0:T(1024)S(1)}, f32[1024]{0:T(1024)}, u32[]{:S(2)}) copy-start(f32[1024]{0:T(1024)} %copy-done.49) | copy-start | bytes 12292
  237.7 13.4 %copy-start.52 = (f32[640]{0:T(1024)S(1)}, f32[640]{0:T(1024)}, u32[]{:S(2)}) copy-start(f32[640]{0:T(1024)} %copy-done.51) | copy-start | bytes 7684
  251.1 4.4 copy-start.29
  262.3 219.2 %all-reduce.13.cloned.1.call-start = ((), (), s32[]{:S(2)}) async-start(), calls=%async_computation.20 | async-start | bytes 5242880 | tf_op jit(solution)/shard_map/psum | solution.py:346
  264.9 4.4 copy-start.35
  265.0 4.4 copy-start.53
  265.0 4.4 copy-start.54
  277.9 4.4 copy-start.35
  277.9 4.4 copy-start.53
  378.0 39.4 %copy-start.21 = (f32[5,128,32]{1,2,0:T(8,128)S(1)}, f32[5,128,32]{1,2,0:T(8,128)}, u32[]{:S(2)}) copy-start(f32[5,128,32]{1,2,0:T(8,128)} %copy-done.20) | copy-start | bytes 245764
  378.0 40.4 %copy-start.13 = (f32[5,128,2,64]{1,3,2,0:T(8,128)S(1)}, f32[5,128,2,64]{1,3,2,0:T(8,128)}, u32[]{:S(2)}) copy-start(f32[5,128,2,64]{1,3,2,0:T(8,128)} %copy-done.12) | copy-start | bytes 983044
  378.0 40.4 %copy-start.46 = (f32[5,128,2]{1,2,0:T(2,128)S(1)}, f32[5,128,2]{1,2,0:T(2,128)}, u32[]{:S(2)}) copy-start(f32[5,128,2]{1,2,0:T(2,128)} %copy-done.45) | copy-start | bytes 15364
  378.1 40.4 %copy-start.58 = (f32[64]{0:T(128)S(1)}, f32[64]{0:T(128)}, u32[]{:S(2)}) copy-start(f32[64]{0:T(128)} %copy-done.57) | copy-start | bytes 772
  380.0 4.7 copy-start.33
  380.0 4.7 copy-start.34
  399.1 4.7 copy-start.33
  399.1 4.7 copy-start.34
  423.0 158.9 %reduce-scatter.20.cloned.1.call-start = ((), (), s32[]{:S(2)}) async-start(), calls=%async_computation.19 | async-start | bytes 5308416 | tf_op jit(solution)/shard_map/reduce_scatter | solution.py:480
  429.0 220.3 %reduce-scatter.8.cloned.1.call-start = ((), (), s32[]{:S(2)}) async-start(), calls=%async_computation.13 | async-start | bytes 1179648 | tf_op jit(solution)/shard_map/reduce_scatter | solution.py:474
  432.3 283.8 %reduce-scatter.14.cloned.1.call-start = ((), (), s32[]{:S(2)}) async-start(), calls=%async_computation.16 | async-start | bytes 1179648 | tf_op jit(solution)/shard_map/reduce_scatter | solution.py:477
  435.8 345.2 %reduce-scatter.10.cloned.1.call-start = ((), (), s32[]{:S(2)}) async-start(), calls=%async_computation.14 | async-start | bytes 589824 | tf_op jit(solution)/shard_map/reduce_scatter | solution.py:475
  438.5 407.5 %reduce-scatter.12.cloned.1.call-start = ((), (), s32[]{:S(2)}) async-start(), calls=%async_computation.15 | async-start | bytes 589824 | tf_op jit(solution)/shard_map/reduce_scatter | solution.py:476
  441.3 503.3 %reduce-scatter.16.cloned.1.call-start = ((), (), s32[]{:S(2)}) async-start(), calls=%async_computation.17 | async-start | bytes 5308416 | tf_op jit(solution)/shard_map/reduce_scatter | solution.py:478
  447.6 596.1 %reduce-scatter.18.cloned.1.call-start = ((), (), s32[]{:S(2)}) async-start(), calls=%async_computation.18 | async-start | bytes 5308416 | tf_op jit(solution)/shard_map/reduce_scatter | solution.py:479
  453.8 27.6 %copy-start.44 = (f32[1024]{0:T(1024)S(1)}, f32[1024]{0:T(1024)}, u32[]{:S(2)}) copy-start(f32[1024]{0:T(1024)} %copy-done.43) | copy-start | bytes 12292
  453.8 27.6 %copy-start.48 = (f32[640]{0:T(1024)S(1)}, f32[640]{0:T(1024)}, u32[]{:S(2)}) copy-start(f32[640]{0:T(1024)} %copy-done.47) | copy-start | bytes 7684
  526.5 517.2 %copy-start.1 = (bf16[1024,1152]{1,0:T(8,128)(2,1)S(1)}, bf16[1024,1152]{1,0:T(8,128)(2,1)}, u32[]{:S(2)}) copy-start(bf16[1024,1152]{1,0:T(8,128)(2,1)} %param.34) | copy-start | bytes 7077892
  (42 other events, 88.6 us)
Sparse Core Ops, SparseCore 0:
  34.5 41.5 all-gather.6
  78.7 39.9 all-gather.8
  156.9 37.5 all-reduce.8
  212.1 38.9 all-reduce.10
  253.6 57.2 all-gather.10
  313.4 55.1 all-gather.12
  423.1 58.2 all-reduce.12
  485.1 96.7 reduce-scatter.19
  585.9 63.2 reduce-scatter.7
  653.5 62.5 reduce-scatter.13
  720.0 60.8 reduce-scatter.9
  785.1 60.8 reduce-scatter.11
  850.2 94.2 reduce-scatter.15
  948.6 94.9 reduce-scatter.17
where the time goes:
time: 1060 us; the launch traced here: 1050 us
  waiting for transfers between devices  667 us (63%)
  matrix products  130 us (12%)
  blocking collectives  128 us (12%)
  local copies, waits for them, and re-layouts  60.5 us (6%)
  other arithmetic  47.1 us (4%)
  between operations  15.8 us (1%)
    reduce_scatter x1, waiting for transfers between devices, on_device(): lax.psum_scatter(w_up_grad, 'ctx', scatter_dimension=0, tiled=True)  99.1 us
    reduce_scatter x1, waiting for transfers between devices, on_device(): lax.psum_scatter(w_gate_grad, 'ctx', scatter_dimension=0, tiled=True)  98.5 us
    reduce_scatter x1, waiting for transfers between devices, on_device(): lax.psum_scatter(w_out_grad, 'ctx', scatter_dimension=0, tiled=True)  66.8 us
    reduce_scatter x1, waiting for transfers between devices, on_device(): lax.psum_scatter(w_query_grad, 'ctx', scatter_dimension=0, tiled=True)  65.2 us
    reduce_scatter x1, waiting for transfers between devices, on_device(): lax.psum_scatter(w_value_grad, 'ctx', scatter_dimension=0, tiled=True)  65.1 us
    reduce_scatter x1, waiting for transfers between devices, on_device(): lax.psum_scatter(w_key_grad, 'ctx', scatter_dimension=0, tiled=True)  64.8 us
    reduce_scatter x1, waiting for transfers between devices, on_device(): lax.psum_scatter(w_down_grad, 'ctx', scatter_dimension=0, tiled=True)  49.3 us
    all_gather x1, waiting for transfers between devices, on_device(): lax.all_gather(grad_heads_low.reshape(sequences, seq_rows, q_local * head...  45.5 us
  transfers between devices with their start and end apart: 14, of which 13 were waited for; matrix products, arithmetic and copies ran while one was open for 11% of the time, Pallas kernels for 0%

commit v1 on v0

--- a/solution.py
+++ b/solution.py
@@ -9,20 +9,6 @@
 EPS = 1e-05
 THETA = 1000000.0
 NEG = -1e30
-
-
-def carried_in(value, axis, join, neutral):
-    count, mine = (lax.axis_size(axis), lax.axis_index(axis))
-    pieces = jax.tree.map(lambda part: lax.all_gather(part, axis), value)
-    running = jax.tree.map(
-        lambda part, zero: jnp.full_like(part, 0) + jnp.asarray(zero, part.dtype), value, neutral
-    )
-
-    def step(position, running):
-        longer = join(running, jax.tree.map(lambda part: part[position], pieces))
-        return jax.tree.map(lambda new, old: jnp.where(position < mine, new, old), longer, running)
-
-    return lax.fori_loop(0, count - 1, step, running)
 
 
 def product(left, right):
@@ -63,34 +49,6 @@
         ],
         axis=-1,
     )
-
-
-def chain_starts(earlier, later):
-    earlier_seg, prior_start = earlier
-    later_seg, later_start = later
-    joined = jnp.where(earlier_seg == later_seg, jnp.minimum(prior_start, later_start), later_start)
-    return (
-        jnp.where(later_seg < 0, earlier_seg, later_seg),
-        jnp.where(later_seg < 0, prior_start, joined),
-    )
-
-
-def doc_positions(segments, places):
-    same_doc = segments[:, :, None] == segments[:, None, :]
-    first_place = jnp.min(jnp.where(same_doc, places[None, None, :], 1 << 30), axis=2)
-    identity = (
-        jnp.full(segments.shape[:1], -1, jnp.int32),
-        jnp.full(segments.shape[:1], 1 << 30, jnp.int32),
-    )
-    before_seg, before_start = carried_in(
-        (segments[:, -1], first_place[:, -1]), "ctx", chain_starts, identity
-    )
-    starts = jnp.where(
-        segments == before_seg[:, None],
-        jnp.minimum(first_place, before_start[:, None]),
-        first_place,
-    )
-    return places[None, :] - starts
 
 
 def split_blocks(array, block_len):
@@ -147,7 +105,7 @@
     return folded
 
 
-def query_grad_piece(
+def grad_piece(
     folded,
     pieces,
     first_row,
@@ -173,7 +131,7 @@
     seg_blocks = split_blocks(seg_piece, block_len)
     offsets = block_len * jnp.arange(piece_rows // block_len, dtype=jnp.int32)
 
-    def query_block_step(running, block_item):
+    def grad_block_step(running, block_item):
         key_block, value_block, seg_block, offset = block_item
         key_places = offset + jnp.arange(block_len, dtype=jnp.int32)
         allowed = (key_places[None, None, :] <= query_places[None, :, None]) & (
@@ -192,76 +150,22 @@
         running = running + jnp.einsum(
             "sgrqk,skgd->sqgrd", grad_scores, key_block, preferred_element_type=jnp.float32
         )
-        return (running, None)
-
-    folded, unused = lax.scan(
-        query_block_step, folded, (key_blocks, value_tiles, seg_blocks, offsets)
-    )
-    return folded
-
-
-def key_grad_piece(
-    folded, pieces, first_row, keys_here, values_here, key_places, key_segs, score_scale
-):
-    query_piece, grad_piece, total_piece, delta_piece, seg_piece = pieces
-    sequences, piece_rows = seg_piece.shape
-    kv_local = keys_here.shape[2]
-    head_dim = keys_here.shape[3]
-    per_group = query_piece.shape[2] // (kv_local * head_dim)
-    block_len = math.gcd(piece_rows, 512)
-    query_blocks = split_blocks(
-        query_piece.reshape(sequences, piece_rows, kv_local, per_group, head_dim), block_len
-    )
-    grad_blocks = split_blocks(
-        grad_piece.reshape(sequences, piece_rows, kv_local, per_group, head_dim), block_len
-    )
-    total_blocks = split_blocks(
-        total_piece.reshape(sequences, piece_rows, kv_local, per_group), block_len
-    )
-    delta_blocks = split_blocks(
-        delta_piece.reshape(sequences, piece_rows, kv_local, per_group), block_len
-    )
-    seg_blocks = split_blocks(seg_piece, block_len)
-    offsets = block_len * jnp.arange(piece_rows // block_len, dtype=jnp.int32)
-
-    def key_block_step(running, block_item):
-        grad_keys, grad_values = running
-        query_block, grad_block, total_block, delta_block, seg_block, offset = block_item
-        query_rows = offset + jnp.arange(block_len, dtype=jnp.int32)
-        allowed = (key_places[None, None, :] <= query_rows[None, :, None]) & (
-            seg_block[:, :, None] == key_segs[:, None, :]
-        )
-        allowed = allowed[:, None, None]
-        scores = (
-            jnp.einsum(
-                "sqgrd,skgd->sgrqk", query_block, keys_here, preferred_element_type=jnp.float32
-            )
-            * score_scale
-        )
-        total_cols = jnp.transpose(total_block, (0, 2, 3, 1))
-        delta_cols = jnp.transpose(delta_block, (0, 2, 3, 1))
-        probs = jnp.where(allowed, jnp.exp(scores - total_cols[..., None]), 0.0)
-        grad_probs = jnp.einsum(
-            "sqgrd,skgd->sgrqk", grad_block, values_here, preferred_element_type=jnp.float32
-        )
-        grad_scores = (probs * (grad_probs - delta_cols[..., None])).astype(jnp.bfloat16)
-        grad_values = grad_values + jnp.einsum(
+        grad_keys = jnp.einsum(
+            "sgrqk,sqgrd->skgd", grad_scores, queries, preferred_element_type=jnp.float32
+        )
+        grad_values = jnp.einsum(
             "sgrqk,sqgrd->skgd",
             probs.astype(jnp.bfloat16),
-            grad_block,
+            grad_heads,
             preferred_element_type=jnp.float32,
         )
-        grad_keys = grad_keys + jnp.einsum(
-            "sgrqk,sqgrd->skgd", grad_scores, query_block, preferred_element_type=jnp.float32
-        )
-        return ((grad_keys, grad_values), None)
-
-    folded, unused = lax.scan(
-        key_block_step,
-        folded,
-        (query_blocks, grad_blocks, total_blocks, delta_blocks, seg_blocks, offsets),
-    )
-    return folded
+        grads = jnp.stack([grad_keys, grad_values], axis=2).astype(jnp.bfloat16)
+        return (running, grads)
+
+    folded, grads = lax.scan(
+        grad_block_step, folded, (key_blocks, value_tiles, seg_blocks, offsets)
+    )
+    return folded, jnp.moveaxis(grads, 0, 1).reshape((sequences, piece_rows) + grads.shape[3:])
 
 
 def on_device(
@@ -288,9 +192,8 @@
     score_scale = 1.0 / math.sqrt(head_dim)
     all_rows = sequences * seq_rows
     places = lax.axis_index("ctx") * seq_rows + jnp.arange(seq_rows, dtype=jnp.int32)
-    positions = doc_positions(segments, places)
     frequency = THETA ** (-jnp.arange(0, head_dim, 2, dtype=jnp.float32) / head_dim)
-    angles = positions.astype(jnp.float32)[:, :, None] * frequency
+    angles = places.astype(jnp.float32)[None, :, None] * frequency
     cosine_table = jnp.cos(angles)[:, :, None, :]
     sine_table = jnp.sin(angles)[:, :, None, :]
     inputs = tokens.astype(jnp.float32).reshape(all_rows, model_width)
@@ -321,13 +224,18 @@
         jnp.zeros((sequences, kv_local, per_group, seq_rows), jnp.float32),
         jnp.zeros((sequences, seq_rows, kv_local, per_group, head_dim), jnp.float32),
     )
+    keys_values = lax.all_gather(
+        jnp.concatenate([key_flat, value_low], axis=-1), "ctx", axis=1, tiled=True
+    )
+    kv_width = kv_local * head_dim
+    gathered = (
+        keys_values[..., :kv_width],
+        keys_values[..., kv_width:],
+        lax.all_gather(segments, "ctx", axis=1, tiled=True),
+    )
     row_max, row_sum, weighted = attend(
         start_state,
-        (
-            lax.all_gather(key_flat, "ctx", axis=1, tiled=True),
-            lax.all_gather(value_low, "ctx", axis=1, tiled=True),
-            lax.all_gather(segments, "ctx", axis=1, tiled=True),
-        ),
+        gathered,
         jnp.int32(0),
     )
     mixed_heads = weighted / jnp.transpose(row_sum, (0, 3, 1, 2))[..., None]
@@ -345,17 +253,6 @@
     output_rows = (
         residual + lax.psum(mlp_term.astype(jnp.bfloat16), "wt").astype(jnp.float32)
     ).astype(jnp.bfloat16)
-    row_max, row_sum, weighted = attend(
-        start_state,
-        (
-            lax.all_gather(key_flat, "ctx", axis=1, tiled=True),
-            lax.all_gather(value_low, "ctx", axis=1, tiled=True),
-            lax.all_gather(segments, "ctx", axis=1, tiled=True),
-        ),
-        jnp.int32(0),
-    )
-    mixed_heads = weighted / jnp.transpose(row_sum, (0, 3, 1, 2))[..., None]
-    mixed_low = mixed_heads.astype(jnp.bfloat16).reshape(all_rows, q_local * head_dim)
     log_total = row_max + jnp.log(row_sum)
     grad_rows = cotangent.reshape(all_rows, model_width)
     w_down_grad = transpose_by(grad_rows, hidden_low)
@@ -379,7 +276,7 @@
     delta_rows = jnp.sum(grad_groups.astype(jnp.float32) * mixed_heads, axis=-1)
     delta_cols = jnp.transpose(delta_rows, (0, 2, 3, 1))
     query_grad_fn = partial(
-        query_grad_piece,
+        grad_piece,
         queries=query_groups,
         grad_heads=grad_groups,
         log_total=log_total,
@@ -388,53 +285,16 @@
         query_segs=segments,
         score_scale=score_scale,
     )
-    grad_query = query_grad_fn(
+    grad_query, grad_pairs = query_grad_fn(
         jnp.zeros((sequences, seq_rows, kv_local, per_group, head_dim), jnp.float32),
-        (
-            lax.all_gather(key_flat, "ctx", axis=1, tiled=True),
-            lax.all_gather(value_low, "ctx", axis=1, tiled=True),
-            lax.all_gather(segments, "ctx", axis=1, tiled=True),
-        ),
+        gathered,
         jnp.int32(0),
     )
-    key_grad_fn = partial(
-        key_grad_piece,
-        keys_here=key_low,
-        values_here=value_low.reshape(sequences, seq_rows, kv_local, head_dim),
-        key_places=places,
-        key_segs=segments,
-        score_scale=score_scale,
-    )
-    total_rows = jnp.transpose(log_total, (0, 3, 1, 2)).reshape(sequences, seq_rows, q_local)
-    zero_keys = jnp.zeros((sequences, seq_rows, kv_local, head_dim), jnp.float32)
-    grad_key, grad_value = key_grad_fn(
-        (zero_keys, zero_keys),
-        (
-            lax.all_gather(
-                query_low.reshape(sequences, seq_rows, q_local * head_dim),
-                "ctx",
-                axis=1,
-                tiled=True,
-            ),
-            lax.all_gather(
-                grad_heads_low.reshape(sequences, seq_rows, q_local * head_dim),
-                "ctx",
-                axis=1,
-                tiled=True,
-            ),
-            lax.all_gather(total_rows.astype(jnp.bfloat16), "ctx", axis=1, tiled=True).astype(
-                jnp.float32
-            ),
-            lax.all_gather(
-                delta_rows.reshape(sequences, seq_rows, q_local).astype(jnp.bfloat16),
-                "ctx",
-                axis=1,
-                tiled=True,
-            ).astype(jnp.float32),
-            lax.all_gather(segments, "ctx", axis=1, tiled=True),
-        ),
-        jnp.int32(0),
-    )
+    grad_pairs = lax.psum_scatter(grad_pairs, "ctx", scatter_dimension=1, tiled=True).astype(
+        jnp.float32
+    )
+    grad_key = grad_pairs[:, :, 0]
+    grad_value = grad_pairs[:, :, 1]
     grad_query = rotate(
         grad_query.reshape(sequences, seq_rows, q_local, head_dim) * score_scale,
         cosine_table,
@@ -470,15 +330,22 @@
     ).astype(jnp.bfloat16)
     output = output_rows.reshape(sequences, seq_rows, model_width)
     tokens_grad = tokens_rows.reshape(sequences, seq_rows, model_width)
-    w_query_grad, w_key_grad, w_value_grad, w_out_grad, w_gate_grad, w_up_grad, w_down_grad = (
-        lax.psum_scatter(w_query_grad, "ctx", scatter_dimension=0, tiled=True),
-        lax.psum_scatter(w_key_grad, "ctx", scatter_dimension=0, tiled=True),
-        lax.psum_scatter(w_value_grad, "ctx", scatter_dimension=0, tiled=True),
-        lax.psum_scatter(w_out_grad, "ctx", scatter_dimension=0, tiled=True),
-        lax.psum_scatter(w_gate_grad, "ctx", scatter_dimension=0, tiled=True),
-        lax.psum_scatter(w_up_grad, "ctx", scatter_dimension=0, tiled=True),
-        lax.psum_scatter(w_down_grad, "ctx", scatter_dimension=0, tiled=True),
-    )
+    partial_sums = (
+        w_down_grad,
+        w_gate_grad,
+        w_up_grad,
+        w_out_grad,
+        w_query_grad,
+        w_key_grad,
+        w_value_grad,
+    )
+    summed = [
+        lax.psum_scatter(part.astype(jnp.bfloat16), "ctx", scatter_dimension=0, tiled=True).astype(
+            jnp.float32
+        )
+        for part in partial_sums
+    ]
+    w_down_grad, w_gate_grad, w_up_grad, w_out_grad, w_query_grad, w_key_grad, w_value_grad = summed
     attn_gain_grad, q_gain_grad, k_gain_grad, ffn_gain_grad = lax.psum(
         (attn_gain_part, q_gain_part, k_gain_part, ffn_gain_part), ("ctx", "wt")
     )

time: 1060 us -> 931 us (0.88)
  blocking collectives: 128 us -> 72.4 us
  matrix products: 130 us -> 76.4 us
  waiting for transfers between devices: 667 us -> 639 us
  local copies, waits for them, and re-layouts: 60.5 us -> 72.4 us
    reduce_scatter x7 -> x6, waiting for transfers between devices: 509 us -> 374 us  [on_device(): lax.psum_scatter(part.astype(jnp.bfloat16), 'ctx', scatter_dimension=0, t...]
    unnamed x14, waiting for transfers between devices: 0.23 us -> 107 us
    all_gather x4 -> x1, waiting for transfers between devices: 83.8 us -> 22 us  [on_device(): lax.all_gather(jnp.concatenate([key_flat, value_low], axis=-1), 'ctx', ax...]
    all_gather x2 -> x0, blocking collectives: 42 us -> none  [the longest x1 21.1 us: on_device(): lax.all_gather(delta_rows.reshape(sequences, seq_rows, q_local).astype(jn...]
    dot_general x10, matrix products: 53.1 us -> 13.1 us  [the longest x2 4.04 us: grad_block_step(): jnp.einsum('sqgrd,skgd->sgrqk', queries, key_block, preferred_element_typ...]
    psum x1, waiting for transfers between devices: 27.6 us -> 60.6 us  [on_device(): lax.psum(mlp_term.astype(jnp.bfloat16), 'wt').astype(jnp.float32)]
    psum x1, waiting for transfers between devices: 8.97 us -> 38.6 us  [on_device(): lax.psum(grad_normed_ffn.astype(jnp.bfloat16), 'wt').astype(jnp.float32)]
    unnamed x139 -> x99, local copies, waits for them, and re-layouts: 27.2 us -> 47 us
  transfers between devices with their start and end apart: 14 -> 12, of which waited for: 13 -> 12; matrix products, arithmetic and copies ran while one was open for 11% -> 7% of each run, Pallas kernels for 0% -> 0%
where the time goes in v1:
time: 931 us; the launch traced here: 925 us
  waiting for transfers between devices  639 us (69%)
  matrix products  76.4 us (8%)
  local copies, waits for them, and re-layouts  72.4 us (8%)
  blocking collectives  72.4 us (8%)
  other arithmetic  47.5 us (5%)
  between operations  15.1 us (2%)
    reduce_scatter x6, waiting for transfers between devices, on_device(): lax.psum_scatter(part.astype(jnp.bfloat16), 'ctx', scatter_dimension=0, t...  374 us
    unnamed x14, waiting for transfers between devices  107 us
    psum x1, waiting for transfers between devices, on_device(): lax.psum(mlp_term.astype(jnp.bfloat16), 'wt').astype(jnp.float32)  60.6 us
    unnamed x99, local copies, waits for them, and re-layouts  47 us
    psum x1, blocking collectives, on_device(): lax.psum((attn_gain_part, q_gain_part, k_gain_part, ffn_gain_part), ('ctx...  39.7 us
    psum x1, waiting for transfers between devices, on_device(): lax.psum(grad_normed_ffn.astype(jnp.bfloat16), 'wt').astype(jnp.float32)  38.6 us
    psum x1, waiting for transfers between devices, on_device(): lax.psum(attn_term.astype(jnp.bfloat16), 'wt').astype(jnp.float32)  37 us
    all_gather x1, blocking collectives, on_device(): lax.all_gather(segments, 'ctx', axis=1, tiled=True)  32.7 us
  transfers between devices with their start and end apart: 12, of which 12 were waited for; matrix products, arithmetic and copies ran while one was open for 7% of the time, Pallas kernels for 0%

profile of v1, /device:TPU:0, one launch (start us, length us, event | category | flops | bytes accessed | tf_op | source)
XLA Modules:
  0.0 925.1 jit_solution(11752861120223772836)
XLA Ops:
  16.4 2.0 copy.64
  18.5 32.7 %all_gather.6 = s32[5,1024]{1,0:T(8,128)S(1)} all-gather(s32[5,128]{1,0:T(8,128)S(1)} %copy-done.33), channel_id=1, replica_groups=mesh['ctx'=8,'wt'=4] {'ctx'}, dimensions={1}, use_global_device_ids=true | all-gather | bytes 23040 | tf_op jit(solution)/shard_map/all_gather | solution.py:234
  51.2 2.1 multiply_reduce_fusion.6
  54.2 22.0 %all-gather.2.cloned.1.call-done = bf16[5,1024,256]{1,2,0:T(8,128)(2,1)} async-done(((bf16[5,128,256]{1,2,0:T(8,128)(2,1)}), bf16[5,1024,256]{1,2,0:T(8,128)(2,1)}) %all-gather.2.cloned.1.call-update) | async-done | bytes 2621456 | tf_op jit(solution)/shard_map/all_gather | solution.py:227
  76.2 3.4 fusion.109
  79.6 4.4 reshape_reshape.9
  84.0 2.6 copy.66
  86.6 4.4 reshape_reshape.8
  91.0 2.6 copy.65
  93.6 13.6 %while.28 = (s32[]{:T(128)}, f32[5,2,2,128]{3,2,1,0:T(2,128)S(1)}, f32[5,2,2,128]{3,2,1,0:T(2,128)S(1)}, f32[5,128,2,2,64]{1,4,3,2,0:T(8,128)S(1)}, s32[2]{0:T(1...) while((s32[]{:T(128)}, f32[5,2,2,128]{3,2,1,0:T(2,128)S(1)}, ...), condition=%wide.region_6.7_spmd.clone, body=%wide.region_3.6_spmd.clone.sunk | while | flops 353812096 | bytes 25564876 | solution.py:102
  95.6 2.1 fusion.178
  102.4 2.1 fusion.178
  108.5 2.7 convolution_convert_fusion.3
  111.5 37.0 %all-reduce.6.cloned.1.call-done = bf16[640,1024]{1,0:T(8,128)(2,1)} async-done(((bf16[640,1024]{1,0:T(8,128)(2,1)}), bf16[640,1024]{1,0:T(8,128)(2,1)}) %all-reduce.6.cloned.1.call-update) | async-done | bytes 1310736 | tf_op jit(solution)/shard_map/psum | solution.py:244
  148.4 2.4 multiply_reduce_fusion.2
  154.6 1.9 fusion.112
  156.5 3.6 multiply_convert_fusion
  160.1 1.9 fusion.114
  162.0 3.8 fusion.110
  166.4 38.6 %all-reduce.8.cloned.1.call-done = bf16[640,1024]{1,0:T(8,128)(2,1)} async-done(((bf16[640,1024]{1,0:T(8,128)(2,1)}), bf16[640,1024]{1,0:T(8,128)(2,1)}) %all-reduce.8.cloned.1.call-update) | async-done | bytes 1310736 | tf_op jit(solution)/shard_map/psum | solution.py:268
  205.0 4.0 multiply_reduce_fusion
  215.0 2.1 reshape.393
  220.7 22.6 %while.29 = (s32[]{:T(128)}, f32[5,128,2,2,64]{1,4,3,2,0:T(8,128)S(1)}, bf16[2,5,512,2,2,64]{2,5,4,1,3,0:T(8,128)(2,1)}, bf16[2,5,512,2,64]{2,4,3,1,0:T(8,128)(2...) while((s32[]{:T(128)}, ...), condition=%wide.region_14.15_spmd.clone, body=%wide.region_13.14_spmd.clone.sunk | while | flops 856294016 | bytes 66064208 | solution.py:165
  222.6 2.0 fusion.193
  233.9 2.0 fusion.193
  243.3 11.3 %copy.94 = bf16[5,2,512,2,2,64]{5,4,0,3,2,1:T(2,128)(2,1)} copy(bf16[5,2,512,2,2,64]{2,5,4,0,3,1:T(8,128)(2,1)} %bitcast.343) | data formatting | bytes 5242880
  254.6 10.3 %reshape.407 = bf16[1024,1280]{1,0:T(8,128)(2,1)} reshape(bf16[1024,2,5,2,64]{4,3,2,1,0:T(2,128)(2,1)} %bitcast.336) | data formatting | bytes 5242880
  265.9 3.3 convolution_convert_fusion.5
  273.7 5.2 fusion.64
  279.0 4.4 copy.92
  283.5 5.4 convolution_convert_fusion.1
  289.0 5.4 convolution_convert_fusion.2
  294.4 4.3 convolution_convert_fusion.4
  298.8 36.6 %reduce-scatter.25.cloned.1.call-done = bf16[128,1280]{1,0:T(8,128)(2,1)} async-done(((bf16[1024,1280]{1,0:T(8,128)(2,1)}), bf16[128,1280]{1,0:T(8,128)(2,1)}) %reduce-scatter.25.cloned.1.call-update) | async-done | bytes 327696
  342.4 2.6 convolution_convert_fusion.9
  345.0 3.2 fusion.101
  350.1 2.5 fusion.111
  352.7 47.3 %reduce-scatter.19.cloned.1.call-done = bf16[128,256]{1,0:T(8,128)(2,1)} async-done(((bf16[1024,256]{1,0:T(8,128)(2,1)}), bf16[128,256]{1,0:T(8,128)(2,1)}) %reduce-scatter.19.cloned.1.call-update) | async-done | bytes 65552 | tf_op jit(solution)/shard_map/reduce_scatter | solution.py:343
  401.5 63.6 %reduce-scatter.13.cloned.1.call-done = bf16[128,256]{1,0:T(8,128)(2,1)} async-done(((bf16[1024,256]{1,0:T(8,128)(2,1)}), bf16[128,256]{1,0:T(8,128)(2,1)}) %reduce-scatter.13.cloned.1.call-update) | async-done | bytes 65552 | tf_op jit(solution)/shard_map/reduce_scatter | solution.py:343
  466.6 70.0 %reduce-scatter.27.cloned.1.call-done = bf16[128,1152]{1,0:T(8,128)(2,1)} async-done(((bf16[1024,1152]{1,0:T(8,128)(2,1)}), bf16[128,1152]{1,0:T(8,128)(2,1)}) %reduce-scatter.27.cloned.1.call-update) | async-done | bytes 294928
  538.8 69.7 %reduce-scatter.23.cloned.1.call-done = bf16[128,1152]{1,0:T(8,128)(2,1)} async-done(((bf16[1024,1152]{1,0:T(8,128)(2,1)}), bf16[128,1152]{1,0:T(8,128)(2,1)}) %reduce-scatter.23.cloned.1.call-update) | async-done | bytes 294928 | tf_op jit(solution)/shard_map/reduce_scatter | solution.py:343
  610.3 69.8 %reduce-scatter.21.cloned.1.call-done = bf16[128,1152]{1,0:T(8,128)(2,1)} async-done(((bf16[1024,1152]{1,0:T(8,128)(2,1)}), bf16[128,1152]{1,0:T(8,128)(2,1)}) %reduce-scatter.21.cloned.1.call-update) | async-done | bytes 294928 | tf_op jit(solution)/shard_map/reduce_scatter | solution.py:343
  681.9 61.7 %reduce-scatter.17.cloned.1.call-done = bf16[128,128]{1,0:T(8,128)(2,1)} async-done(((bf16[1024,128]{1,0:T(8,128)(2,1)}), bf16[128,128]{1,0:T(8,128)(2,1)}) %reduce-scatter.17.cloned.1.call-update) | async-done | bytes 32784 | tf_op jit(solution)/shard_map/reduce_scatter | solution.py:343
  744.9 62.2 %reduce-scatter.15.cloned.1.call-done = bf16[128,128]{1,0:T(8,128)(2,1)} async-done(((bf16[1024,128]{1,0:T(8,128)(2,1)}), bf16[128,128]{1,0:T(8,128)(2,1)}) %reduce-scatter.15.cloned.1.call-update) | async-done | bytes 32784 | tf_op jit(solution)/shard_map/reduce_scatter | solution.py:343
  808.6 60.6 %all-reduce.10.cloned.1.call-done = (bf16[640,1024]{1,0:T(8,128)(2,1)}, bf16[640,1024]{1,0:T(8,128)(2,1)}) async-done(((bf16[640,1024]{1,0:T(8,128)(2,1)}, bf16[640,1024]{1,0:T(8,128)(2,1)}), (bf16[640,1024]{1,0:T(8,128)(2,1)}, bf16[640,1024]{1,0:T(8,128)(2,1)})) %all-reduce.10.cloned.1.call-update) | async-done | bytes 2621456 | tf_op jit(solution)/shard_map/psum | solution.py:254
  869.1 3.3 fusion.76
  872.5 39.7 %all-reduce = (f32[1024]{0:T(1024)}, f32[64]{0:T(128)}, f32[64]{0:T(128)}, f32[1024]{0:T(1024)}) all-reduce(f32[1024]{0:T(1024)S(1)} %get-tuple-element.333, f32[64]{0:T(128)S(1)} %get-tuple-element.331, f32[64]{0:T(128)S(1)} %get-tuple-element.335, f32[1024]{0:T(1024)S(1)} %get-tuple-element.329), channel_id=1, replica_groups=mesh['ctx'=8,'wt'=4] {'ctx','wt'}, use_global_device_ids=true, to_apply=%region_21.22 | all-reduce | flops 2176 | bytes 17408 | tf_op jit(solution)/shard_map/psum | solution.py:349
  912.1 5.9 fusion.75
  (250 shorter events, 78.8 us)
Async XLA Ops:
  7.2 149.3 %copy-start = (bf16[1024,1152]{1,0:T(8,128)(2,1)S(1)}, bf16[1024,1152]{1,0:T(8,128)(2,1)}, u32[]{:S(2)}) copy-start(bf16[1024,1152]{1,0:T(8,128)(2,1)} %param.30) | copy-start | bytes 7077892
  7.2 69.0 %all-gather.2.cloned.1.call-start = ((), (), s32[]{:S(2)}) async-start(), calls=%async_computation.8 | async-start | bytes 2949120 | tf_op jit(solution)/shard_map/all_gather | solution.py:227
  8.1 7.3 copy-start.41
  8.8 5.2 copy-start.35
  10.4 3.5 copy-start.39
  11.5 2.4 copy-start.1
  14.5 1.9 copy-start.46
  14.5 4.0 copy-start.33
  16.3 132.1 %all-reduce.6.cloned.1.call-start = ((), (), s32[]{:S(2)}) async-start(), calls=%async_computation.9 | async-start | bytes 2621440 | tf_op jit(solution)/shard_map/psum | solution.py:244
  107.2 43.6 %copy-start.18 = (f32[5,128,2,2,64]{1,4,3,2,0:T(8,128)}, f32[5,128,2,2,64]{1,4,3,2,0:T(8,128)S(1)}, u32[]{:S(2)}) copy-start(f32[5,128,2,2,64]{1,4,3,2,0:T(8,128)S(1)} %get-tuple-element.140) | copy-start | bytes 1966084
  107.2 4.2 copy-start.43
  111.1 93.9 %all-reduce.8.cloned.1.call-start = ((), (), s32[]{:S(2)}) async-start(), calls=%async_computation.10 | async-start | bytes 2621440 | tf_op jit(solution)/shard_map/psum | solution.py:268
  148.4 2.4 copy-start.2
  148.4 2.5 copy-start.6
  152.5 1.9 copy-start.31
  152.5 2.1 copy-start.44
  154.6 1.9 copy-start.29
  160.1 1.9 copy-start.48
  160.1 1.9 copy-start.47
  165.9 169.6 %reduce-scatter.25.cloned.1.call-start = ((), (), s32[]{:S(2)}) async-start(), calls=%async_computation.17 | async-start | bytes 2949120
  205.0 4.0 copy-start.3
  205.0 4.0 copy-start.7
  205.0 4.0 copy-start.16
  205.0 4.4 copy-start.30
  209.4 2.5 copy-start.22
  222.6 2.0 copy-start.34
  226.0 1.8 copy-start.4
  233.9 2.0 copy-start.34
  264.9 135.1 %reduce-scatter.19.cloned.1.call-start = ((), (), s32[]{:S(2)}) async-start(), calls=%async_computation.14 | async-start | bytes 589824 | tf_op jit(solution)/shard_map/reduce_scatter | solution.py:343
  265.9 4.9 copy-start.13
  269.2 195.9 %reduce-scatter.13.cloned.1.call-start = ((), (), s32[]{:S(2)}) async-start(), calls=%async_computation.11 | async-start | bytes 589824 | tf_op jit(solution)/shard_map/reduce_scatter | solution.py:343
  269.4 2.8 copy-start.9
  273.7 262.9 %reduce-scatter.27.cloned.1.call-start = ((), (), s32[]{:S(2)}) async-start(), calls=%async_computation.18 | async-start | bytes 2654208
  283.4 325.1 %reduce-scatter.23.cloned.1.call-start = ((), (), s32[]{:S(2)}) async-start(), calls=%async_computation.16 | async-start | bytes 2654208 | tf_op jit(solution)/shard_map/reduce_scatter | solution.py:343
  288.9 391.1 %reduce-scatter.21.cloned.1.call-start = ((), (), s32[]{:S(2)}) async-start(), calls=%async_computation.15 | async-start | bytes 2654208 | tf_op jit(solution)/shard_map/reduce_scatter | solution.py:343
  294.4 449.2 %reduce-scatter.17.cloned.1.call-start = ((), (), s32[]{:S(2)}) async-start(), calls=%async_computation.13 | async-start | bytes 294912 | tf_op jit(solution)/shard_map/reduce_scatter | solution.py:343
  298.8 41.5 %copy-start.15 = (f32[5,128,2,64]{1,3,2,0:T(8,128)S(1)}, f32[5,128,2,64]{1,3,2,0:T(8,128)}, u32[]{:S(2)}) copy-start(f32[5,128,2,64]{1,3,2,0:T(8,128)} %copy-done.14) | copy-start | bytes 983044
  298.8 41.5 %copy-start.38 = (f32[5,128,2]{1,2,0:T(2,128)S(1)}, f32[5,128,2]{1,2,0:T(2,128)}, u32[]{:S(2)}) copy-start(f32[5,128,2]{1,2,0:T(2,128)} %copy-done.37) | copy-start | bytes 15364
  298.8 41.5 %copy-start.42 = (f32[64]{0:T(128)S(1)}, f32[64]{0:T(128)}, u32[]{:S(2)}) copy-start(f32[64]{0:T(128)} %copy-done.41) | copy-start | bytes 772
  337.9 2.9 copy-start.10
  340.7 4.3 copy-start.26
  342.1 465.0 %reduce-scatter.15.cloned.1.call-start = ((), (), s32[]{:S(2)}) async-start(), calls=%async_computation.12 | async-start | bytes 294912 | tf_op jit(solution)/shard_map/reduce_scatter | solution.py:343
  345.0 5.0 copy-start.21
  345.0 5.0 copy-start.24
  348.2 520.9 %all-reduce.10.cloned.1.call-start = ((), (), s32[]{:S(2)}) async-start(), calls=%async_computation.19 | async-start | bytes 5242880 | tf_op jit(solution)/shard_map/psum | solution.py:254
  348.2 1.9 copy-start.11
  352.6 516.5 %copy-start.36 = (f32[1024]{0:T(1024)S(1)}, f32[1024]{0:T(1024)}, u32[]{:S(2)}) copy-start(f32[1024]{0:T(1024)} %copy-done.35) | copy-start | bytes 12292
  352.6 516.5 %copy-start.40 = (f32[640]{0:T(1024)S(1)}, f32[640]{0:T(1024)}, u32[]{:S(2)}) copy-start(f32[640]{0:T(1024)} %copy-done.39) | copy-start | bytes 7684
  (19 other events, 25.9 us)
Sparse Core Ops, SparseCore 0:
  16.4 59.6 all-gather.1
  111.3 37.1 all-reduce.5
  166.0 38.9 all-reduce.7
  265.0 70.3 reduce-scatter.24
  339.2 60.7 reduce-scatter.18
  404.1 60.9 reduce-scatter.12
  468.6 67.9 reduce-scatter.26
  540.1 68.3 reduce-scatter.22
  612.0 68.0 reduce-scatter.20
  683.2 60.2 reduce-scatter.16
  746.9 60.2 reduce-scatter.14
  810.0 59.1 all-reduce.9

commit v2 on v1

--- a/solution.py
+++ b/solution.py
@@ -4,6 +4,8 @@
 import jax
 import jax.numpy as jnp
 from jax import lax
+from jax.experimental import pallas as pl
+from jax.experimental.pallas import tpu as pltpu
 from jax.sharding import PartitionSpec as P
 
 EPS = 1e-05
@@ -166,6 +168,149 @@
         grad_block_step, folded, (key_blocks, value_tiles, seg_blocks, offsets)
     )
     return folded, jnp.moveaxis(grads, 0, 1).reshape((sequences, piece_rows) + grads.shape[3:])
+
+
+MESH = pl.DeviceIdType.MESH
+MIB = 1 << 20
+
+
+def ring_place(index, count):
+    return lax.select(
+        lax.rem(index, 2) == 0, lax.div(index, 2), count - 1 - lax.div(index, 2)
+    )
+
+
+def ring_index(place, count):
+    place = lax.rem(place + 2 * count, count)
+    return lax.select(
+        place < lax.div(count, 2), 2 * place, 2 * (count - 1 - place) + 1
+    )
+
+
+class Ring:
+    def __init__(self, count, slots, send_sems, recv_sems):
+        self.count, self.slots = count, slots
+        self.send_sems, self.recv_sems = send_sems, recv_sems
+        self.other = lax.axis_index("wt")
+        self.place = ring_place(lax.axis_index("ctx"), count)
+        self.right = ring_index(self.place + 1, count)
+        self.left = ring_index(self.place + count - 1, count)
+        self.half = slots.shape[2] // 2
+
+    def copy(self, which, step, way):
+        rows = pl.ds(way * self.half, self.half)
+        later = step + 1 if isinstance(step, int) else lax.add(step, 1)
+        return pltpu.make_async_remote_copy(
+            src_ref=self.slots.at[which, step, rows],
+            dst_ref=self.slots.at[which, later, rows],
+            send_sem=self.send_sems.at[which, step, way],
+            recv_sem=self.recv_sems.at[which, step, way],
+            device_id=((self.right, self.left)[way], self.other),
+            device_id_type=MESH,
+        )
+
+    def tick(self, which, step, left_ref, right_ref, first=False, result=None):
+        half = self.half
+        rows = [
+            ring_index(target, self.count) * (2 * half) + way * half
+            for way, target in enumerate(
+                (self.place + self.count - 1 - step, self.place + 1 + step)
+            )
+        ]
+        left = jnp.concatenate(
+            [left_ref[pl.ds(pl.multiple_of(row, half), half), :] for row in rows], axis=0
+        )
+        total = jnp.dot(left, right_ref[...], preferred_element_type=jnp.float32)
+        if not first:
+            for way in range(2):
+                self.copy(which, step - 1, way).wait_recv()
+            total = total + self.slots[which, step].astype(jnp.float32)
+        if result is None:
+            self.slots[which, step] = total.astype(jnp.bfloat16)
+            for way in range(2):
+                self.copy(which, step, way).start()
+        else:
+            result[...] = total
+
+    def finish(self, which):
+        for way in range(2):
+
+            def wait(step, carry):
+                self.copy(which, step, way).wait_send()
+                return carry
+
+            lax.fori_loop(0, self.count - 1, wait, 0)
+
+
+def greet(peers):
+    barrier = pltpu.get_barrier_semaphore()
+    for peer in peers:
+        pl.semaphore_signal(barrier, inc=1, device_id=peer, device_id_type=MESH)
+    pl.semaphore_wait(barrier, len(peers))
+
+
+def ring_kernel(count, *refs):
+    (cot_t, normed_ffn_t, grad_res_t, normed_t, ffn_grads, heads, grad_qkv) = refs[:7]
+    (ffn_sums, out_sums, qkv_sums) = refs[7:10]
+    scratch = refs[10:]
+    rings = [Ring(count, *scratch[3 * i : 3 * i + 3]) for i in range(3)]
+    greet([(rings[0].right, rings[0].other), (rings[0].left, rings[0].other)])
+    ffn, out, qkv = rings
+    lefts = (cot_t, normed_ffn_t, normed_ffn_t)
+    for i in range(3):
+        ffn.tick(i, 0, lefts[i], ffn_grads.at[i], first=True)
+    out.tick(0, 0, grad_res_t, heads, first=True)
+    qkv.tick(0, 0, normed_t, grad_qkv, first=True)
+
+    def middle(step, carry):
+        for i in range(3):
+            ffn.tick(i, step, lefts[i], ffn_grads.at[i])
+        out.tick(0, step, grad_res_t, heads)
+        qkv.tick(0, step, normed_t, grad_qkv)
+        return carry
+
+    lax.fori_loop(1, count - 1, middle, 0)
+    for i in range(3):
+        ffn.tick(i, count - 1, lefts[i], ffn_grads.at[i], result=ffn_sums.at[i])
+    out.tick(0, count - 1, grad_res_t, heads, result=out_sums)
+    qkv.tick(0, count - 1, normed_t, grad_qkv, result=qkv_sums)
+    for i in range(3):
+        ffn.finish(i)
+    out.finish(0)
+    qkv.finish(0)
+
+
+def ring_sums(cot_t, normed_ffn_t, grad_res_t, normed_t, ffn_grads, heads, grad_qkv):
+    count = lax.axis_size("ctx")
+    rows = cot_t.shape[0] // count
+    widths = [(3, ffn_grads.shape[2]), (1, heads.shape[1]), (1, grad_qkv.shape[1])]
+    scratch = []
+    for arrays, width in widths:
+        scratch += [
+            pltpu.VMEM((arrays, count, rows, width), jnp.bfloat16),
+            pltpu.SemaphoreType.DMA((arrays, count - 1, 2)),
+            pltpu.SemaphoreType.DMA((arrays, count - 1, 2)),
+        ]
+    vmem = pl.BlockSpec(memory_space=pltpu.VMEM)
+    return pl.pallas_call(
+        partial(ring_kernel, count),
+        out_shape=[
+            jax.ShapeDtypeStruct((3, rows, widths[0][1]), jnp.float32),
+            jax.ShapeDtypeStruct((rows, widths[1][1]), jnp.float32),
+            jax.ShapeDtypeStruct((rows, widths[2][1]), jnp.float32),
+        ],
+        in_specs=[vmem] * 7,
+        out_specs=[vmem] * 3,
+        scratch_shapes=scratch,
+        compiler_params=pltpu.CompilerParams(
+            collective_id=1, has_side_effects=True, vmem_limit_bytes=60 * MIB
+        ),
+    )(cot_t, normed_ffn_t, grad_res_t, normed_t, ffn_grads, heads, grad_qkv)
+
+
+def ring_fits(model_width, all_rows):
+    count = lax.axis_size("ctx")
+    return count % 2 == 0 and model_width % (32 * count) == 0 and all_rows <= 640
 
 
 def on_device(
@@ -255,14 +400,11 @@
     ).astype(jnp.bfloat16)
     log_total = row_max + jnp.log(row_sum)
     grad_rows = cotangent.reshape(all_rows, model_width)
-    w_down_grad = transpose_by(grad_rows, hidden_low)
     grad_hidden = product(grad_rows, w_down)
     grad_gate = (
         grad_hidden * up_proj * gate_sigmoid * (1.0 + gate_proj * (1.0 - gate_sigmoid))
     ).astype(jnp.bfloat16)
     grad_up = (grad_hidden * gate_silu).astype(jnp.bfloat16)
-    w_gate_grad = transpose_by(normed_ffn_low, grad_gate)
-    w_up_grad = transpose_by(normed_ffn_low, grad_up)
     grad_normed_ffn = by_transpose(grad_gate, w_gate) + by_transpose(grad_up, w_up)
     ffn_gain_part = jnp.sum(grad_normed_ffn * ffn_unit, axis=0)
     grad_normed_ffn = lax.psum(grad_normed_ffn.astype(jnp.bfloat16), "wt").astype(jnp.float32)
@@ -270,7 +412,6 @@
         grad_normed_ffn, ffn_unit, ffn_inverse, ffn_gain
     )
     grad_residual_low = grad_residual.astype(jnp.bfloat16)
-    w_out_grad = transpose_by(grad_residual_low, mixed_low)
     grad_heads_low = product(grad_residual_low, w_out).astype(jnp.bfloat16)
     grad_groups = grad_heads_low.reshape(sequences, seq_rows, kv_local, per_group, head_dim)
     delta_rows = jnp.sum(grad_groups.astype(jnp.float32) * mixed_heads, axis=-1)
@@ -315,9 +456,6 @@
         .reshape(all_rows, kv_local * head_dim)
     )
     grad_value_low = grad_value.astype(jnp.bfloat16).reshape(all_rows, kv_local * head_dim)
-    w_query_grad = transpose_by(normed_low, grad_query_low)
-    w_key_grad = transpose_by(normed_low, grad_key_low)
-    w_value_grad = transpose_by(normed_low, grad_value_low)
     grad_normed = (
         by_transpose(grad_query_low, w_query)
         + by_transpose(grad_key_low, key_matrix)
@@ -330,22 +468,39 @@
     ).astype(jnp.bfloat16)
     output = output_rows.reshape(sequences, seq_rows, model_width)
     tokens_grad = tokens_rows.reshape(sequences, seq_rows, model_width)
-    partial_sums = (
-        w_down_grad,
-        w_gate_grad,
-        w_up_grad,
-        w_out_grad,
-        w_query_grad,
-        w_key_grad,
-        w_value_grad,
-    )
-    summed = [
-        lax.psum_scatter(part.astype(jnp.bfloat16), "ctx", scatter_dimension=0, tiled=True).astype(
-            jnp.float32
-        )
-        for part in partial_sums
-    ]
-    w_down_grad, w_gate_grad, w_up_grad, w_out_grad, w_query_grad, w_key_grad, w_value_grad = summed
+    if not ring_fits(model_width, all_rows):
+        partial_sums = (
+            transpose_by(grad_rows, hidden_low),
+            transpose_by(normed_ffn_low, grad_gate),
+            transpose_by(normed_ffn_low, grad_up),
+            transpose_by(grad_residual_low, mixed_low),
+            transpose_by(normed_low, grad_query_low),
+            transpose_by(normed_low, grad_key_low),
+            transpose_by(normed_low, grad_value_low),
+        )
+        summed = [
+            lax.psum_scatter(
+                part.astype(jnp.bfloat16), "ctx", scatter_dimension=0, tiled=True
+            ).astype(jnp.float32)
+            for part in partial_sums
+        ]
+        w_down_grad, w_gate_grad, w_up_grad, w_out_grad = summed[:4]
+        w_query_grad, w_key_grad, w_value_grad = summed[4:]
+    else:
+        ffn_sums, w_out_grad, qkv_sums = ring_sums(
+            grad_rows.T,
+            normed_ffn_low.T,
+            grad_residual_low.T,
+            normed_low.T,
+            jnp.stack([hidden_low, grad_gate, grad_up]),
+            mixed_low,
+            jnp.concatenate([grad_query_low, grad_key_low, grad_value_low], axis=1),
+        )
+        w_down_grad, w_gate_grad, w_up_grad = ffn_sums[0], ffn_sums[1], ffn_sums[2]
+        query_width, key_width = q_local * head_dim, kv_local * head_dim
+        w_query_grad = qkv_sums[:, :query_width]
+        w_key_grad = qkv_sums[:, query_width : query_width + key_width]
+        w_value_grad = qkv_sums[:, query_width + key_width :]
     attn_gain_grad, q_gain_grad, k_gain_grad, ffn_gain_grad = lax.psum(
         (attn_gain_part, q_gain_part, k_gain_part, ffn_gain_part), ("ctx", "wt")
     )

time: 931 us -> 597 us (0.64)
  waiting for transfers between devices: 639 us -> 211 us
  Pallas kernels: 0 us -> 92.3 us
  local copies, waits for them, and re-layouts: 72.4 us -> 86.6 us
    reduce_scatter x6 -> x0, waiting for transfers between devices: 374 us -> none  [on_device(): lax.psum_scatter(part.astype(jnp.bfloat16), 'ctx', scatter_dimension=0, t...]
    pallas_call x0 -> x1, Pallas kernels: none -> 92.3 us  [ring_sums(): pl.pallas_call(partial(ring_kernel, count), out_shape=[jax.ShapeDtypeStru...]
    unnamed x14 -> x6, waiting for transfers between devices: 107 us -> 63.7 us
    dot_general x7 -> x0, matrix products: 24.6 us -> none  [transpose_by(): lax.dot_general(left, right, (((0,), (0,)), ((), ())), preferred_element_...]
    convert_element_type x9 -> x1, other arithmetic: 12.6 us -> 0.95 us  [on_device(): grad_residual_low = grad_residual.astype(jnp.bfloat16)]
  transfers between devices with their start and end apart: 12 -> 5, of which waited for: 12 -> 5; matrix products, arithmetic and copies ran while one was open for 7% -> 3% of each run, Pallas kernels for 0% -> 0%
where the time goes in v2:
time: 597 us; the launch traced here: 593 us
  waiting for transfers between devices  211 us (35%)
  Pallas kernels  92.3 us (15%)
  local copies, waits for them, and re-layouts  86.6 us (15%)
  blocking collectives  72.4 us (12%)
  matrix products  70.5 us (12%)
  other arithmetic  43.3 us (7%)
  between operations  14.6 us (2%)
    pallas_call x1, Pallas kernels, ring_sums(): pl.pallas_call(partial(ring_kernel, count), out_shape=[jax.ShapeDtypeStru...  92.3 us
    unnamed x6, waiting for transfers between devices  63.7 us
    psum x1, waiting for transfers between devices, on_device(): lax.psum(mlp_term.astype(jnp.bfloat16), 'wt').astype(jnp.float32)  51.8 us
    unnamed x99, local copies, waits for them, and re-layouts  42.7 us
    psum x1, blocking collectives, on_device(): lax.psum((attn_gain_part, q_gain_part, k_gain_part, ffn_gain_part), ('ctx...  39.6 us
    psum x1, waiting for transfers between devices, on_device(): lax.psum(attn_term.astype(jnp.bfloat16), 'wt').astype(jnp.float32)  37 us
    psum x1, waiting for transfers between devices, on_device(): lax.psum(grad_normed_ffn.astype(jnp.bfloat16), 'wt').astype(jnp.float32)  36.1 us
    all_gather x1, blocking collectives, on_device(): lax.all_gather(segments, 'ctx', axis=1, tiled=True)  32.7 us
  transfers between devices with their start and end apart: 5, of which 5 were waited for; matrix products, arithmetic and copies ran while one was open for 3% of the time, Pallas kernels for 0%

profile of v2, /device:TPU:0, one launch (start us, length us, event | category | flops | bytes accessed | tf_op | source)
XLA Modules:
  0.0 592.6 jit_solution(13555709528499863029)
XLA Ops:
  10.9 2.0 multiply_reduce_fusion.12
  12.9 3.0 copy.101
  15.9 3.2 convolution_convert_fusion.3
  22.5 32.7 %all_gather.6 = s32[5,1024]{1,0:T(8,128)S(1)} all-gather(s32[5,128]{1,0:T(8,128)S(1)} %copy-done.31), channel_id=1, replica_groups=mesh['ctx'=8,'wt'=4] {'ctx'}, dimensions={1}, use_global_device_ids=true | all-gather | bytes 23040 | tf_op jit(solution)/shard_map/all_gather | solution.py:379
  55.2 2.2 multiply_reduce_fusion.9
  58.3 22.9 %all-gather.2.cloned.1.call-done = bf16[5,1024,256]{1,2,0:T(8,128)(2,1)} async-done(((bf16[5,128,256]{1,2,0:T(8,128)(2,1)}), bf16[5,1024,256]{1,2,0:T(8,128)(2,1)}) %all-gather.2.cloned.1.call-update) | async-done | bytes 2621456 | tf_op jit(solution)/shard_map/all_gather | solution.py:372
  81.1 3.4 fusion.75
  84.6 4.4 reshape_reshape.8
  88.9 2.6 copy.96
  91.6 4.4 reshape_reshape.9
  95.9 2.6 copy.97
  98.5 25.7 %while.28 = (s32[]{:T(128)}, f32[5,2,2,128]{3,2,1,0:T(2,128)S(1)}, f32[5,2,2,128]{3,2,1,0:T(2,128)S(1)}, f32[5,128,2,2,64]{1,4,3,2,0:T(8,128)}, s32[2]{0:T(128)S...) while((s32[]{:T(128)}, f32[5,2,2,128]{3,2,1,0:T(2,128)S(1)}, ...), condition=%wide.region_6.7_spmd.clone, body=%wide.region_3.6_spmd.clone.sunk | while | flops 353812096 | bytes 41294520 | solution.py:104
  100.5 4.5 fusion.143
  105.0 5.0 fusion.147
  113.3 4.5 fusion.143
  117.8 5.1 fusion.147
  126.6 2.7 convolution_convert_fusion
  129.7 37.0 %all-reduce.6.cloned.1.call-done = bf16[640,1024]{0,1:T(8,128)(2,1)} async-done(((bf16[640,1024]{0,1:T(8,128)(2,1)}), bf16[640,1024]{0,1:T(8,128)(2,1)}) %all-reduce.6.cloned.1.call-update) | async-done | bytes 1310736 | tf_op jit(solution)/shard_map/psum | solution.py:389
  166.6 2.7 multiply_reduce_fusion.4
  171.6 1.9 fusion.80
  175.7 3.8 multiply_convert_fusion
  179.4 2.2 fusion.82
  181.6 4.1 fusion.78
  186.3 2.5 copy.104
  188.8 36.1 %all-reduce.8.cloned.1.call-done = bf16[640,1024]{0,1:T(8,128)(2,1)} async-done(((bf16[640,1024]{0,1:T(8,128)(2,1)}), bf16[640,1024]{0,1:T(8,128)(2,1)}) %all-reduce.8.cloned.1.call-update) | async-done | bytes 1310736 | tf_op jit(solution)/shard_map/psum | solution.py:410
  224.9 4.9 multiply_reduce_fusion
  235.3 2.1 reshape.362
  241.0 26.4 %while.29 = (s32[]{:T(128)}, f32[5,128,2,2,64]{1,4,3,2,0:T(8,128)S(1)}, bf16[2,5,512,2,2,64]{2,5,4,1,3,0:T(8,128)(2,1)}, bf16[2,5,512,2,64]{2,4,3,1,0:T(8,128)(2...) while((s32[]{:T(128)}, ...), condition=%wide.region_14.15_spmd.clone, body=%wide.region_13.14_spmd.clone.sunk | while | flops 856294016 | bytes 50337028 | solution.py:167
  242.9 2.1 fusion.158
  251.6 2.6 fusion.160
  256.2 2.1 fusion.158
  264.8 2.6 fusion.160
  267.4 11.4 %copy.145 = bf16[5,2,512,2,2,64]{5,4,0,3,2,1:T(2,128)(2,1)} copy(bf16[5,2,512,2,2,64]{2,5,4,0,3,1:T(8,128)(2,1)} %bitcast.25) | data formatting | bytes 5242880
  278.8 10.3 %reshape.376 = bf16[1024,1280]{1,0:T(8,128)(2,1)} reshape(bf16[1024,2,5,2,64]{4,3,2,1,0:T(2,128)(2,1)} %bitcast.290) | data formatting | bytes 5242880
  289.3 4.6 convolution_convert_fusion.1
  296.2 63.6 %reduce-scatter.4.cloned.1.call-done = bf16[128,1280]{1,0:T(8,128)(2,1)} async-done(((bf16[1024,1280]{1,0:T(8,128)(2,1)}), bf16[128,1280]{1,0:T(8,128)(2,1)}) %reduce-scatter.4.cloned.1.call-update) | async-done | bytes 327696
  359.8 2.2 reshape.377
  362.0 2.2 fusion.76
  371.3 2.5 fusion.79
  375.7 3.9 pad_maximum_fusion.refs_4_
  381.1 51.8 %all-reduce.10.cloned.1.call-done = (bf16[640,1024]{0,1:T(8,128)(2,1)}, bf16[640,1024]{0,1:T(8,128)(2,1)}) async-done(((bf16[640,1024]{0,1:T(8,128)(2,1)}, bf16[640,1024]{0,1:T(8,128)(2,1)}), (bf16[640,1024]{0,1:T(8,128)(2,1)}, bf16[640,1024]{0,1:T(8,128)(2,1)})) %all-reduce.10.cloned.1.call-update) | async-done | bytes 2621456 | tf_op jit(solution)/shard_map/psum | solution.py:399
  433.0 4.7 multiply_reduce_fusion.1
  437.7 92.3 %shard_map.237 = (f32[3,128,1152]{2,1,0:T(8,128)}, f32[128,256]{1,0:T(8,128)}, f32[128,512]{1,0:T(8,128)}) custom-call(bf16[1024,640]{1,0:T(8,128)(2,1)} %bitcast.291, bf16[1024,640]{1,0:T(8,128)(2,1)} %bitcast.289, bf16[1024,640]{1,0:T(8,128)(2,1)} %bitcast.295, bf16[1024,640]{1,0:T(8,128)(2,1)} %get-tuple-element.380.refs_3_, ...), custom_call_target="tpu_custom_call" | custom-call | tf_op jit(solution)/shard_map/pallas_call | solution.py:295
  533.4 2.7 slice_bitcast_fusion
  536.1 4.6 add_convert_fusion
  540.7 2.5 copy.103
  543.2 2.4 copy.119
  545.6 39.6 %all-reduce = (f32[1024]{0:T(1024)}, f32[64]{0:T(128)}, f32[64]{0:T(128)}, f32[1024]{0:T(1024)}) all-reduce(f32[1024]{0:T(1024)S(1)} %get-tuple-element.311, f32[64]{0:T(128)S(1)} %copy-done.42, f32[64]{0:T(128)S(1)} %get-tuple-element.315, f32[1024]{0:T(1024)S(1)} %copy-done.40), channel_id=1, replica_groups=mesh['ctx'=8,'wt'=4] {'ctx','wt'}, use_global_device_ids=true, to_apply=%region_21.22 | all-reduce | flops 2176 | bytes 17408 | tf_op jit(solution)/shard_map/psum | solution.py:504
  (219 shorter events, 64.4 us)
Async XLA Ops:
  7.2 168.5 %copy-start = (bf16[1024,1152]{1,0:T(8,128)(2,1)S(1)}, bf16[1024,1152]{1,0:T(8,128)(2,1)}, u32[]{:S(2)}) copy-start(bf16[1024,1152]{1,0:T(8,128)(2,1)} %param.30) | copy-start | bytes 7077892
  7.2 5.7 copy-start.44
  7.2 73.9 %all-gather.2.cloned.1.call-start = ((), (), s32[]{:S(2)}) async-start(), calls=%async_computation.1 | async-start | bytes 2949120 | tf_op jit(solution)/shard_map/all_gather | solution.py:372
  8.1 47.1 %copy-start.36 = (f32[1024]{0:T(1024)}, f32[1024]{0:T(1024)S(1)}, u32[]{:S(2)}) copy-start(f32[1024]{0:T(1024)S(1)} %convert_element_type.130) | copy-start | bytes 12292
  9.8 6.1 %copy-start.34 = (f32[640]{0:T(1024)}, f32[640]{0:T(1024)S(1)}, u32[]{:S(2)}) copy-start(f32[640]{0:T(1024)S(1)} %get-tuple-element.399) | copy-start | bytes 7684
  12.8 7.6 %copy-start.16 = (f32[5,128,2,64]{1,3,2,0:T(8,128)}, f32[5,128,2,64]{1,3,2,0:T(8,128)S(1)}, u32[]{:S(2)}) copy-start(f32[5,128,2,64]{1,3,2,0:T(8,128)S(1)} %get-tuple-element.404) | copy-start | bytes 983044
  12.8 3.1 copy-start.28
  12.9 7.5 %copy-start.41 = (f32[64]{0:T(128)}, f32[64]{0:T(128)S(1)}, u32[]{:S(2)}) copy-start(f32[64]{0:T(128)S(1)} %convert_element_type.132) | copy-start | bytes 772
  15.9 5.6 copy-start.22
  19.1 3.3 copy-start.45
  19.1 3.3 copy-start.31
  21.4 145.3 %all-reduce.6.cloned.1.call-start = ((), (), s32[]{:S(2)}) async-start(), calls=%async_computation.2 | async-start | bytes 2621440 | tf_op jit(solution)/shard_map/psum | solution.py:389
  105.0 5.0 copy-start.1
  117.8 5.1 copy-start.1
  124.3 5.4 copy-start.43
  129.3 95.6 %all-reduce.8.cloned.1.call-start = ((), (), s32[]{:S(2)}) async-start(), calls=%async_computation.3 | async-start | bytes 2621440 | tf_op jit(solution)/shard_map/psum | solution.py:410
  166.6 2.9 copy-start.3
  166.6 3.3 copy-start.6
  169.9 1.7 copy-start.20
  171.6 1.9 copy-start.9
  171.6 2.1 copy-start.21
  173.7 1.9 copy-start.26
  179.4 2.2 copy-start.25
  179.4 2.2 copy-start.24
  185.8 174.1 %reduce-scatter.4.cloned.1.call-start = ((), (), s32[]{:S(2)}) async-start(), calls=%async_computation.4 | async-start | bytes 2949120
  224.9 4.9 copy-start.4
  224.9 4.9 copy-start.7
  224.9 5.0 copy-start.10
  224.9 5.2 copy-start.12
  230.1 2.0 copy-start.30
  242.9 2.1 copy-start.27
  242.9 2.1 copy-start.32
  246.9 1.5 copy-start.2
  256.1 2.1 copy-start.27
  256.1 2.1 copy-start.32
  289.1 143.9 %all-reduce.10.cloned.1.call-start = ((), (), s32[]{:S(2)}) async-start(), calls=%async_computation.5 | async-start | bytes 5242880 | tf_op jit(solution)/shard_map/psum | solution.py:399
  296.1 69.4 %copy-start.17 = (f32[5,128,2,64]{1,3,2,0:T(8,128)S(1)}, f32[5,128,2,64]{1,3,2,0:T(8,128)}, u32[]{:S(2)}) copy-start(f32[5,128,2,64]{1,3,2,0:T(8,128)} %copy-done.16) | copy-start | bytes 983044
  367.2 3.6 copy-start.29
  369.3 2.0 copy-start.23
  379.7 53.3 %copy-start.35 = (f32[640]{0:T(1024)S(1)}, f32[640]{0:T(1024)}, u32[]{:S(2)}) copy-start(f32[640]{0:T(1024)} %copy-done.34) | copy-start | bytes 7684
  379.7 53.3 %copy-start.37 = (f32[1024]{0:T(1024)S(1)}, f32[1024]{0:T(1024)}, u32[]{:S(2)}) copy-start(f32[1024]{0:T(1024)} %copy-done.36) | copy-start | bytes 12292
  437.7 98.3 %copy-start.11 = (bf16[640,1024]{0,1:T(8,128)(2,1)S(1)}, bf16[640,1024]{0,1:T(8,128)(2,1)}, u32[]{:S(2)}) copy-start(bf16[640,1024]{0,1:T(8,128)(2,1)} %copy.104) | copy-start | bytes 3932164
  530.1 5.9 %copy-start.5 = (f32[640,1024]{0,1:T(8,128)S(1)}, f32[640,1024]{0,1:T(8,128)}, u32[]{:S(2)}) copy-start(f32[640,1024]{0,1:T(8,128)} %copy.101) | copy-start | bytes 7864324
  530.1 5.9 %copy-start.8 = (bf16[640,1024]{0,1:T(8,128)(2,1)S(1)}, bf16[640,1024]{0,1:T(8,128)(2,1)}, u32[]{:S(2)}) copy-start(bf16[640,1024]{0,1:T(8,128)(2,1)} %all-reduce.6.cloned.1.call-done) | copy-start | bytes 3932164
  530.1 5.9 %copy-start.39 = (f32[640]{0:T(1024)S(1)}, f32[640]{0:T(1024)}, u32[]{:S(2)}) copy-start(f32[640]{0:T(1024)} %copy-done.38) | copy-start | bytes 7684
  540.7 4.9 copy-start.40
  540.7 4.9 copy-start.42
  540.7 44.6 %copy-start.33 = (f32[128,256]{1,0:T(8,128)S(1)}, f32[128,256]{1,0:T(8,128)}, u32[]{:S(2)}) copy-start(f32[128,256]{1,0:T(8,128)} %get-tuple-element.670) | copy-start | bytes 393220
  (7 other events, 7.1 us)
Sparse Core Ops, SparseCore 0:
  21.5 59.5 all-gather.1
  129.5 37.1 all-reduce.5
  185.9 38.9 all-reduce.7
  289.2 70.5 reduce-scatter.3
  374.0 58.9 all-reduce.9

commit v3 on v1

--- a/solution.py
+++ b/solution.py
@@ -3,7 +3,10 @@
 
 import jax
 import jax.numpy as jnp
+import numpy as np
 from jax import lax
+from jax.experimental import pallas as pl
+from jax.experimental.pallas import tpu as pltpu
 from jax.sharding import PartitionSpec as P
 
 EPS = 1e-05
@@ -168,7 +171,1148 @@
     return folded, jnp.moveaxis(grads, 0, 1).reshape((sequences, piece_rows) + grads.shape[3:])
 
 
-def on_device(
+MESH = pl.DeviceIdType.MESH
+MIB = 1 << 20
+
+
+def ring_place(index, count):
+    return lax.select(
+        lax.rem(index, 2) == 0, lax.div(index, 2), count - 1 - lax.div(index, 2)
+    )
+
+
+def ring_index(place, count):
+    place = lax.rem(place + 2 * count, count)
+    return lax.select(
+        place < lax.div(count, 2), 2 * place, 2 * (count - 1 - place) + 1
+    )
+
+
+class Ring:
+    def __init__(self, count, slots, send_sems, recv_sems):
+        self.count, self.slots = count, slots
+        self.send_sems, self.recv_sems = send_sems, recv_sems
+        self.other = lax.axis_index("wt")
+        self.place = ring_place(lax.axis_index("ctx"), count)
+        self.right = ring_index(self.place + 1, count)
+        self.left = ring_index(self.place + count - 1, count)
+        self.half = slots.shape[2] // 2
+
+    def copy(self, which, step, way):
+        rows = pl.ds(way * self.half, self.half)
+        later = step + 1 if isinstance(step, int) else lax.add(step, 1)
+        return pltpu.make_async_remote_copy(
+            src_ref=self.slots.at[which, step, rows],
+            dst_ref=self.slots.at[which, later, rows],
+            send_sem=self.send_sems.at[which, step, way],
+            recv_sem=self.recv_sems.at[which, step, way],
+            device_id=((self.right, self.left)[way], self.other),
+            device_id_type=MESH,
+        )
+
+    def tick(self, which, step, left_ref, right_ref, first=False, result=None):
+        half = self.half
+        rows = [
+            ring_index(target, self.count) * (2 * half) + way * half
+            for way, target in enumerate(
+                (self.place + self.count - 1 - step, self.place + 1 + step)
+            )
+        ]
+        left = jnp.concatenate(
+            [left_ref[pl.ds(pl.multiple_of(row, half), half), :] for row in rows], axis=0
+        )
+        total = jnp.dot(left, right_ref[...], preferred_element_type=jnp.float32)
+        if not first:
+            for way in range(2):
+                self.copy(which, step - 1, way).wait_recv()
+            total = total + self.slots[which, step].astype(jnp.float32)
+        if result is None:
+            self.slots[which, step] = total.astype(jnp.bfloat16)
+            for way in range(2):
+                self.copy(which, step, way).start()
+        else:
+            result[...] = total
+
+    def finish(self, which):
+        for way in range(2):
+
+            def wait(step, carry):
+                self.copy(which, step, way).wait_send()
+                return carry
+
+            lax.fori_loop(0, self.count - 1, wait, 0)
+
+
+def pair_lanes(shape):
+    return lax.broadcasted_iota(jnp.int32, shape, 1)
+
+
+def swap_halves(values, head_dim):
+    lanes = pair_lanes(values.shape)
+    width = values.shape[1]
+    quarter = head_dim // 2
+    return jnp.where(
+        lax.rem(lanes, head_dim) < quarter,
+        pltpu.roll(values, width - quarter, 1),
+        pltpu.roll(values, quarter, 1),
+    )
+
+
+def pair_mean(values, head_dim):
+    low = pair_lanes(values.shape) < head_dim
+    first = jnp.sum(jnp.where(low, values, 0.0), axis=-1, keepdims=True)
+    second = jnp.sum(jnp.where(low, 0.0, values), axis=-1, keepdims=True)
+    return jnp.where(low, first, second) * (1.0 / head_dim)
+
+
+def pair_norm(values, head_dim):
+    inverse = lax.rsqrt(pair_mean(values * values, head_dim) + EPS)
+    return values * inverse, inverse
+
+
+def double(row):
+    return jnp.concatenate([row, row], axis=-1)
+
+
+def dot_nn(left, right):
+    return jnp.dot(left, right, preferred_element_type=jnp.float32)
+
+
+def dot_nt(left, right):
+    return lax.dot_general(
+        left, right, (((1,), (1,)), ((), ())), preferred_element_type=jnp.float32
+    )
+
+
+def as_column(row):
+    size = row.shape[1]
+    rows = lax.broadcasted_iota(jnp.int32, (size, size), 0)
+    lanes = lax.broadcasted_iota(jnp.int32, (size, size), 1)
+    return jnp.sum(jnp.where(rows == lanes, row, 0.0), axis=1, keepdims=True)
+
+
+class Place:
+    def __init__(self, count):
+        self.count = count
+        self.ctx, self.wt = lax.axis_index("ctx"), lax.axis_index("wt")
+        self.odd = lax.rem(self.ctx, 2)
+        self.level = lax.div(self.ctx, 2)
+        self.core_bit = lax.rem(self.wt, 2)
+        self.beside_ctx = self.ctx + 1 - 2 * self.odd
+        self.beside = (self.beside_ctx, self.wt)
+        self.above = (lax.rem(self.ctx + 2, count), self.wt)
+        self.below = (lax.rem(self.ctx + count - 2, count), self.wt)
+        self.has_above = self.ctx + 2 < count
+        self.has_below = self.ctx >= 2
+        self.core_wt = self.wt + 1 - 2 * self.core_bit
+        self.chip_wt = lax.rem(self.wt + 2, 4)
+        self.far_wt = lax.rem(self.core_wt + 2, 4)
+        self.core = (self.ctx, self.core_wt)
+        self.chip = (self.ctx, self.chip_wt)
+
+    def greet(self, more=()):
+        barrier = pltpu.get_barrier_semaphore()
+        peers = [self.beside, self.core, self.chip, *more]
+        for peer in peers:
+            pl.semaphore_signal(barrier, inc=1, device_id=peer, device_id_type=MESH)
+        for there, peer in ((self.has_above, self.above), (self.has_below, self.below)):
+
+            @pl.when(there)
+            def _():
+                pl.semaphore_signal(barrier, inc=1, device_id=peer, device_id_type=MESH)
+
+        edges = self.has_above.astype(jnp.int32) + self.has_below.astype(jnp.int32)
+        pl.semaphore_wait(barrier, len(peers) + edges)
+
+
+    def greet_all(self):
+        barrier = pltpu.get_barrier_semaphore()
+
+        def signal(peer):
+            pl.semaphore_signal(barrier, inc=1, device_id=peer, device_id_type=MESH)
+
+        for shift in range(1, self.count):
+            signal((lax.rem(self.ctx + shift, self.count), self.wt))
+        signal(self.core)
+        signal(self.chip)
+        pl.semaphore_wait(barrier, self.count + 1)
+
+
+def send_to(source, target, send_sem, recv_sem, device):
+    return pltpu.make_async_remote_copy(
+        src_ref=source,
+        dst_ref=target,
+        send_sem=send_sem,
+        recv_sem=recv_sem,
+        device_id=device,
+        device_id_type=MESH,
+    )
+
+
+def forward_kernel(
+    count,
+    tokens,
+    segments,
+    table,
+    attn_gain,
+    q_gain,
+    k_gain,
+    w_query,
+    w_key,
+    w_value,
+    w_out,
+    residual,
+    heads_out,
+    mixed_t,
+    query_t,
+    logs,
+    starts,
+    keys_values,
+    keys_t,
+    query_raw,
+    key_raw,
+    normed_t,
+    all_segs,
+    all_out,
+    all_heads,
+    acc,
+    row_sum,
+    up_send,
+    up_recv,
+    side_send,
+    side_recv,
+    seg_send,
+    seg_recv,
+    out_send,
+    out_recv,
+    head_send,
+    head_recv,
+):
+    sequences, tile = segments.shape
+    head_dim = q_gain.shape[1]
+    levels = count // 2
+    here = Place(count)
+    me = here.ctx
+    all_segs[me] = jnp.zeros_like(all_segs[me])
+    all_segs[me, pl.ds(0, sequences)] = segments[...]
+    all_out[here.wt] = w_out[...]
+    here.greet()
+
+    def out_copy(hop, arriving=False):
+        sent = (here.wt, here.wt, here.chip_wt)
+        landed = (here.chip_wt, here.core_wt, here.far_wt)
+        ref = all_out.at[(landed if arriving else sent)[hop]]
+        device = here.chip if hop == 0 else here.core
+        return send_to(ref, ref, out_send.at[hop], out_recv.at[hop], device)
+
+    out_copy(0).start()
+    out_copy(1).start()
+
+    def rows_of(seq):
+        return pl.ds(pl.multiple_of(seq * tile, tile), tile)
+
+    def block_of(index, step):
+        return lax.rem(index - 2 * step + 2 * count, count)
+
+    def up_copy(step, seq):
+        rows = keys_values.at[block_of(me, step), rows_of(seq)]
+        return send_to(rows, rows, up_send.at[step, seq], up_recv.at[step, seq], here.above)
+
+    def up_wait(step, seq):
+        rows = keys_values.at[block_of(me, step), rows_of(seq)]
+        earlier = step - 1
+        send_to(
+            rows, rows, up_send.at[earlier, seq], up_recv.at[earlier, seq], here.above
+        ).wait_recv()
+
+    def side_copy(step, seq, index=me):
+        rows = keys_values.at[block_of(index, step), rows_of(seq)]
+        return send_to(
+            rows, rows, side_send.at[step, seq], side_recv.at[step, seq], here.beside
+        )
+
+    def side_wait(step, seq):
+        side_copy(step, seq, here.beside_ctx).wait_recv()
+
+    def seg_copy(step, way, index=me):
+        ref = all_segs.at[block_of(index, step)]
+        device = here.beside if way else here.above
+        return send_to(ref, ref, seg_send.at[step, way], seg_recv.at[step, way], device)
+
+    def seg_wait(step, way):
+        if way:
+            seg_copy(step, 1, here.beside_ctx).wait_recv()
+        else:
+            ref = all_segs.at[block_of(me, step)]
+            earlier = step - 1
+            send_to(
+                ref, ref, seg_send.at[earlier, 0], seg_recv.at[earlier, 0], here.above
+            ).wait_recv()
+
+    def goes_up(step):
+        return here.has_above & (me >= 2 * step)
+
+    def goes_aside(step):
+        block = me - 2 * step
+        return (block >= 0) & (block < here.beside_ctx)
+
+    def pass_segs(step):
+        @pl.when(goes_up(step))
+        def _():
+            seg_copy(step, 0).start()
+
+        @pl.when(goes_aside(step))
+        def _():
+            seg_copy(step, 1).start()
+
+    def pass_rows(step, seq):
+        @pl.when(goes_up(step))
+        def _():
+            up_copy(step, seq).start()
+
+        @pl.when(goes_aside(step))
+        def _():
+            side_copy(step, seq).start()
+
+    pass_segs(0)
+    cosine = table[:, pl.ds(0, 2 * head_dim)]
+    sine = table[:, pl.ds(2 * head_dim, 2 * head_dim)]
+    q_gain_pair = double(q_gain[...].astype(jnp.float32))
+    k_gain_pair = double(k_gain[...].astype(jnp.float32))
+    gain = attn_gain[...].astype(jnp.float32)
+
+    def turn(values):
+        return values * cosine + swap_halves(values, head_dim) * sine
+
+    def project(seq, carry):
+        rows = rows_of(seq)
+        inputs = tokens[rows, :].astype(jnp.float32)
+        inverse = lax.rsqrt(jnp.mean(inputs * inputs, axis=-1, keepdims=True) + EPS)
+        normed = (inputs * inverse * gain).astype(jnp.bfloat16)
+        raw_k = dot_nn(normed, w_key[...])
+        key_raw[rows, :] = raw_k
+        unit, unused = pair_norm(raw_k, head_dim)
+        keys_values[me, rows, pl.ds(0, 2 * head_dim)] = turn(unit * k_gain_pair).astype(
+            jnp.bfloat16
+        )
+        keys_values[me, rows, pl.ds(2 * head_dim, 2 * head_dim)] = dot_nn(
+            normed, w_value[...]
+        ).astype(jnp.bfloat16)
+        pass_rows(0, seq)
+        raw_q = dot_nn(normed, w_query[...])
+        query_raw[rows, :] = raw_q
+        query_t[seq] = jnp.zeros_like(query_t[seq])
+        for group in range(2):
+            unit, unused = pair_norm(
+                raw_q[:, group * 2 * head_dim : (group + 1) * 2 * head_dim], head_dim
+            )
+            turned = turn(unit * q_gain_pair) * (head_dim**-0.5)
+            flipped = turned.T.astype(jnp.bfloat16)
+            for member in range(2):
+                query_t[
+                    seq,
+                    pl.ds(group * head_dim, head_dim),
+                    pl.ds((2 * group + member) * tile, tile),
+                ] = flipped[member * head_dim : (member + 1) * head_dim]
+        normed_t[:, rows] = normed.T
+        acc[seq] = jnp.zeros_like(acc[seq])
+        row_sum[seq] = jnp.zeros_like(row_sum[seq])
+        starts[seq] = jnp.zeros_like(starts[seq])
+        return carry
+
+    lax.fori_loop(0, sequences, project, 0)
+    key_rows = lax.broadcasted_iota(jnp.int32, (tile, 4 * tile), 0)
+    query_cols = lax.rem(lax.broadcasted_iota(jnp.int32, (tile, 4 * tile), 1), tile)
+
+    def attend(block, seq, own):
+        rows = rows_of(seq)
+        keys = keys_values[block, rows, pl.ds(0, 2 * head_dim)]
+        values = keys_values[block, rows, pl.ds(2 * head_dim, 2 * head_dim)]
+        seg_query = all_segs[me, pl.ds(seq, 1)].astype(jnp.float32)
+        seg_key = as_column(all_segs[block, pl.ds(seq, 1)].astype(jnp.float32))
+        earlier = jnp.where(seg_key < seg_query, 1.0, 0.0)
+        starts[seq] += jnp.sum(earlier, axis=0, keepdims=True)
+        seg_wide = jnp.concatenate([seg_query] * 4, axis=1)
+        if own:
+            allowed = (seg_key == seg_wide) & (key_rows <= query_cols)
+        else:
+            allowed = seg_key >= seg_wide
+        scores = dot_nn(keys, query_t[seq])
+        weights = jnp.where(allowed, jnp.exp(scores), 0.0)
+        row_sum[seq] += jnp.sum(weights, axis=0, keepdims=True)
+        low = weights.astype(jnp.bfloat16)
+        values_t = values.T
+        for group in range(2):
+            acc[seq, group] += dot_nn(
+                values_t[group * head_dim : (group + 1) * head_dim],
+                low[:, group * 2 * tile : (group + 1) * 2 * tile],
+            )
+        keys_t[block, seq] = keys.T
+
+    def own_block(seq, carry):
+        attend(me, seq, True)
+        return carry
+
+    lax.fori_loop(0, sequences, own_block, 0)
+
+    @pl.when(goes_back_aside(here, 0))
+    def _():
+        seg_wait(0, 1)
+
+        def side_block(seq, carry):
+            side_wait(0, seq)
+            attend(here.beside_ctx, seq, False)
+            return carry
+
+        lax.fori_loop(0, sequences, side_block, 0)
+
+    out_copy(0, True).wait_recv()
+    out_copy(2).start()
+
+    def level(step, carry):
+        @pl.when(me >= 2 * step)
+        def _():
+            seg_wait(step, 0)
+            pass_segs(step)
+            seg_wait(step, 1)
+
+            def line_block(seq, carry):
+                up_wait(step, seq)
+                pass_rows(step, seq)
+                attend(me - 2 * step, seq, False)
+                return carry
+
+            lax.fori_loop(0, sequences, line_block, 0)
+
+            def side_block(seq, carry):
+                side_wait(step, seq)
+                attend(here.beside_ctx - 2 * step, seq, False)
+                return carry
+
+            lax.fori_loop(0, sequences, side_block, 0)
+
+        return carry
+
+    lax.fori_loop(1, levels, level, 0)
+
+    def head_copy(hop, seq, arriving=False):
+        sent = (here.wt, here.wt, here.chip_wt)
+        landed = (here.chip_wt, here.core_wt, here.far_wt)
+        ref = all_heads.at[(landed if arriving else sent)[hop], rows_of(seq)]
+        device = here.chip if hop == 0 else here.core
+        return send_to(ref, ref, head_send.at[hop, seq], head_recv.at[hop, seq], device)
+
+    def mix(seq, carry):
+        rows = rows_of(seq)
+        total = row_sum[seq]
+        logs[seq] = jnp.log(total)
+        for group in range(2):
+            cols = slice(group * 2 * tile, (group + 1) * 2 * tile)
+            part = acc[seq, group] / total[:, cols]
+            mixed = jnp.concatenate([part[:, :tile], part[:, tile:]], axis=0)
+            mixed_t[seq, group] = mixed
+            all_heads[here.wt, rows, pl.ds(group * 2 * head_dim, 2 * head_dim)] = mixed.T.astype(
+                jnp.bfloat16
+            )
+        head_copy(0, seq).start()
+        head_copy(1, seq).start()
+        return carry
+
+    lax.fori_loop(0, sequences, mix, 0)
+    heads_out[...] = all_heads[here.wt]
+    out_copy(1, True).wait_recv()
+    out_copy(2, True).wait_recv()
+
+    def finish(turn_, carry):
+        @pl.when(turn_ < sequences)
+        def _():
+            head_copy(0, turn_, True).wait_recv()
+            head_copy(2, turn_).start()
+
+        @pl.when(turn_ > 0)
+        def _():
+            seq = turn_ - 1
+            rows = rows_of(seq)
+            head_copy(1, seq, True).wait_recv()
+            head_copy(2, seq, True).wait_recv()
+            total = tokens[rows, :].astype(jnp.float32)
+            for slot in range(4):
+                total = total + dot_nt(all_heads[slot, rows], all_out[slot])
+            residual[rows, :] = total
+
+        return carry
+
+    lax.fori_loop(0, sequences + 1, finish, 0)
+    for hop in range(3):
+        out_copy(hop).wait_send()
+
+        def sent(seq, carry):
+            head_copy(hop, seq).wait_send()
+            return carry
+
+        lax.fori_loop(0, sequences, sent, 0)
+
+    def drain(step, carry):
+        @pl.when(goes_up(step))
+        def _():
+            seg_copy(step, 0).wait_send()
+
+            def sent(seq, carry):
+                up_copy(step, seq).wait_send()
+                return carry
+
+            lax.fori_loop(0, sequences, sent, 0)
+
+        @pl.when(goes_aside(step))
+        def _():
+            seg_copy(step, 1).wait_send()
+
+            def sent(seq, carry):
+                side_copy(step, seq).wait_send()
+                return carry
+
+            lax.fori_loop(0, sequences, sent, 0)
+
+        return carry
+
+    lax.fori_loop(0, levels, drain, 0)
+
+
+def goes_back_aside(here, step):
+    block = here.beside_ctx - 2 * step
+    return (block >= 0) & (block < here.ctx)
+
+
+def forward(tokens, segments, table, attn_gain, q_gain, k_gain, w_query, w_key, w_value, w_out):
+    count = lax.axis_size("ctx")
+    sequences, tile = segments.shape
+    rows, width = tokens.shape
+    head_dim = q_gain.shape[1]
+    pair = 2 * head_dim
+    levels = count // 2
+    vmem = pl.BlockSpec(memory_space=pltpu.VMEM)
+    f32, bf16 = jnp.float32, jnp.bfloat16
+    outs = [
+        ((rows, width), f32),
+        ((rows, 2 * pair), bf16),
+        ((sequences, 2, pair, tile), f32),
+        ((sequences, pair, 4 * tile), bf16),
+        ((sequences, 1, 4 * tile), f32),
+        ((sequences, 1, tile), f32),
+        ((count, rows, 2 * pair), bf16),
+        ((count, sequences, pair, tile), bf16),
+        ((rows, 2 * pair), f32),
+        ((rows, pair), f32),
+        ((width, rows), bf16),
+    ]
+    dma = pltpu.SemaphoreType.DMA
+    return pl.pallas_call(
+        partial(forward_kernel, count),
+        out_shape=[jax.ShapeDtypeStruct(shape, kind) for shape, kind in outs],
+        in_specs=[vmem] * 10,
+        out_specs=[vmem] * len(outs),
+        scratch_shapes=[
+            pltpu.VMEM((count, 8, tile), jnp.int32),
+            pltpu.VMEM((4, width, 2 * pair), bf16),
+            pltpu.VMEM((4, rows, 2 * pair), bf16),
+            pltpu.VMEM((sequences, 2, head_dim, 2 * tile), f32),
+            pltpu.VMEM((sequences, 1, 4 * tile), f32),
+            dma((levels, sequences)),
+            dma((levels, sequences)),
+            dma((levels, sequences)),
+            dma((levels, sequences)),
+            dma((levels, 2)),
+            dma((levels, 2)),
+            dma((3,)),
+            dma((3,)),
+            dma((3, sequences)),
+            dma((3, sequences)),
+        ],
+        compiler_params=pltpu.CompilerParams(
+            collective_id=2, has_side_effects=True, vmem_limit_bytes=60 * MIB
+        ),
+    )(tokens, segments, table, attn_gain, q_gain, k_gain, w_query, w_key, w_value, w_out)
+
+
+class WtSum:
+    def __init__(self, here, tile, part, got, far, full, send_sems, recv_sems):
+        self.here, self.tile = here, tile
+        self.part, self.got, self.far, self.full = part, got, far, full
+        self.send_sems, self.recv_sems = send_sems, recv_sems
+        self.mine, self.theirs = here.core_bit, 1 - here.core_bit
+
+    def rows(self, seq):
+        return pl.ds(pl.multiple_of(seq * self.tile, self.tile), self.tile)
+
+    def copy(self, hop, seq, arriving=False):
+        rows = self.rows(seq)
+        half = self.theirs if arriving else self.mine
+        source = (
+            self.part.at[self.theirs, rows],
+            self.got.at[rows],
+            self.full.at[half, rows],
+        )[hop]
+        target = (self.got.at[rows], self.far.at[rows], self.full.at[half, rows])[hop]
+        device = self.here.chip if hop == 1 else self.here.core
+        return send_to(
+            source, target, self.send_sems.at[hop, seq], self.recv_sems.at[hop, seq], device
+        )
+
+    def offer(self, seq, value):
+        rows = self.rows(seq)
+        half = value.shape[1] // 2
+        self.part[0, rows] = value[:, :half].astype(jnp.bfloat16)
+        self.part[1, rows] = value[:, half:].astype(jnp.bfloat16)
+        self.copy(0, seq).start()
+
+    def cross(self, seq):
+        rows = self.rows(seq)
+        self.copy(0, seq).wait_recv()
+        total = self.part[self.mine, rows].astype(jnp.float32) + self.got[rows].astype(
+            jnp.float32
+        )
+        self.got[rows] = total.astype(jnp.bfloat16)
+        self.copy(1, seq).start()
+
+    def close(self, seq):
+        rows = self.rows(seq)
+        self.copy(1, seq).wait_recv()
+        total = self.got[rows].astype(jnp.float32) + self.far[rows].astype(jnp.float32)
+        self.full[self.mine, rows] = total.astype(jnp.bfloat16)
+        self.copy(2, seq).start()
+
+    def result(self, seq):
+        rows = self.rows(seq)
+        self.copy(2, seq, True).wait_recv()
+        return jnp.concatenate([self.full[0, rows], self.full[1, rows]], axis=1).astype(
+            jnp.float32
+        )
+
+    def finish(self, sequences):
+        def sent(seq, carry):
+            for hop in range(3):
+                self.copy(hop, seq).wait_send()
+            return carry
+
+        lax.fori_loop(0, sequences, sent, 0)
+
+
+def wt_sum_scratch(sequences, rows, width):
+    half = width // 2
+    return [
+        pltpu.VMEM((2, rows, half), jnp.bfloat16),
+        pltpu.VMEM((rows, half), jnp.bfloat16),
+        pltpu.VMEM((rows, half), jnp.bfloat16),
+        pltpu.VMEM((2, rows, half), jnp.bfloat16),
+        pltpu.SemaphoreType.DMA((3, sequences)),
+        pltpu.SemaphoreType.DMA((3, sequences)),
+    ]
+
+
+def ring_scratch(count, arrays, rows, width):
+    return [
+        pltpu.VMEM((arrays, count, rows, width), jnp.bfloat16),
+        pltpu.SemaphoreType.DMA((arrays, count - 1, 2)),
+        pltpu.SemaphoreType.DMA((arrays, count - 1, 2)),
+    ]
+
+
+class GainSum:
+    def __init__(self, here, slots, beside, sends, recvs, pair_sends, pair_recvs):
+        self.here, self.slots, self.beside = here, slots, beside
+        self.sends, self.recvs = sends, recvs
+        self.pair_sends, self.pair_recvs = pair_sends, pair_recvs
+
+    def copy(self, shift, arriving=False):
+        here = self.here
+        target = lax.rem(here.ctx + shift, here.count)
+        origin = lax.rem(here.ctx + here.count - shift, here.count)
+        ref = self.slots.at[origin if arriving else here.ctx]
+        return send_to(
+            ref, ref, self.sends.at[shift - 1], self.recvs.at[shift - 1], (target, here.wt)
+        )
+
+    def pair_copy(self, hop):
+        device = (self.here.core, self.here.chip)[hop]
+        return send_to(
+            self.beside.at[hop, 0],
+            self.beside.at[hop, 1],
+            self.pair_sends.at[hop],
+            self.pair_recvs.at[hop],
+            device,
+        )
+
+    def start(self):
+        for shift in range(1, self.here.count):
+            self.copy(shift).start()
+
+    def total(self):
+        for shift in range(1, self.here.count):
+            self.copy(shift, True).wait_recv()
+        total = self.slots[0]
+        for index in range(1, self.here.count):
+            total = total + self.slots[index]
+        for hop in range(2):
+            self.beside[hop, 0] = total
+            self.pair_copy(hop).start()
+            self.pair_copy(hop).wait_recv()
+            total = total + self.beside[hop, 1]
+        for shift in range(1, self.here.count):
+            self.copy(shift).wait_send()
+        for hop in range(2):
+            self.pair_copy(hop).wait_send()
+        return total
+
+
+def backward_kernel(count, *refs):
+    (
+        grad_res,
+        tokens,
+        table,
+        attn_gain,
+        q_gain,
+        k_gain,
+        w_query,
+        w_key,
+        w_value,
+        w_out,
+        heads,
+        mixed_t,
+        query_t,
+        logs,
+        starts,
+        keys_values,
+        keys_t,
+        query_raw,
+        key_raw,
+        normed_t,
+        cot_t,
+        normed_ffn_t,
+        ffn_grads,
+        ffn_gain_part,
+    ) = refs[:24]
+    (
+        tokens_grad,
+        down_sum,
+        gate_sum,
+        up_sum,
+        out_sum,
+        query_sum,
+        key_sum,
+        value_sum,
+        attn_gain_sum,
+        ffn_gain_sum,
+        q_gain_sum,
+        k_gain_sum,
+    ) = refs[24:36]
+    (
+        grad_res_t,
+        grad_heads_t,
+        deltas,
+        grad_query_t,
+        own_grads,
+        grad_qkv,
+        side_in,
+        side_out,
+        line_in,
+        line_out,
+        qkv_total,
+        side_send,
+        side_recv,
+        line_send,
+        line_recv,
+    ) = refs[36:51]
+    rest = refs[51:]
+    sequences, tile = mixed_t.shape[0], mixed_t.shape[3]
+    head_dim = q_gain.shape[1]
+    pair = 2 * head_dim
+    levels = count // 2
+    here = Place(count)
+    me = here.ctx
+    wt_sum = WtSum(here, tile, *rest[:6])
+    gains = GainSum(here, *rest[6:12])
+    gain_slots = rest[6]
+    ffn = Ring(count, *rest[12:15])
+    out = Ring(count, *rest[15:18])
+    qkv = Ring(count, *rest[18:21])
+    last = count - 1
+    here.greet_all()
+    lefts = (cot_t, normed_ffn_t, normed_ffn_t)
+    ffn_sums = (down_sum, gate_sum, up_sum)
+
+    def ffn_ticks(step, first=False, final=False):
+        for i in range(3):
+            ffn.tick(
+                i,
+                step,
+                lefts[i],
+                ffn_grads.at[i],
+                first=first,
+                result=ffn_sums[i] if final else None,
+            )
+
+    def rows_of(seq):
+        return pl.ds(pl.multiple_of(seq * tile, tile), tile)
+
+    ffn_ticks(0, first=True)
+
+    def prepare(seq, carry):
+        rows = rows_of(seq)
+        grads = grad_res[rows, :]
+        grad_res_t[:, rows] = grads.T
+        grad_heads_t[seq] = jnp.zeros_like(grad_heads_t[seq])
+        low = dot_nn(grads, w_out[...]).astype(jnp.bfloat16)
+        for group in range(2):
+            flipped = low[:, group * pair : (group + 1) * pair].T
+            product_t = flipped.astype(jnp.float32) * mixed_t[seq, group]
+            for member in range(2):
+                part = slice(member * head_dim, (member + 1) * head_dim)
+                cols = pl.ds((2 * group + member) * tile, tile)
+                grad_heads_t[seq, pl.ds(group * head_dim, head_dim), cols] = flipped[part]
+                deltas[seq, :, cols] = jnp.sum(product_t[part], axis=0, keepdims=True)
+        grad_query_t[seq] = jnp.zeros_like(grad_query_t[seq])
+        return carry
+
+    lax.fori_loop(0, sequences, prepare, 0)
+    out.tick(0, 0, grad_res_t, heads, first=True)
+    key_rows = lax.broadcasted_iota(jnp.int32, (tile, 4 * tile), 0)
+    query_cols = lax.rem(lax.broadcasted_iota(jnp.int32, (tile, 4 * tile), 1), tile)
+
+    def grads_of(block, seq, own):
+        rows = rows_of(seq)
+        keys = keys_values[block, rows, pl.ds(0, pair)]
+        values = keys_values[block, rows, pl.ds(pair, pair)]
+        places = (key_rows + block * tile).astype(jnp.float32)
+        start = starts[seq]
+        allowed = places >= jnp.concatenate([start] * 4, axis=1)
+        if own:
+            allowed = allowed & (key_rows <= query_cols)
+        queries = query_t[seq]
+        grad_heads = grad_heads_t[seq]
+        scores = dot_nn(keys, queries)
+        probs = jnp.where(allowed, jnp.exp(scores - logs[seq]), 0.0)
+        grad_probs = dot_nn(values, grad_heads)
+        grad_scores = (probs * (grad_probs - deltas[seq])).astype(jnp.bfloat16)
+        flipped = keys_t[block, seq]
+        for group in range(2):
+            cols = slice(group * 2 * tile, (group + 1) * 2 * tile)
+            grad_query_t[seq, group] += dot_nn(
+                flipped[group * head_dim : (group + 1) * head_dim], grad_scores[:, cols]
+            )
+        grad_keys = dot_nt(grad_scores, queries)
+        grad_values = dot_nt(probs.astype(jnp.bfloat16), grad_heads)
+        return jnp.concatenate([grad_keys, grad_values], axis=1)
+
+    def side_copy(step, seq):
+        return send_to(
+            side_out.at[step, rows_of(seq)],
+            side_in.at[step, rows_of(seq)],
+            side_send.at[step, seq],
+            side_recv.at[step, seq],
+            here.beside,
+        )
+
+    def line_copy(step, seq):
+        earlier = step - 1
+        return send_to(
+            line_out.at[earlier, rows_of(seq)],
+            line_in.at[earlier, rows_of(seq)],
+            line_send.at[earlier, seq],
+            line_recv.at[earlier, seq],
+            here.below,
+        )
+
+    def from_above(step, seq):
+        later = step + 1
+        return line_copy(later, seq)
+
+    def block_there(step):
+        block = here.beside_ctx - 2 * step
+        return (block >= 0) & (block < me)
+
+    def block_comes(step):
+        return (me >= 2 * step) & (me - 2 * step < here.beside_ctx)
+
+    def send_aside(step):
+        @pl.when(block_there(step))
+        def _():
+            def one(seq, carry):
+                side_out[step, rows_of(seq)] = grads_of(
+                    here.beside_ctx - 2 * step, seq, False
+                ).astype(jnp.bfloat16)
+                side_copy(step, seq).start()
+                return carry
+
+            lax.fori_loop(0, sequences, one, 0)
+
+    def level(turn_, carry):
+        step = levels - 1 - turn_
+        send_aside(step)
+
+        @pl.when(me >= 2 * step)
+        def _():
+            def one(seq, carry):
+                rows = rows_of(seq)
+                own_grads[rows, :] = grads_of(me - 2 * step, seq, False)
+                side_copy(step, seq).wait_recv()
+                total = own_grads[rows, :] + side_in[step, rows].astype(jnp.float32)
+                own_grads[rows, :] = total
+
+                @pl.when(here.has_above)
+                def _():
+                    from_above(step, seq).wait_recv()
+                    own_grads[rows, :] += line_in[step, rows].astype(jnp.float32)
+
+                line_out[step - 1, rows] = own_grads[rows, :].astype(jnp.bfloat16)
+                line_copy(step, seq).start()
+                return carry
+
+            lax.fori_loop(0, sequences, one, 0)
+
+        ffn_ticks(1 + turn_)
+        return carry
+
+    lax.fori_loop(0, levels - 1, level, 0)
+    send_aside(0)
+
+    def own_block(seq, carry):
+        own_grads[rows_of(seq), :] = grads_of(me, seq, True)
+        return carry
+
+    lax.fori_loop(0, sequences, own_block, 0)
+    ffn_ticks(levels)
+    out.tick(0, 1, grad_res_t, heads)
+    cosine = table[:, pl.ds(0, pair)]
+    sine = table[:, pl.ds(pair, pair)]
+    q_gain_pair = double(q_gain[...].astype(jnp.float32))
+    k_gain_pair = double(k_gain[...].astype(jnp.float32))
+    gain = attn_gain[...].astype(jnp.float32)
+    gain_slots[me] = jnp.zeros_like(gain_slots[me])
+    gain_slots[me, pl.ds(1, 1)] = ffn_gain_part[...]
+
+    def back_through(grads, raw, gain_pair, row):
+        turned = grads * cosine - swap_halves(grads, head_dim) * sine
+        unit, inverse = pair_norm(raw, head_dim)
+        gain_slots[me, pl.ds(row, 1), pl.ds(0, pair)] += jnp.sum(
+            turned * unit, axis=0, keepdims=True
+        )
+        scaled = turned * gain_pair
+        return (inverse * (scaled - unit * pair_mean(scaled * unit, head_dim))).astype(
+            jnp.bfloat16
+        )
+
+    def token_unit(rows):
+        inputs = tokens[rows, :].astype(jnp.float32)
+        inverse = lax.rsqrt(jnp.mean(inputs * inputs, axis=-1, keepdims=True) + EPS)
+        return inputs * inverse, inverse
+
+    def project_back(seq, carry):
+        rows = rows_of(seq)
+        for group in range(2):
+            grads = grad_query_t[seq, group] * (head_dim**-0.5)
+            grads = jnp.concatenate([grads[:, :tile], grads[:, tile:]], axis=0).T
+            cols = pl.ds(group * pair, pair)
+            grad_qkv[rows, cols] = back_through(grads, query_raw[rows, cols], q_gain_pair, 2)
+
+        @pl.when(block_comes(0))
+        def _():
+            side_copy(0, seq).wait_recv()
+            own_grads[rows, :] += side_in[0, rows].astype(jnp.float32)
+
+        @pl.when(here.has_above)
+        def _():
+            from_above(0, seq).wait_recv()
+            own_grads[rows, :] += line_in[0, rows].astype(jnp.float32)
+
+        grad_qkv[rows, pl.ds(2 * pair, pair)] = back_through(
+            own_grads[rows, pl.ds(0, pair)], key_raw[rows, :], k_gain_pair, 3
+        )
+        grad_qkv[rows, pl.ds(3 * pair, pair)] = own_grads[rows, pl.ds(pair, pair)].astype(
+            jnp.bfloat16
+        )
+        grads = (
+            dot_nt(grad_qkv[rows, pl.ds(0, 2 * pair)], w_query[...])
+            + dot_nt(grad_qkv[rows, pl.ds(2 * pair, pair)], w_key[...])
+            + dot_nt(grad_qkv[rows, pl.ds(3 * pair, pair)], w_value[...])
+        )
+        unit, inverse = token_unit(rows)
+        gain_slots[me, pl.ds(0, 1)] += jnp.sum(grads * unit, axis=0, keepdims=True)
+        wt_sum.offer(seq, grads)
+        return carry
+
+    lax.fori_loop(0, sequences, project_back, 0)
+    gains.start()
+    qkv.tick(0, 0, normed_t, grad_qkv, first=True)
+
+    def crossing(seq, carry):
+        wt_sum.cross(seq)
+        return carry
+
+    lax.fori_loop(0, sequences, crossing, 0)
+
+    def tail(step, carry):
+        qkv.tick(0, step, normed_t, grad_qkv)
+        out.tick(0, step + 1, grad_res_t, heads)
+
+        @pl.when(step + levels < last)
+        def _():
+            ffn_ticks(step + levels)
+
+        return carry
+
+    lax.fori_loop(1, last - 1, tail, 0)
+    ffn_ticks(last, final=True)
+    out.tick(0, last, grad_res_t, heads, result=out_sum)
+
+    def closing(seq, carry):
+        wt_sum.close(seq)
+        return carry
+
+    lax.fori_loop(0, sequences, closing, 0)
+    qkv.tick(0, last - 1, normed_t, grad_qkv)
+
+    def token_rows(seq, carry):
+        rows = rows_of(seq)
+        unit, inverse = token_unit(rows)
+        scaled = wt_sum.result(seq) * gain
+        grads = inverse * (scaled - unit * jnp.mean(scaled * unit, axis=-1, keepdims=True))
+        tokens_grad[rows, :] = (grad_res[rows, :].astype(jnp.float32) + grads).astype(
+            jnp.bfloat16
+        )
+        return carry
+
+    lax.fori_loop(0, sequences, token_rows, 0)
+    total = gains.total()
+    attn_gain_sum[...] = total[0:1]
+    ffn_gain_sum[...] = total[1:2]
+    folded = total[:, :pair]
+    folded = folded + pltpu.roll(folded, head_dim, 1)
+    q_gain_sum[...] = folded[2:3, :head_dim]
+    k_gain_sum[...] = folded[3:4, :head_dim]
+    qkv.tick(0, last, normed_t, grad_qkv, result=qkv_total)
+    query_sum[...] = qkv_total[:, pl.ds(0, 2 * pair)]
+    key_sum[...] = qkv_total[:, pl.ds(2 * pair, pair)]
+    value_sum[...] = qkv_total[:, pl.ds(3 * pair, pair)]
+    wt_sum.finish(sequences)
+    for i in range(3):
+        ffn.finish(i)
+    out.finish(0)
+    qkv.finish(0)
+
+    def drain(step, carry):
+        @pl.when(block_there(step))
+        def _():
+            def sent(seq, carry):
+                side_copy(step, seq).wait_send()
+                return carry
+
+            lax.fori_loop(0, sequences, sent, 0)
+
+        @pl.when((step > 0) & (me >= 2 * step))
+        def _():
+            def sent(seq, carry):
+                line_copy(step, seq).wait_send()
+                return carry
+
+            lax.fori_loop(0, sequences, sent, 0)
+
+        return carry
+
+    lax.fori_loop(0, levels, drain, 0)
+
+
+def backward(*arrays):
+    (grad_res, tokens, table, attn_gain, q_gain) = arrays[:5]
+    mixed_t, cot_t, ffn_grads = arrays[11], arrays[20], arrays[22]
+    count = lax.axis_size("ctx")
+    sequences, tile = mixed_t.shape[0], mixed_t.shape[3]
+    rows, width = tokens.shape
+    head_dim = q_gain.shape[1]
+    pair = 2 * head_dim
+    levels = count // 2
+    block = width // count
+    hidden = ffn_grads.shape[2]
+    vmem = pl.BlockSpec(memory_space=pltpu.VMEM)
+    f32, bf16 = jnp.float32, jnp.bfloat16
+    outs = [
+        ((rows, width), bf16),
+        ((block, hidden), f32),
+        ((block, hidden), f32),
+        ((block, hidden), f32),
+        ((block, 2 * pair), f32),
+        ((block, 2 * pair), f32),
+        ((block, pair), f32),
+        ((block, pair), f32),
+        ((1, width), f32),
+        ((1, width), f32),
+        ((1, head_dim), f32),
+        ((1, head_dim), f32),
+    ]
+    dma = pltpu.SemaphoreType.DMA
+    return pl.pallas_call(
+        partial(backward_kernel, count),
+        out_shape=[jax.ShapeDtypeStruct(shape, kind) for shape, kind in outs],
+        in_specs=[vmem] * len(arrays),
+        out_specs=[vmem] * len(outs),
+        scratch_shapes=[
+            pltpu.VMEM((width, rows), bf16),
+            pltpu.VMEM((sequences, pair, 4 * tile), bf16),
+            pltpu.VMEM((sequences, 1, 4 * tile), f32),
+            pltpu.VMEM((sequences, 2, head_dim, 2 * tile), f32),
+            pltpu.VMEM((rows, 2 * pair), f32),
+            pltpu.VMEM((rows, 4 * pair), bf16),
+            pltpu.VMEM((levels, rows, 2 * pair), bf16),
+            pltpu.VMEM((levels, rows, 2 * pair), bf16),
+            pltpu.VMEM((levels - 1, rows, 2 * pair), bf16),
+            pltpu.VMEM((levels - 1, rows, 2 * pair), bf16),
+            pltpu.VMEM((block, 4 * pair), f32),
+            dma((levels, sequences)),
+            dma((levels, sequences)),
+            dma((levels - 1, sequences)),
+            dma((levels - 1, sequences)),
+            *wt_sum_scratch(sequences, rows, width),
+            pltpu.VMEM((count, 8, width), f32),
+            pltpu.VMEM((2, 2, 8, width), f32),
+            dma((count - 1,)),
+            dma((count - 1,)),
+            dma((2,)),
+            dma((2,)),
+            *ring_scratch(count, 3, block, hidden),
+            *ring_scratch(count, 1, block, 2 * pair),
+            *ring_scratch(count, 1, block, 4 * pair),
+        ],
+        compiler_params=pltpu.CompilerParams(
+            collective_id=3, has_side_effects=True, vmem_limit_bytes=62 * MIB
+        ),
+    )(*arrays)
+
+
+def rotary_table(length, head_dim):
+    half = head_dim // 2
+    frequency = THETA ** (-2.0 * np.arange(half) / head_dim)
+    angles = np.arange(length)[:, None] * frequency[None, :]
+    cosine, sine = np.cos(angles), np.sin(angles)
+    return np.concatenate([cosine] * 4 + [-sine, sine] * 2, axis=1).astype(np.float32)
+
+
+def kernels_fit(tokens, w_query, key_matrix, q_gain):
+    sequences, tile, width = tokens.shape
+    count, head_dim = lax.axis_size("ctx"), q_gain.shape[0]
+    return (
+        lax.axis_size("wt") == 4
+        and count % 2 == 0
+        and count >= 4
+        and tile == 128
+        and sequences <= 8
+        and sequences * count <= 40
+        and head_dim == 64
+        and w_query.shape[1] == 4 * head_dim
+        and key_matrix.shape[1] == 2 * head_dim
+        and width % (128 * count) == 0
+    )
+
+
+def on_device_plain(
     tokens,
     segments,
     attn_gain,
@@ -255,14 +1399,11 @@
     ).astype(jnp.bfloat16)
     log_total = row_max + jnp.log(row_sum)
     grad_rows = cotangent.reshape(all_rows, model_width)
-    w_down_grad = transpose_by(grad_rows, hidden_low)
     grad_hidden = product(grad_rows, w_down)
     grad_gate = (
         grad_hidden * up_proj * gate_sigmoid * (1.0 + gate_proj * (1.0 - gate_sigmoid))
     ).astype(jnp.bfloat16)
     grad_up = (grad_hidden * gate_silu).astype(jnp.bfloat16)
-    w_gate_grad = transpose_by(normed_ffn_low, grad_gate)
-    w_up_grad = transpose_by(normed_ffn_low, grad_up)
     grad_normed_ffn = by_transpose(grad_gate, w_gate) + by_transpose(grad_up, w_up)
     ffn_gain_part = jnp.sum(grad_normed_ffn * ffn_unit, axis=0)
     grad_normed_ffn = lax.psum(grad_normed_ffn.astype(jnp.bfloat16), "wt").astype(jnp.float32)
@@ -270,7 +1411,6 @@
         grad_normed_ffn, ffn_unit, ffn_inverse, ffn_gain
     )
     grad_residual_low = grad_residual.astype(jnp.bfloat16)
-    w_out_grad = transpose_by(grad_residual_low, mixed_low)
     grad_heads_low = product(grad_residual_low, w_out).astype(jnp.bfloat16)
     grad_groups = grad_heads_low.reshape(sequences, seq_rows, kv_local, per_group, head_dim)
     delta_rows = jnp.sum(grad_groups.astype(jnp.float32) * mixed_heads, axis=-1)
@@ -315,9 +1455,6 @@
         .reshape(all_rows, kv_local * head_dim)
     )
     grad_value_low = grad_value.astype(jnp.bfloat16).reshape(all_rows, kv_local * head_dim)
-    w_query_grad = transpose_by(normed_low, grad_query_low)
-    w_key_grad = transpose_by(normed_low, grad_key_low)
-    w_value_grad = transpose_by(normed_low, grad_value_low)
     grad_normed = (
         by_transpose(grad_query_low, w_query)
         + by_transpose(grad_key_low, key_matrix)
@@ -331,13 +1468,13 @@
     output = output_rows.reshape(sequences, seq_rows, model_width)
     tokens_grad = tokens_rows.reshape(sequences, seq_rows, model_width)
     partial_sums = (
-        w_down_grad,
-        w_gate_grad,
-        w_up_grad,
-        w_out_grad,
-        w_query_grad,
-        w_key_grad,
-        w_value_grad,
+        transpose_by(grad_rows, hidden_low),
+        transpose_by(normed_ffn_low, grad_gate),
+        transpose_by(normed_ffn_low, grad_up),
+        transpose_by(grad_residual_low, mixed_low),
+        transpose_by(normed_low, grad_query_low),
+        transpose_by(normed_low, grad_key_low),
+        transpose_by(normed_low, grad_value_low),
     )
     summed = [
         lax.psum_scatter(part.astype(jnp.bfloat16), "ctx", scatter_dimension=0, tiled=True).astype(
@@ -345,7 +1482,8 @@
         )
         for part in partial_sums
     ]
-    w_down_grad, w_gate_grad, w_up_grad, w_out_grad, w_query_grad, w_key_grad, w_value_grad = summed
+    w_down_grad, w_gate_grad, w_up_grad, w_out_grad = summed[:4]
+    w_query_grad, w_key_grad, w_value_grad = summed[4:]
     attn_gain_grad, q_gain_grad, k_gain_grad, ffn_gain_grad = lax.psum(
         (attn_gain_part, q_gain_part, k_gain_part, ffn_gain_part), ("ctx", "wt")
     )
@@ -360,6 +1498,142 @@
         k_gain_grad,
         w_out_grad,
         ffn_gain_grad,
+        w_gate_grad,
+        w_up_grad,
+        w_down_grad,
+    )
+
+
+def on_device(
+    tokens,
+    segments,
+    attn_gain,
+    w_query,
+    key_matrix,
+    value_matrix,
+    q_gain,
+    k_gain,
+    w_out,
+    ffn_gain,
+    w_gate,
+    w_up,
+    w_down,
+    cotangent,
+):
+    if not kernels_fit(tokens, w_query, key_matrix, q_gain):
+        return on_device_plain(
+            tokens,
+            segments,
+            attn_gain,
+            w_query,
+            key_matrix,
+            value_matrix,
+            q_gain,
+            k_gain,
+            w_out,
+            ffn_gain,
+            w_gate,
+            w_up,
+            w_down,
+            cotangent,
+        )
+    sequences, seq_rows, model_width = tokens.shape
+    count, head_dim = lax.axis_size("ctx"), q_gain.shape[0]
+    token_rows = tokens.reshape(sequences * seq_rows, model_width)
+    table = lax.dynamic_slice_in_dim(
+        jnp.asarray(rotary_table(count * seq_rows, head_dim)),
+        lax.axis_index("ctx") * seq_rows,
+        seq_rows,
+        0,
+    )
+    gains = (attn_gain[None], q_gain[None], k_gain[None])
+    (
+        residual,
+        heads,
+        mixed_t,
+        query_t,
+        logs,
+        starts,
+        keys_values,
+        keys_t,
+        query_raw,
+        key_raw,
+        normed_t,
+    ) = forward(
+        token_rows, segments, table, *gains, w_query, key_matrix, value_matrix, w_out
+    )
+    normed_ffn, ffn_unit, ffn_inverse = norm_rows(residual, ffn_gain)
+    normed_ffn_low = normed_ffn.astype(jnp.bfloat16)
+    gate_proj = product(normed_ffn_low, w_gate)
+    up_proj = product(normed_ffn_low, w_up)
+    gate_sigmoid = jax.nn.sigmoid(gate_proj)
+    gate_silu = gate_proj * gate_sigmoid
+    hidden_low = (gate_silu * up_proj).astype(jnp.bfloat16)
+    mlp_term = by_transpose(hidden_low, w_down)
+    output_rows = (
+        residual + lax.psum(mlp_term.astype(jnp.bfloat16), "wt").astype(jnp.float32)
+    ).astype(jnp.bfloat16)
+    grad_rows = cotangent.reshape(token_rows.shape)
+    grad_hidden = product(grad_rows, w_down)
+    grad_gate = (
+        grad_hidden * up_proj * gate_sigmoid * (1.0 + gate_proj * (1.0 - gate_sigmoid))
+    ).astype(jnp.bfloat16)
+    grad_up = (grad_hidden * gate_silu).astype(jnp.bfloat16)
+    grad_normed_ffn = by_transpose(grad_gate, w_gate) + by_transpose(grad_up, w_up)
+    ffn_gain_part = jnp.sum(grad_normed_ffn * ffn_unit, axis=0, keepdims=True)
+    grad_normed_ffn = lax.psum(grad_normed_ffn.astype(jnp.bfloat16), "wt").astype(jnp.float32)
+    grad_residual = (
+        grad_rows.astype(jnp.float32)
+        + norm_back(grad_normed_ffn, ffn_unit, ffn_inverse, ffn_gain)
+    ).astype(jnp.bfloat16)
+    (
+        tokens_grad,
+        w_down_grad,
+        w_gate_grad,
+        w_up_grad,
+        w_out_grad,
+        w_query_grad,
+        w_key_grad,
+        w_value_grad,
+        attn_gain_grad,
+        ffn_gain_grad,
+        q_gain_grad,
+        k_gain_grad,
+    ) = backward(
+        grad_residual,
+        token_rows,
+        table,
+        *gains,
+        w_query,
+        key_matrix,
+        value_matrix,
+        w_out,
+        heads,
+        mixed_t,
+        query_t,
+        logs,
+        starts,
+        keys_values,
+        keys_t,
+        query_raw,
+        key_raw,
+        normed_t,
+        grad_rows.T,
+        normed_ffn_low.T,
+        jnp.stack([hidden_low, grad_gate, grad_up]),
+        ffn_gain_part,
+    )
+    return (
+        output_rows.reshape(tokens.shape),
+        tokens_grad.reshape(tokens.shape),
+        attn_gain_grad[0],
+        w_query_grad,
+        w_key_grad,
+        w_value_grad,
+        q_gain_grad[0],
+        k_gain_grad[0],
+        w_out_grad,
+        ffn_gain_grad[0],
         w_gate_grad,
         w_up_grad,
         w_down_grad,

time: 931 us -> 319 us (0.34)
  waiting for transfers between devices: 639 us -> 79.9 us
  Pallas kernels: 0 us -> 173 us
  blocking collectives: 72.4 us -> 0 us
  matrix products: 76.4 us -> 15.9 us
  local copies, waits for them, and re-layouts: 72.4 us -> 19.5 us
  other arithmetic: 47.5 us -> 15.8 us
    reduce_scatter x6 -> x0, waiting for transfers between devices: 374 us -> none  [on_device(): lax.psum_scatter(part.astype(jnp.bfloat16), 'ctx', scatter_dimension=0, t...]
    pallas_call x0 -> x2, Pallas kernels: none -> 173 us  [the longest x1 140 us: backward(): pl.pallas_call(partial(backward_kernel, count), out_shape=[jax.ShapeDtype...]
    unnamed x14 -> x1, waiting for transfers between devices: 107 us -> 0.02 us
    psum x2 -> x0, waiting for transfers between devices: 75.6 us -> none  [the longest x1 38.6 us: on_device(): lax.psum(grad_normed_ffn.astype(jnp.bfloat16), 'wt').astype(jnp.float32)]
    dot_general x21 -> x0, matrix products: 44.7 us -> none  [the longest x7 24.6 us: transpose_by(): lax.dot_general(left, right, (((0,), (0,)), ((), ())), preferred_element_...]
    psum x1 -> x0, blocking collectives: 39.7 us -> none  [on_device(): lax.psum((attn_gain_part, q_gain_part, k_gain_part, ffn_gain_part), ('ctx...]
    unnamed x99 -> x62, local copies, waits for them, and re-layouts: 47 us -> 9.62 us
    all_gather x1 -> x0, blocking collectives: 32.7 us -> none  [on_device(): lax.all_gather(segments, 'ctx', axis=1, tiled=True)]
  transfers between devices with their start and end apart: 12 -> 1, of which waited for: 12 -> 1; matrix products, arithmetic and copies ran while one was open for 7% -> 2% of each run, Pallas kernels for 0% -> 0%
where the time goes in v3:
time: 319 us; the launch traced here: 318 us
  Pallas kernels  173 us (54%)
  waiting for transfers between devices  79.9 us (25%)
  local copies, waits for them, and re-layouts  19.5 us (6%)
  matrix products  15.9 us (5%)
  other arithmetic  15.8 us (5%)
  between operations  14.3 us (4%)
    pallas_call x1, Pallas kernels, backward(): pl.pallas_call(partial(backward_kernel, count), out_shape=[jax.ShapeDtype...  140 us
    psum x1, waiting for transfers between devices, on_device(): lax.psum(mlp_term.astype(jnp.bfloat16), 'wt').astype(jnp.float32)  79.9 us
    pallas_call x1, Pallas kernels, forward(): pl.pallas_call(partial(forward_kernel, count), out_shape=[jax.ShapeDtypeS...  33.2 us
    unnamed x62, local copies, waits for them, and re-layouts  9.62 us
    dot_general x3, matrix products, by_transpose(): lax.dot_general(left, right, (((1,), (1,)), ((), ())), preferred_element_...  9.24 us
    dot_general x3, matrix products, product(): return jnp.dot(left, right, preferred_element_type=jnp.float32)  6.66 us
  transfers between devices with their start and end apart: 1, of which 1 were waited for; matrix products, arithmetic and copies ran while one was open for 2% of the time, Pallas kernels for 0%

profile of v3, /device:TPU:0, one launch (start us, length us, event | category | flops | bytes accessed | tf_op | source)
XLA Modules:
  0.0 318.4 jit_solution(11276086372464170839)
XLA Ops:
  7.2 0.0 all-reduce.3.cloned.1.call-start
  7.2 1.3 broadcast_in_dim.16.attn_gain.refs_3_
  8.5 1.6 constant_dynamic-slice_fusion.table.refs_2_
  10.1 33.2 %shard_map.246 = (f32[640,1024]{1,0:T(8,128)}, bf16[640,256]{1,0:T(8,128)(2,1)}, f32[5,2,128,128]{3,2,1,0:T(8,128)}, bf16[5,128,512]{2,1,0:T(8,128)(2,1)}, f32[5...) custom-call(bf16[640,1024]{1,0:T(8,128)(2,1)} %bitcast.30, ...), custom_call_target="tpu_custom_call" | custom-call | tf_op jit(solution)/shard_map/pallas_call | solution.py:709
  43.3 2.2 copy.33
  45.4 0.0 copy-start.19
  45.4 0.0 copy-start.22
  45.4 2.1 multiply_reduce_fusion.2
  47.6 0.3 copy-done.22
  47.9 2.0 fusion.3
  49.9 0.0 copy-start.8
  49.9 0.0 copy-start.21
  49.9 2.0 fusion.2
  51.9 0.0 copy-done.21
  52.0 2.7 multiply_convert_fusion
  54.7 2.2 fusion.4
  56.9 0.0 copy-done.4
  56.9 0.0 copy-done.6
  56.9 2.9 convolution_convert_fusion
  59.8 4.1 %fusion.1 = (bf16[640,1024]{0,1:T(8,128)(2,1)}, f32[640,1024]{0,1:T(8,128)}) fusion(f32[640,1024]{0,1:T(8,128)S(1)} %fusion.4, bf16[640,1152]{1,0:T(8,128)(2,1)S(1)} %get-tuple-element.63, bf16[1024,1152]{1,0:T(8,128)(2,1)S(1)} %copy-done.22), kind=kOutput, calls=%fused_computation.18 | convolution fusion | flops 1511260160 | bytes 10387456 | tf_op jit(solution)/shard_map/dot_general | solution.py:22
  64.0 0.0 all-reduce.3.cloned.1.call-update
  64.0 2.4 copy.34
  66.4 1.4 fusion.17.refs_21_
  67.8 0.3 copy-done.3
  68.1 0.6 copy-done.5
  68.7 3.5 %pad_maximum_fusion.refs_22_ = bf16[3,640,1152]{2,1,0:T(8,128)(2,1)} fusion(bf16[1,640,1152]{2,1,0:T(8,128)(2,1)S(1)} %bitcast.32, bf16[1,640,1152]{2,1,0:T(8,128)(2,1)S(1)} %bitcast.33, bf16[1,640,1152]{2,1,0:T(8,128)(2,1)} %bitcast.34), kind=kLoop, calls=%fused_computation | loop fusion | flops 4423680 | bytes 8847360 | tf_op jit(solution)/shard_map/stack | solution.py:1623
  72.2 79.9 %all-reduce.3.cloned.1.call-done = (bf16[640,1024]{1,0:T(8,128)(2,1)}, bf16[640,1024]{0,1:T(8,128)(2,1)}) async-done(((bf16[640,1024]{1,0:T(8,128)(2,1)}, bf16[640,1024]{0,1:T(8,128)(2,1)}), (bf16[640,1024]{1,0:T(8,128)(2,1)}, bf16[640,1024]{0,1:T(8,128)(2,1)})) %all-reduce.3.cloned.1.call-update) | async-done | bytes 2621456 | tf_op jit(solution)/shard_map/psum | solution.py:1574
  152.1 3.6 %multiply_reduce_fusion = (f32[1024]{0:T(1024)}, f32[640]{0:T(1024)S(1)}) fusion(f32[640,1024]{0,1:T(8,128)} %get-tuple-element.67, f32[640,1024]{0,1:T(8,128)S(1)} %copy.33, f32[640]{0:T(1024)S(1)} %add_rsqrt_fusion, f32[1024]{0:T(1024)S(1)} %convert_element_type.37, bf16[640,1024]{0,1:T(8,128)(2,1)} %get-tuple-element.62), kind=kLoop, calls=%fused_computation.6 | loop fusion | flops 4585856 | bytes 6566912 | tf_op jit(solution)/shard_map/reduce_sum | solution.py:1583
  155.7 0.0 copy-done.1
  155.7 1.8 add_convert_fusion
  157.5 2.4 copy.38.refs_0_
  160.0 139.8 %shard_map.247 = (bf16[640,1024]{1,0:T(8,128)(2,1)}, f32[128,1152]{1,0:T(8,128)}, f32[128,1152]{1,0:T(8,128)}, f32[128,1152]{1,0:T(8,128)}, f32[128,256]{1,0:T(8...) custom-call(bf16[640,1024]{1,0:T(8,128)(2,1)} %copy.38.refs_0_, ...), custom_call_target="tpu_custom_call" | custom-call | tf_op jit(solution)/shard_map/pallas_call | solution.py:1252
  299.7 3.4 %add_convert_fusion.1 = bf16[640,1024]{1,0:T(8,128)(2,1)} fusion(f32[640,1024]{1,0:T(8,128)} %get-tuple-element.36, bf16[640,1024]{1,0:T(8,128)(2,1)S(1)} %copy-done.7), kind=kLoop, calls=%fused_computation.10 | loop fusion | flops 1966080 | bytes 5242880 | tf_op jit(solution)/shard_map/convert_element_type | solution.py:1575
  303.1 0.0 copy-start.24
  303.1 0.0 copy-start.23
  303.1 0.0 copy-start.13
  303.2 1.1 copy.55
  304.3 0.6 copy.56
  304.9 0.7 copy.57
  305.5 0.6 copy.58
  306.1 0.6 copy.59
  306.8 0.5 copy.60
  307.3 0.5 copy.61
  307.8 0.7 copy.62
  308.5 0.6 copy.63
  309.1 0.8 copy.64
  309.9 0.8 copy.65
  310.7 0.8 copy.66
  (39 shorter events, 0.1 us)
Async XLA Ops:
  7.2 144.9 %all-reduce.3.cloned.1.call-start = ((), (), s32[]{:S(2)}) async-start(), calls=%async_computation | async-start | bytes 5242880 | tf_op jit(solution)/shard_map/psum | solution.py:1574
  45.4 2.2 copy-start.19
  45.4 2.5 copy-start.22
  47.9 2.0 copy-start.20
  49.9 2.0 copy-start.8
  49.9 2.1 copy-start.21
  54.7 2.2 copy-start.4
  54.7 2.2 copy-start.6
  54.7 5.2 %copy-start.2 = (bf16[640,1152]{1,0:T(8,128)(2,1)}, bf16[640,1152]{1,0:T(8,128)(2,1)S(1)}, u32[]{:S(2)}) copy-start(bf16[640,1152]{1,0:T(8,128)(2,1)S(1)} %get-tuple-element.63) | copy-start | bytes 4423684
  66.4 1.7 copy-start.3
  66.4 2.3 copy-start.5
  152.1 3.6 %copy-start = (bf16[640,1024]{0,1:T(8,128)(2,1)S(1)}, bf16[640,1024]{0,1:T(8,128)(2,1)}, u32[]{:S(2)}) copy-start(bf16[640,1024]{0,1:T(8,128)(2,1)} %copy.34) | copy-start | bytes 3932164
  152.1 3.6 %copy-start.1 = (bf16[640,1024]{0,1:T(8,128)(2,1)S(1)}, bf16[640,1024]{0,1:T(8,128)(2,1)}, u32[]{:S(2)}) copy-start(bf16[640,1024]{0,1:T(8,128)(2,1)} %get-tuple-element.62) | copy-start | bytes 3932164
  160.0 139.8 %copy-start.7 = (bf16[640,1024]{1,0:T(8,128)(2,1)S(1)}, bf16[640,1024]{1,0:T(8,128)(2,1)}, u32[]{:S(2)}) copy-start(bf16[640,1024]{1,0:T(8,128)(2,1)} %get-tuple-element.61) | copy-start | bytes 3932164
  299.7 3.4 %copy-start.9 = (bf16[640,1024]{1,0:T(8,128)(2,1)S(1)}, bf16[640,1024]{1,0:T(8,128)(2,1)}, u32[]{:S(2)}) copy-start(bf16[640,1024]{1,0:T(8,128)(2,1)} %get-tuple-element.47) | copy-start | bytes 3932164
  303.1 1.2 copy-start.18
  303.1 1.7 copy-start.14
  303.1 2.4 copy-start.16
  303.1 3.0 copy-start.15
  303.1 3.7 %copy-start.24 = (f32[1,64]{1,0:T(1,128)S(1)}, f32[1,64]{1,0:T(1,128)}, u32[]{:S(2)}) copy-start(f32[1,64]{1,0:T(1,128)} %get-tuple-element.52) | copy-start | bytes 772
  303.1 4.2 %copy-start.23 = (f32[1,64]{1,0:T(1,128)S(1)}, f32[1,64]{1,0:T(1,128)}, u32[]{:S(2)}) copy-start(f32[1,64]{1,0:T(1,128)} %get-tuple-element.53) | copy-start | bytes 772
  303.1 4.7 %copy-start.13 = (f32[128,256]{1,0:T(8,128)S(1)}, f32[128,256]{1,0:T(8,128)}, u32[]{:S(2)}) copy-start(f32[128,256]{1,0:T(8,128)} %get-tuple-element.89) | copy-start | bytes 393220
  303.1 5.3 %copy-start.17 = (f32[1,1024]{1,0:T(1,128)S(1)}, f32[1,1024]{1,0:T(1,128)}, u32[]{:S(2)}) copy-start(f32[1,1024]{1,0:T(1,128)} %get-tuple-element.55) | copy-start | bytes 12292
  303.2 5.9 %copy-start.12 = (f32[128,1152]{1,0:T(8,128)S(1)}, f32[128,1152]{1,0:T(8,128)}, u32[]{:S(2)}) copy-start(f32[128,1152]{1,0:T(8,128)} %get-tuple-element.91) | copy-start | bytes 1769476
  303.2 6.7 %copy-start.11 = (f32[128,1152]{1,0:T(8,128)S(1)}, f32[128,1152]{1,0:T(8,128)}, u32[]{:S(2)}) copy-start(f32[128,1152]{1,0:T(8,128)} %get-tuple-element.92) | copy-start | bytes 1769476
  303.2 7.5 %copy-start.10 = (f32[128,1152]{1,0:T(8,128)S(1)}, f32[128,1152]{1,0:T(8,128)}, u32[]{:S(2)}) copy-start(f32[128,1152]{1,0:T(8,128)} %get-tuple-element.93) | copy-start | bytes 1769476
Sparse Core Ops, SparseCore 0:
  64.1 87.9 all-reduce.2

commit v4 on v3

--- a/solution.py
+++ b/solution.py
@@ -189,8 +189,8 @@
 
 
 class Ring:
-    def __init__(self, count, slots, send_sems, recv_sems):
-        self.count, self.slots = count, slots
+    def __init__(self, count, slots, send_sems, recv_sems, base=0):
+        self.count, self.slots, self.base = count, slots, base
         self.send_sems, self.recv_sems = send_sems, recv_sems
         self.other = lax.axis_index("wt")
         self.place = ring_place(lax.axis_index("ctx"), count)
@@ -200,17 +200,21 @@
 
     def copy(self, which, step, way):
         rows = pl.ds(way * self.half, self.half)
-        later = step + 1 if isinstance(step, int) else lax.add(step, 1)
+        slot = step - self.base
         return pltpu.make_async_remote_copy(
-            src_ref=self.slots.at[which, step, rows],
-            dst_ref=self.slots.at[which, later, rows],
-            send_sem=self.send_sems.at[which, step, way],
-            recv_sem=self.recv_sems.at[which, step, way],
+            src_ref=self.slots.at[which, slot, rows],
+            dst_ref=self.slots.at[which, slot + 1, rows],
+            send_sem=self.send_sems.at[which, slot, way],
+            recv_sem=self.recv_sems.at[which, slot, way],
             device_id=((self.right, self.left)[way], self.other),
             device_id_type=MESH,
         )
 
-    def tick(self, which, step, left_ref, right_ref, first=False, result=None):
+    def arrived(self, which, step):
+        for way in range(2):
+            self.copy(which, step - 1, way).wait_recv()
+
+    def tick(self, which, step, left_ref, right_ref, first=False, given=None, result=None):
         half = self.half
         rows = [
             ring_index(target, self.count) * (2 * half) + way * half
@@ -222,25 +226,26 @@
             [left_ref[pl.ds(pl.multiple_of(row, half), half), :] for row in rows], axis=0
         )
         total = jnp.dot(left, right_ref[...], preferred_element_type=jnp.float32)
-        if not first:
-            for way in range(2):
-                self.copy(which, step - 1, way).wait_recv()
-            total = total + self.slots[which, step].astype(jnp.float32)
+        if given is not None:
+            total = total + given[...].astype(jnp.float32)
+        elif not first:
+            self.arrived(which, step)
+            total = total + self.slots[which, step - self.base].astype(jnp.float32)
         if result is None:
-            self.slots[which, step] = total.astype(jnp.bfloat16)
+            self.slots[which, step - self.base] = total.astype(jnp.bfloat16)
             for way in range(2):
                 self.copy(which, step, way).start()
         else:
             result[...] = total
 
-    def finish(self, which):
+    def finish(self, which, end):
         for way in range(2):
 
             def wait(step, carry):
                 self.copy(which, step, way).wait_send()
                 return carry
 
-            lax.fori_loop(0, self.count - 1, wait, 0)
+            lax.fori_loop(self.base, end, wait, 0)
 
 
 def pair_lanes(shape):
@@ -349,6 +354,136 @@
     )
 
 
+class WtSum:
+    def __init__(self, here, tile, part, got, far, full, send_sems, recv_sems):
+        self.here, self.tile = here, tile
+        self.part, self.got, self.far, self.full = part, got, far, full
+        self.send_sems, self.recv_sems = send_sems, recv_sems
+        self.mine, self.theirs = here.core_bit, 1 - here.core_bit
+
+    def rows(self, seq):
+        return pl.ds(pl.multiple_of(seq * self.tile, self.tile), self.tile)
+
+    def copy(self, hop, seq, arriving=False):
+        rows = self.rows(seq)
+        half = self.theirs if arriving else self.mine
+        source = (
+            self.part.at[self.theirs, rows],
+            self.got.at[rows],
+            self.full.at[half, rows],
+        )[hop]
+        target = (self.got.at[rows], self.far.at[rows], self.full.at[half, rows])[hop]
+        device = self.here.chip if hop == 1 else self.here.core
+        return send_to(
+            source, target, self.send_sems.at[hop, seq], self.recv_sems.at[hop, seq], device
+        )
+
+    def offer(self, seq, value):
+        rows = self.rows(seq)
+        half = value.shape[1] // 2
+        self.part[0, rows] = value[:, :half].astype(jnp.bfloat16)
+        self.part[1, rows] = value[:, half:].astype(jnp.bfloat16)
+        self.copy(0, seq).start()
+
+    def cross(self, seq):
+        rows = self.rows(seq)
+        self.copy(0, seq).wait_recv()
+        total = self.part[self.mine, rows].astype(jnp.float32) + self.got[rows].astype(
+            jnp.float32
+        )
+        self.got[rows] = total.astype(jnp.bfloat16)
+        self.copy(1, seq).start()
+
+    def close(self, seq):
+        rows = self.rows(seq)
+        self.copy(1, seq).wait_recv()
+        total = self.got[rows].astype(jnp.float32) + self.far[rows].astype(jnp.float32)
+        self.full[self.mine, rows] = total.astype(jnp.bfloat16)
+        self.copy(2, seq).start()
+
+    def result(self, seq):
+        rows = self.rows(seq)
+        self.copy(2, seq, True).wait_recv()
+        return jnp.concatenate([self.full[0, rows], self.full[1, rows]], axis=1).astype(
+            jnp.float32
+        )
+
+    def finish(self, sequences):
+        def sent(seq, carry):
+            for hop in range(3):
+                self.copy(hop, seq).wait_send()
+            return carry
+
+        lax.fori_loop(0, sequences, sent, 0)
+
+
+def wt_sum_scratch(sequences, rows, width):
+    half = width // 2
+    return [
+        pltpu.VMEM((2, rows, half), jnp.bfloat16),
+        pltpu.VMEM((rows, half), jnp.bfloat16),
+        pltpu.VMEM((rows, half), jnp.bfloat16),
+        pltpu.VMEM((2, rows, half), jnp.bfloat16),
+        pltpu.SemaphoreType.DMA((3, sequences)),
+        pltpu.SemaphoreType.DMA((3, sequences)),
+    ]
+
+
+def ring_scratch(count, arrays, rows, width):
+    return [
+        pltpu.VMEM((arrays, count, rows, width), jnp.bfloat16),
+        pltpu.SemaphoreType.DMA((arrays, count - 1, 2)),
+        pltpu.SemaphoreType.DMA((arrays, count - 1, 2)),
+    ]
+
+
+class GainSum:
+    def __init__(self, here, slots, beside, sends, recvs, pair_sends, pair_recvs):
+        self.here, self.slots, self.beside = here, slots, beside
+        self.sends, self.recvs = sends, recvs
+        self.pair_sends, self.pair_recvs = pair_sends, pair_recvs
+
+    def copy(self, shift, arriving=False):
+        here = self.here
+        target = lax.rem(here.ctx + shift, here.count)
+        origin = lax.rem(here.ctx + here.count - shift, here.count)
+        ref = self.slots.at[origin if arriving else here.ctx]
+        return send_to(
+            ref, ref, self.sends.at[shift - 1], self.recvs.at[shift - 1], (target, here.wt)
+        )
+
+    def pair_copy(self, hop):
+        device = (self.here.core, self.here.chip)[hop]
+        return send_to(
+            self.beside.at[hop, 0],
+            self.beside.at[hop, 1],
+            self.pair_sends.at[hop],
+            self.pair_recvs.at[hop],
+            device,
+        )
+
+    def start(self):
+        for shift in range(1, self.here.count):
+            self.copy(shift).start()
+
+    def total(self):
+        for shift in range(1, self.here.count):
+            self.copy(shift, True).wait_recv()
+        total = self.slots[0]
+        for index in range(1, self.here.count):
+            total = total + self.slots[index]
+        for hop in range(2):
+            self.beside[hop, 0] = total
+            self.pair_copy(hop).start()
+            self.pair_copy(hop).wait_recv()
+            total = total + self.beside[hop, 1]
+        for shift in range(1, self.here.count):
+            self.copy(shift).wait_send()
+        for hop in range(2):
+            self.pair_copy(hop).wait_send()
+        return total
+
+
 def forward_kernel(
     count,
     tokens,
@@ -361,6 +496,11 @@
     w_key,
     w_value,
     w_out,
+    cotangent,
+    ffn_gain,
+    w_gate_in,
+    w_up_in,
+    w_down_in,
     residual,
     heads_out,
     mixed_t,
@@ -372,6 +512,13 @@
     query_raw,
     key_raw,
     normed_t,
+    grad_res,
+    cot_t,
+    normed_ffn_t,
+    ffn_grads,
+    ffn_gain_part,
+    mlp_part,
+    ring_state,
     all_segs,
     all_out,
     all_heads,
@@ -387,12 +534,28 @@
     out_recv,
     head_send,
     head_recv,
+    w_gate,
+    w_up,
+    w_down,
+    grad_hidden,
+    load_sems,
+    *rest,
 ):
     sequences, tile = segments.shape
     head_dim = q_gain.shape[1]
     levels = count // 2
     here = Place(count)
     me = here.ctx
+    loads = [
+        pltpu.make_async_copy(source, target, load_sems.at[i])
+        for i, (source, target) in enumerate(
+            ((w_down_in, w_down), (w_gate_in, w_gate), (w_up_in, w_up))
+        )
+    ]
+    for load in loads:
+        load.start()
+    wt_sum = WtSum(here, tile, *rest[:6])
+    ffn = Ring(count, *rest[6:9])
     all_segs[me] = jnp.zeros_like(all_segs[me])
     all_segs[me, pl.ds(0, sequences)] = segments[...]
     all_out[here.wt] = w_out[...]
@@ -554,6 +717,16 @@
         return carry
 
     lax.fori_loop(0, sequences, own_block, 0)
+    loads[0].wait()
+
+    def back_down(seq, carry):
+        rows = rows_of(seq)
+        grads = cotangent[rows, :]
+        cot_t[:, rows] = grads.T
+        grad_hidden[rows, :] = dot_nn(grads, w_down[...]).astype(jnp.bfloat16)
+        return carry
+
+    lax.fori_loop(0, sequences, back_down, 0)
 
     @pl.when(goes_back_aside(here, 0))
     def _():
@@ -623,7 +796,40 @@
     out_copy(1, True).wait_recv()
     out_copy(2, True).wait_recv()
 
-    def finish(turn_, carry):
+    loads[1].wait()
+    loads[2].wait()
+    ffn_gain_row = ffn_gain[...].astype(jnp.float32)
+    ffn_gain_part[...] = jnp.zeros_like(ffn_gain_part)
+
+    def ffn_unit(rows):
+        values = residual[rows, :]
+        inverse = lax.rsqrt(jnp.mean(values * values, axis=-1, keepdims=True) + EPS)
+        return values * inverse, inverse
+
+    def feed(seq):
+        rows = rows_of(seq)
+        total = tokens[rows, :].astype(jnp.float32)
+        for slot in range(4):
+            total = total + dot_nt(all_heads[slot, rows], all_out[slot])
+        residual[rows, :] = total
+        unit, unused = ffn_unit(rows)
+        normed = (unit * ffn_gain_row).astype(jnp.bfloat16)
+        normed_ffn_t[:, rows] = normed.T
+        gate = dot_nn(normed, w_gate[...])
+        up = dot_nn(normed, w_up[...])
+        sigmoid = jax.nn.sigmoid(gate)
+        silu = gate * sigmoid
+        ffn_grads[0, rows] = (silu * up).astype(jnp.bfloat16)
+        grads = grad_hidden[rows, :].astype(jnp.float32)
+        grad_gate = (grads * up * sigmoid * (1.0 + gate * (1.0 - sigmoid))).astype(jnp.bfloat16)
+        grad_up = (grads * silu).astype(jnp.bfloat16)
+        ffn_grads[1, rows] = grad_gate
+        ffn_grads[2, rows] = grad_up
+        grad_normed = dot_nt(grad_gate, w_gate[...]) + dot_nt(grad_up, w_up[...])
+        ffn_gain_part[...] += jnp.sum(grad_normed * unit, axis=0, keepdims=True)
+        wt_sum.offer(seq, grad_normed)
+
+    def feed_turn(turn_, carry):
         @pl.when(turn_ < sequences)
         def _():
             head_copy(0, turn_, True).wait_recv()
@@ -632,17 +838,49 @@
         @pl.when(turn_ > 0)
         def _():
             seq = turn_ - 1
-            rows = rows_of(seq)
             head_copy(1, seq, True).wait_recv()
             head_copy(2, seq, True).wait_recv()
-            total = tokens[rows, :].astype(jnp.float32)
-            for slot in range(4):
-                total = total + dot_nt(all_heads[slot, rows], all_out[slot])
-            residual[rows, :] = total
+            feed(seq)
+
+        @pl.when(turn_ > 1)
+        def _():
+            wt_sum.cross(turn_ - 2)
 
         return carry
 
-    lax.fori_loop(0, sequences + 1, finish, 0)
+    lax.fori_loop(0, sequences + 1, feed_turn, 0)
+    wt_sum.cross(sequences - 1)
+    lefts = (cot_t, normed_ffn_t, normed_ffn_t)
+    for i in range(3):
+        ffn.tick(i, 0, lefts[i], ffn_grads.at[i], first=True)
+    half = tokens.shape[1] // 2
+
+    def down(seq, carry):
+        rows = rows_of(seq)
+        term = dot_nt(ffn_grads[0, rows], w_down[...])
+        mlp_part[0, rows] = term[:, :half].astype(jnp.bfloat16)
+        mlp_part[1, rows] = term[:, half:].astype(jnp.bfloat16)
+        wt_sum.close(seq)
+        return carry
+
+    lax.fori_loop(0, sequences, down, 0)
+    for i in range(3):
+        ffn.tick(i, 1, lefts[i], ffn_grads.at[i])
+
+    def back_norm(seq, carry):
+        rows = rows_of(seq)
+        unit, inverse = ffn_unit(rows)
+        scaled = wt_sum.result(seq) * ffn_gain_row
+        grads = inverse * (scaled - unit * jnp.mean(scaled * unit, axis=-1, keepdims=True))
+        grad_res[rows, :] = (cotangent[rows, :].astype(jnp.float32) + grads).astype(jnp.bfloat16)
+        return carry
+
+    lax.fori_loop(0, sequences, back_norm, 0)
+    for i in range(3):
+        ffn.arrived(i, 2)
+        ring_state[i] = ffn.slots[i, 2]
+        ffn.finish(i, 2)
+    wt_sum.finish(sequences)
     for hop in range(3):
         out_copy(hop).wait_send()
 
@@ -683,13 +921,15 @@
     return (block >= 0) & (block < here.ctx)
 
 
-def forward(tokens, segments, table, attn_gain, q_gain, k_gain, w_query, w_key, w_value, w_out):
+def forward(*arrays):
+    tokens, segments, q_gain, w_gate = arrays[0], arrays[1], arrays[4], arrays[12]
     count = lax.axis_size("ctx")
     sequences, tile = segments.shape
     rows, width = tokens.shape
     head_dim = q_gain.shape[1]
     pair = 2 * head_dim
     levels = count // 2
+    hidden = w_gate.shape[1]
     vmem = pl.BlockSpec(memory_space=pltpu.VMEM)
     f32, bf16 = jnp.float32, jnp.bfloat16
     outs = [
@@ -704,12 +944,19 @@
         ((rows, 2 * pair), f32),
         ((rows, pair), f32),
         ((width, rows), bf16),
+        ((rows, width), bf16),
+        ((width, rows), bf16),
+        ((width, rows), bf16),
+        ((3, rows, hidden), bf16),
+        ((1, width), f32),
+        ((2, rows, width // 2), bf16),
+        ((3, width // count, hidden), bf16),
     ]
     dma = pltpu.SemaphoreType.DMA
     return pl.pallas_call(
         partial(forward_kernel, count),
         out_shape=[jax.ShapeDtypeStruct(shape, kind) for shape, kind in outs],
-        in_specs=[vmem] * 10,
+        in_specs=[vmem] * 12 + [pl.BlockSpec(memory_space=pl.ANY)] * 3,
         out_specs=[vmem] * len(outs),
         scratch_shapes=[
             pltpu.VMEM((count, 8, tile), jnp.int32),
@@ -727,141 +974,18 @@
             dma((3,)),
             dma((3, sequences)),
             dma((3, sequences)),
+            pltpu.VMEM((width, hidden), bf16),
+            pltpu.VMEM((width, hidden), bf16),
+            pltpu.VMEM((width, hidden), bf16),
+            pltpu.VMEM((rows, hidden), bf16),
+            dma((3,)),
+            *wt_sum_scratch(sequences, rows, width),
+            *ring_scratch(3, 3, width // count, hidden),
         ],
         compiler_params=pltpu.CompilerParams(
             collective_id=2, has_side_effects=True, vmem_limit_bytes=60 * MIB
         ),
-    )(tokens, segments, table, attn_gain, q_gain, k_gain, w_query, w_key, w_value, w_out)
-
-
-class WtSum:
-    def __init__(self, here, tile, part, got, far, full, send_sems, recv_sems):
-        self.here, self.tile = here, tile
-        self.part, self.got, self.far, self.full = part, got, far, full
-        self.send_sems, self.recv_sems = send_sems, recv_sems
-        self.mine, self.theirs = here.core_bit, 1 - here.core_bit
-
-    def rows(self, seq):
-        return pl.ds(pl.multiple_of(seq * self.tile, self.tile), self.tile)
-
-    def copy(self, hop, seq, arriving=False):
-        rows = self.rows(seq)
-        half = self.theirs if arriving else self.mine
-        source = (
-            self.part.at[self.theirs, rows],
-            self.got.at[rows],
-            self.full.at[half, rows],
-        )[hop]
-        target = (self.got.at[rows], self.far.at[rows], self.full.at[half, rows])[hop]
-        device = self.here.chip if hop == 1 else self.here.core
-        return send_to(
-            source, target, self.send_sems.at[hop, seq], self.recv_sems.at[hop, seq], device
-        )
-
-    def offer(self, seq, value):
-        rows = self.rows(seq)
-        half = value.shape[1] // 2
-        self.part[0, rows] = value[:, :half].astype(jnp.bfloat16)
-        self.part[1, rows] = value[:, half:].astype(jnp.bfloat16)
-        self.copy(0, seq).start()
-
-    def cross(self, seq):
-        rows = self.rows(seq)
-        self.copy(0, seq).wait_recv()
-        total = self.part[self.mine, rows].astype(jnp.float32) + self.got[rows].astype(
-            jnp.float32
-        )
-        self.got[rows] = total.astype(jnp.bfloat16)
-        self.copy(1, seq).start()
-
-    def close(self, seq):
-        rows = self.rows(seq)
-        self.copy(1, seq).wait_recv()
-        total = self.got[rows].astype(jnp.float32) + self.far[rows].astype(jnp.float32)
-        self.full[self.mine, rows] = total.astype(jnp.bfloat16)
-        self.copy(2, seq).start()
-
-    def result(self, seq):
-        rows = self.rows(seq)
-        self.copy(2, seq, True).wait_recv()
-        return jnp.concatenate([self.full[0, rows], self.full[1, rows]], axis=1).astype(
-            jnp.float32
-        )
-
-    def finish(self, sequences):
-        def sent(seq, carry):
-            for hop in range(3):
-                self.copy(hop, seq).wait_send()
-            return carry
-
-        lax.fori_loop(0, sequences, sent, 0)
-
-
-def wt_sum_scratch(sequences, rows, width):
-    half = width // 2
-    return [
-        pltpu.VMEM((2, rows, half), jnp.bfloat16),
-        pltpu.VMEM((rows, half), jnp.bfloat16),
-        pltpu.VMEM((rows, half), jnp.bfloat16),
-        pltpu.VMEM((2, rows, half), jnp.bfloat16),
-        pltpu.SemaphoreType.DMA((3, sequences)),
-        pltpu.SemaphoreType.DMA((3, sequences)),
-    ]
-
-
-def ring_scratch(count, arrays, rows, width):
-    return [
-        pltpu.VMEM((arrays, count, rows, width), jnp.bfloat16),
-        pltpu.SemaphoreType.DMA((arrays, count - 1, 2)),
-        pltpu.SemaphoreType.DMA((arrays, count - 1, 2)),
-    ]
-
-
-class GainSum:
-    def __init__(self, here, slots, beside, sends, recvs, pair_sends, pair_recvs):
-        self.here, self.slots, self.beside = here, slots, beside
-        self.sends, self.recvs = sends, recvs
-        self.pair_sends, self.pair_recvs = pair_sends, pair_recvs
-
-    def copy(self, shift, arriving=False):
-        here = self.here
-        target = lax.rem(here.ctx + shift, here.count)
-        origin = lax.rem(here.ctx + here.count - shift, here.count)
-        ref = self.slots.at[origin if arriving else here.ctx]
-        return send_to(
-            ref, ref, self.sends.at[shift - 1], self.recvs.at[shift - 1], (target, here.wt)
-        )
-
-    def pair_copy(self, hop):
-        device = (self.here.core, self.here.chip)[hop]
-        return send_to(
-            self.beside.at[hop, 0],
-            self.beside.at[hop, 1],
-            self.pair_sends.at[hop],
-            self.pair_recvs.at[hop],
-            device,
-        )
-
-    def start(self):
-        for shift in range(1, self.here.count):
-            self.copy(shift).start()
-
-    def total(self):
-        for shift in range(1, self.here.count):
-            self.copy(shift, True).wait_recv()
-        total = self.slots[0]
-        for index in range(1, self.here.count):
-            total = total + self.slots[index]
-        for hop in range(2):
-            self.beside[hop, 0] = total
-            self.pair_copy(hop).start()
-            self.pair_copy(hop).wait_recv()
-            total = total + self.beside[hop, 1]
-        for shift in range(1, self.here.count):
-            self.copy(shift).wait_send()
-        for hop in range(2):
-            self.pair_copy(hop).wait_send()
-        return total
+    )(*arrays)
 
 
 def backward_kernel(count, *refs):
@@ -890,8 +1014,12 @@
         normed_ffn_t,
         ffn_grads,
         ffn_gain_part,
-    ) = refs[:24]
+        residual,
+        mlp_part,
+        ring_state,
+    ) = refs[:27]
     (
+        output,
         tokens_grad,
         down_sum,
         gate_sum,
@@ -904,7 +1032,7 @@
         ffn_gain_sum,
         q_gain_sum,
         k_gain_sum,
-    ) = refs[24:36]
+    ) = refs[27:40]
     (
         grad_res_t,
         grad_heads_t,
@@ -921,8 +1049,8 @@
         side_recv,
         line_send,
         line_recv,
-    ) = refs[36:51]
-    rest = refs[51:]
+    ) = refs[40:55]
+    rest = refs[55:]
     sequences, tile = mixed_t.shape[0], mixed_t.shape[3]
     head_dim = q_gain.shape[1]
     pair = 2 * head_dim
@@ -932,29 +1060,39 @@
     wt_sum = WtSum(here, tile, *rest[:6])
     gains = GainSum(here, *rest[6:12])
     gain_slots = rest[6]
-    ffn = Ring(count, *rest[12:15])
+    ffn = Ring(count, *rest[12:15], base=2)
     out = Ring(count, *rest[15:18])
     qkv = Ring(count, *rest[18:21])
+    mlp_sum = WtSum(here, tile, mlp_part, *rest[21:26])
     last = count - 1
     here.greet_all()
     lefts = (cot_t, normed_ffn_t, normed_ffn_t)
     ffn_sums = (down_sum, gate_sum, up_sum)
 
-    def ffn_ticks(step, first=False, final=False):
+    def ffn_ticks(step, given=False, final=False):
         for i in range(3):
             ffn.tick(
                 i,
                 step,
                 lefts[i],
                 ffn_grads.at[i],
-                first=first,
+                given=ring_state.at[i] if given else None,
                 result=ffn_sums[i] if final else None,
             )
 
     def rows_of(seq):
         return pl.ds(pl.multiple_of(seq * tile, tile), tile)
 
-    ffn_ticks(0, first=True)
+    ffn_ticks(2, given=True)
+
+    def each(step):
+        def one(seq, carry):
+            step(seq)
+            return carry
+
+        lax.fori_loop(0, sequences, one, 0)
+
+    each(lambda seq: mlp_sum.copy(0, seq).start())
 
     def prepare(seq, carry):
         rows = rows_of(seq)
@@ -975,6 +1113,7 @@
 
     lax.fori_loop(0, sequences, prepare, 0)
     out.tick(0, 0, grad_res_t, heads, first=True)
+    each(mlp_sum.cross)
     key_rows = lax.broadcasted_iota(jnp.int32, (tile, 4 * tile), 0)
     query_cols = lax.rem(lax.broadcasted_iota(jnp.int32, (tile, 4 * tile), 1), tile)
 
@@ -1069,19 +1208,27 @@
 
             lax.fori_loop(0, sequences, one, 0)
 
-        ffn_ticks(1 + turn_)
+        ffn_ticks(3 + turn_)
+        out.tick(0, 1 + turn_, grad_res_t, heads)
         return carry
 
     lax.fori_loop(0, levels - 1, level, 0)
     send_aside(0)
+    each(mlp_sum.close)
 
     def own_block(seq, carry):
         own_grads[rows_of(seq), :] = grads_of(me, seq, True)
         return carry
 
     lax.fori_loop(0, sequences, own_block, 0)
-    ffn_ticks(levels)
-    out.tick(0, 1, grad_res_t, heads)
+    ffn_ticks(levels + 2)
+    out.tick(0, levels, grad_res_t, heads)
+
+    def output_rows(seq):
+        rows = rows_of(seq)
+        output[rows, :] = (residual[rows, :] + mlp_sum.result(seq)).astype(jnp.bfloat16)
+
+    each(output_rows)
     cosine = table[:, pl.ds(0, pair)]
     sine = table[:, pl.ds(pair, pair)]
     q_gain_pair = double(q_gain[...].astype(jnp.float32))
@@ -1152,16 +1299,15 @@
 
     def tail(step, carry):
         qkv.tick(0, step, normed_t, grad_qkv)
-        out.tick(0, step + 1, grad_res_t, heads)
 
         @pl.when(step + levels < last)
         def _():
-            ffn_ticks(step + levels)
+            out.tick(0, step + levels, grad_res_t, heads)
 
         return carry
 
+    ffn_ticks(last, final=True)
     lax.fori_loop(1, last - 1, tail, 0)
-    ffn_ticks(last, final=True)
     out.tick(0, last, grad_res_t, heads, result=out_sum)
 
     def closing(seq, carry):
@@ -1195,9 +1341,10 @@
     value_sum[...] = qkv_total[:, pl.ds(3 * pair, pair)]
     wt_sum.finish(sequences)
     for i in range(3):
-        ffn.finish(i)
-    out.finish(0)
-    qkv.finish(0)
+        ffn.finish(i, last)
+    out.finish(0, last)
+    qkv.finish(0, last)
+    mlp_sum.finish(sequences)
 
     def drain(step, carry):
         @pl.when(block_there(step))
@@ -1235,6 +1382,7 @@
     vmem = pl.BlockSpec(memory_space=pltpu.VMEM)
     f32, bf16 = jnp.float32, jnp.bfloat16
     outs = [
+        ((rows, width), bf16),
         ((rows, width), bf16),
         ((block, hidden), f32),
         ((block, hidden), f32),
@@ -1277,9 +1425,10 @@
             dma((count - 1,)),
             dma((2,)),
             dma((2,)),
-            *ring_scratch(count, 3, block, hidden),
+            *ring_scratch(count - 2, 3, block, hidden),
             *ring_scratch(count, 1, block, 2 * pair),
             *ring_scratch(count, 1, block, 4 * pair),
+            *wt_sum_scratch(sequences, rows, width)[1:],
         ],
         compiler_params=pltpu.CompilerParams(
             collective_id=3, has_side_effects=True, vmem_limit_bytes=62 * MIB
@@ -1559,34 +1708,30 @@
         query_raw,
         key_raw,
         normed_t,
+        grad_residual,
+        cot_t,
+        normed_ffn_t,
+        ffn_grads,
+        ffn_gain_part,
+        mlp_part,
+        ring_state,
     ) = forward(
-        token_rows, segments, table, *gains, w_query, key_matrix, value_matrix, w_out
-    )
-    normed_ffn, ffn_unit, ffn_inverse = norm_rows(residual, ffn_gain)
-    normed_ffn_low = normed_ffn.astype(jnp.bfloat16)
-    gate_proj = product(normed_ffn_low, w_gate)
-    up_proj = product(normed_ffn_low, w_up)
-    gate_sigmoid = jax.nn.sigmoid(gate_proj)
-    gate_silu = gate_proj * gate_sigmoid
-    hidden_low = (gate_silu * up_proj).astype(jnp.bfloat16)
-    mlp_term = by_transpose(hidden_low, w_down)
-    output_rows = (
-        residual + lax.psum(mlp_term.astype(jnp.bfloat16), "wt").astype(jnp.float32)
-    ).astype(jnp.bfloat16)
-    grad_rows = cotangent.reshape(token_rows.shape)
-    grad_hidden = product(grad_rows, w_down)
-    grad_gate = (
-        grad_hidden * up_proj * gate_sigmoid * (1.0 + gate_proj * (1.0 - gate_sigmoid))
-    ).astype(jnp.bfloat16)
-    grad_up = (grad_hidden * gate_silu).astype(jnp.bfloat16)
-    grad_normed_ffn = by_transpose(grad_gate, w_gate) + by_transpose(grad_up, w_up)
-    ffn_gain_part = jnp.sum(grad_normed_ffn * ffn_unit, axis=0, keepdims=True)
-    grad_normed_ffn = lax.psum(grad_normed_ffn.astype(jnp.bfloat16), "wt").astype(jnp.float32)
-    grad_residual = (
-        grad_rows.astype(jnp.float32)
-        + norm_back(grad_normed_ffn, ffn_unit, ffn_inverse, ffn_gain)
-    ).astype(jnp.bfloat16)
+        token_rows,
+        segments,
+        table,
+        *gains,
+        w_query,
+        key_matrix,
+        value_matrix,
+        w_out,
+        cotangent.reshape(token_rows.shape),
+        ffn_gain[None],
+        w_gate,
+        w_up,
+        w_down,
+    )
     (
+        output_rows,
         tokens_grad,
         w_down_grad,
         w_gate_grad,
@@ -1618,10 +1763,13 @@
         query_raw,
         key_raw,
         normed_t,
-        grad_rows.T,
-        normed_ffn_low.T,
-        jnp.stack([hidden_low, grad_gate, grad_up]),
+        cot_t,
+        normed_ffn_t,
+        ffn_grads,
         ffn_gain_part,
+        residual,
+        mlp_part,
+        ring_state,
     )
     return (
         output_rows.reshape(tokens.shape),

time: 319 us -> 242 us (0.76)
  waiting for transfers between devices: 79.9 us -> 0 us
  Pallas kernels: 173 us -> 226 us
  matrix products: 15.9 us -> 0 us
  other arithmetic: 15.8 us -> 0 us
  between operations: 14.3 us -> 0.74 us
  local copies, waits for them, and re-layouts: 19.5 us -> 15.1 us
    psum x1 -> x0, waiting for transfers between devices: 79.9 us -> none  [on_device(): lax.psum(mlp_term.astype(jnp.bfloat16), 'wt').astype(jnp.float32)]
    pallas_call x1, Pallas kernels: 33.2 us -> 86.5 us  [forward(): pl.pallas_call(partial(forward_kernel, count), out_shape=[jax.ShapeDtypeS...]
    dot_general x6 -> x0, matrix products: 15.9 us -> none  [the longest x3 9.24 us: by_transpose(): lax.dot_general(left, right, (((1,), (1,)), ((), ())), preferred_element_...]
    reduce_sum x2 -> x0, other arithmetic: 5.76 us -> none  [the longest x1 3.63 us: on_device(): ffn_gain_part = jnp.sum(grad_normed_ffn * ffn_unit, axis=0, keepdims=True)]
    convert_element_type x3 -> x0, other arithmetic: 5.19 us -> none  [the longest x1 3.36 us: on_device(): output_rows = (residual + lax.psum(mlp_term.astype(jnp.bfloat16), 'wt').a...]
    another operation x1 -> x0, other arithmetic: 3.47 us -> none  [on_device(): jnp.stack([hidden_low, grad_gate, grad_up])]
    unnamed x62 -> x37, local copies, waits for them, and re-layouts: 9.62 us -> 11 us
  transfers between devices with their start and end apart: 1 -> 0, of which waited for: 1 -> 0; matrix products, arithmetic and copies ran while one was open for 2% -> 0% of each run, Pallas kernels for 0% -> 0%
where the time goes in v4:
time: 242 us
  Pallas kernels  226 us (93%)
  local copies, waits for them, and re-layouts  15.1 us (6%)
    pallas_call x1, Pallas kernels, backward(): pl.pallas_call(partial(backward_kernel, count), out_shape=[jax.ShapeDtype...  140 us
    pallas_call x1, Pallas kernels, forward(): pl.pallas_call(partial(forward_kernel, count), out_shape=[jax.ShapeDtypeS...  86.5 us
    unnamed x37, local copies, waits for them, and re-layouts  11 us

profile of v4, /device:TPU:0, one launch (start us, length us, event | category | flops | bytes accessed | tf_op | source)
XLA Modules:
  0.0 242.1 jit_solution(4326473941513215312)
XLA Ops:
  0.6 1.3 broadcast_in_dim.12.attn_gain.refs_3_
  1.9 1.3 broadcast_in_dim.15.ffn_gain
  3.2 1.6 constant_dynamic-slice_fusion.table.refs_2_
  4.8 86.5 %shard_map.246 = (f32[640,1024]{1,0:T(8,128)}, bf16[640,256]{1,0:T(8,128)(2,1)}, f32[5,2,128,128]{3,2,1,0:T(8,128)}, bf16[5,128,512]{2,1,0:T(8,128)(2,1)}, f32[5...) custom-call(bf16[640,1024]{1,0:T(8,128)(2,1)} %bitcast.10, ...), custom_call_target="tpu_custom_call" | custom-call | tf_op jit(solution)/shard_map/pallas_call | solution.py:956
  91.3 139.7 %shard_map.247 = (bf16[640,1024]{1,0:T(8,128)(2,1)}, bf16[640,1024]{1,0:T(8,128)(2,1)}, f32[128,1152]{1,0:T(8,128)}, f32[128,1152]{1,0:T(8,128)}, f32[128,1152]{...) custom-call(bf16[640,1024]{1,0:T(8,128)(2,1)} %get-tuple-element.44., ...), custom_call_target="tpu_custom_call" | custom-call | tf_op jit(solution)/shard_map/pallas_call | solution.py:1400
  231.0 0.0 copy-start
  231.0 2.6 %copy.41 = bf16[5,128,1024]{2,1,0:T(8,128)(2,1)} copy(bf16[5,128,1024]{2,1,0:T(8,128)(2,1)} %bitcast.14) | data formatting | bytes 2621440
  233.7 0.0 copy-done
  233.7 0.0 copy-start.9
  233.7 0.0 copy-start.5
  233.7 0.0 copy-start.7
  233.7 0.0 copy-start.6
  233.7 0.0 copy-start.11
  233.7 0.0 copy-start.10
  233.7 0.0 copy-start.4
  233.7 0.0 copy-start.8
  233.7 0.0 copy-start.3
  233.7 1.1 copy.42
  234.8 0.0 copy-done.9
  234.8 0.0 copy-start.2
  234.8 0.6 copy.43
  235.4 0.0 copy-done.5
  235.4 0.7 copy.44
  236.0 0.0 copy-done.7
  236.1 0.6 copy.45
  236.7 0.0 copy-done.6
  236.7 0.6 copy.46
  237.3 0.0 copy-done.11
  237.3 0.5 copy.47
  237.8 0.0 copy-done.10
  237.8 0.5 copy.48
  238.3 0.0 copy-done.4
  238.3 0.0 copy-start.1
  238.3 0.7 copy.49
  239.0 0.0 copy-done.8
  239.0 0.6 copy.50
  239.6 0.0 copy-done.3
  239.6 0.8 copy.51
  240.4 0.0 copy-done.2
  240.4 0.8 copy.52
  241.2 0.0 copy-done.1
  241.2 0.8 copy.53
Async XLA Ops:
  231.0 2.6 %copy-start = (bf16[640,1024]{1,0:T(8,128)(2,1)S(1)}, bf16[640,1024]{1,0:T(8,128)(2,1)}, u32[]{:S(2)}) copy-start(bf16[640,1024]{1,0:T(8,128)(2,1)} %get-tuple-element.63) | copy-start | bytes 3932164
  233.7 1.1 copy-start.9
  233.7 1.7 copy-start.5
  233.7 2.4 copy-start.7
  233.7 3.0 %copy-start.6 = (f32[128,128]{1,0:T(8,128)S(1)}, f32[128,128]{1,0:T(8,128)}, u32[]{:S(2)}) copy-start(f32[128,128]{1,0:T(8,128)} %get-tuple-element.93) | copy-start | bytes 196612
  233.7 3.6 %copy-start.11 = (f32[1,64]{1,0:T(1,128)S(1)}, f32[1,64]{1,0:T(1,128)}, u32[]{:S(2)}) copy-start(f32[1,64]{1,0:T(1,128)} %get-tuple-element.68) | copy-start | bytes 772
  233.7 4.1 %copy-start.10 = (f32[1,64]{1,0:T(1,128)S(1)}, f32[1,64]{1,0:T(1,128)}, u32[]{:S(2)}) copy-start(f32[1,64]{1,0:T(1,128)} %get-tuple-element.69) | copy-start | bytes 772
  233.7 4.6 %copy-start.4 = (f32[128,256]{1,0:T(8,128)S(1)}, f32[128,256]{1,0:T(8,128)}, u32[]{:S(2)}) copy-start(f32[128,256]{1,0:T(8,128)} %get-tuple-element.96) | copy-start | bytes 393220
  233.7 5.3 %copy-start.8 = (f32[1,1024]{1,0:T(1,128)S(1)}, f32[1,1024]{1,0:T(1,128)}, u32[]{:S(2)}) copy-start(f32[1,1024]{1,0:T(1,128)} %get-tuple-element.71) | copy-start | bytes 12292
  233.7 5.9 %copy-start.3 = (f32[128,1152]{1,0:T(8,128)S(1)}, f32[128,1152]{1,0:T(8,128)}, u32[]{:S(2)}) copy-start(f32[128,1152]{1,0:T(8,128)} %get-tuple-element.98) | copy-start | bytes 1769476
  234.8 5.6 %copy-start.2 = (f32[128,1152]{1,0:T(8,128)S(1)}, f32[128,1152]{1,0:T(8,128)}, u32[]{:S(2)}) copy-start(f32[128,1152]{1,0:T(8,128)} %get-tuple-element.99) | copy-start | bytes 1769476
  238.3 2.9 %copy-start.1 = (f32[128,1152]{1,0:T(8,128)S(1)}, f32[128,1152]{1,0:T(8,128)}, u32[]{:S(2)}) copy-start(f32[128,1152]{1,0:T(8,128)} %get-tuple-element.100) | copy-start | bytes 1769476

commit v5 on v4

--- a/solution.py
+++ b/solution.py
@@ -214,7 +214,17 @@
         for way in range(2):
             self.copy(which, step - 1, way).wait_recv()
 
-    def tick(self, which, step, left_ref, right_ref, first=False, given=None, result=None):
+    def tick(
+        self,
+        which,
+        step,
+        left_ref,
+        right_ref,
+        first=False,
+        given=None,
+        result=None,
+        final=True,
+    ):
         half = self.half
         rows = [
             ring_index(target, self.count) * (2 * half) + way * half
@@ -231,12 +241,21 @@
         elif not first:
             self.arrived(which, step)
             total = total + self.slots[which, step - self.base].astype(jnp.float32)
-        if result is None:
+        def pass_on():
             self.slots[which, step - self.base] = total.astype(jnp.bfloat16)
             for way in range(2):
                 self.copy(which, step, way).start()
+
+        def keep():
+            result[...] = total
+
+        if result is None:
+            pass_on()
+        elif final is True:
+            keep()
         else:
-            result[...] = total
+            pl.when(final)(keep)
+            pl.when(jnp.logical_not(final))(pass_on)
 
     def finish(self, which, end):
         for way in range(2):
@@ -273,6 +292,10 @@
 def pair_norm(values, head_dim):
     inverse = lax.rsqrt(pair_mean(values * values, head_dim) + EPS)
     return values * inverse, inverse
+
+
+def as_row(ref):
+    return ref[...].astype(jnp.float32).reshape(1, -1)
 
 
 def double(row):
@@ -315,32 +338,32 @@
         self.core = (self.ctx, self.core_wt)
         self.chip = (self.ctx, self.chip_wt)
 
-    def greet(self, more=()):
-        barrier = pltpu.get_barrier_semaphore()
-        peers = [self.beside, self.core, self.chip, *more]
-        for peer in peers:
-            pl.semaphore_signal(barrier, inc=1, device_id=peer, device_id_type=MESH)
+    def signal(self, peer):
+        pl.semaphore_signal(
+            pltpu.get_barrier_semaphore(), inc=1, device_id=peer, device_id_type=MESH
+        )
+
+    def signal_near(self):
+        for peer in (self.beside, self.core, self.chip):
+            self.signal(peer)
         for there, peer in ((self.has_above, self.above), (self.has_below, self.below)):
 
             @pl.when(there)
             def _():
-                pl.semaphore_signal(barrier, inc=1, device_id=peer, device_id_type=MESH)
-
+                self.signal(peer)
+
+    def await_near(self):
         edges = self.has_above.astype(jnp.int32) + self.has_below.astype(jnp.int32)
-        pl.semaphore_wait(barrier, len(peers) + edges)
-
-
-    def greet_all(self):
-        barrier = pltpu.get_barrier_semaphore()
-
-        def signal(peer):
-            pl.semaphore_signal(barrier, inc=1, device_id=peer, device_id_type=MESH)
-
+        pl.semaphore_wait(pltpu.get_barrier_semaphore(), 3 + edges)
+
+    def signal_all(self):
         for shift in range(1, self.count):
-            signal((lax.rem(self.ctx + shift, self.count), self.wt))
-        signal(self.core)
-        signal(self.chip)
-        pl.semaphore_wait(barrier, self.count + 1)
+            self.signal((lax.rem(self.ctx + shift, self.count), self.wt))
+        self.signal(self.core)
+        self.signal(self.chip)
+
+    def await_all(self):
+        pl.semaphore_wait(pltpu.get_barrier_semaphore(), self.count + 1)
 
 
 def send_to(source, target, send_sem, recv_sem, device):
@@ -484,92 +507,73 @@
         return total
 
 
-def forward_kernel(
-    count,
-    tokens,
-    segments,
-    table,
-    attn_gain,
-    q_gain,
-    k_gain,
-    w_query,
-    w_key,
-    w_value,
-    w_out,
-    cotangent,
-    ffn_gain,
-    w_gate_in,
-    w_up_in,
-    w_down_in,
-    residual,
-    heads_out,
-    mixed_t,
-    query_t,
-    logs,
-    starts,
-    keys_values,
-    keys_t,
-    query_raw,
-    key_raw,
-    normed_t,
-    grad_res,
-    cot_t,
-    normed_ffn_t,
-    ffn_grads,
-    ffn_gain_part,
-    mlp_part,
-    ring_state,
-    all_segs,
-    all_out,
-    all_heads,
-    acc,
-    row_sum,
-    up_send,
-    up_recv,
-    side_send,
-    side_recv,
-    seg_send,
-    seg_recv,
-    out_send,
-    out_recv,
-    head_send,
-    head_recv,
-    w_gate,
-    w_up,
-    w_down,
-    grad_hidden,
-    load_sems,
-    *rest,
-):
+class Mover:
+    def __init__(self, pairs, sems):
+        self.copies = [
+            pltpu.make_async_copy(source, target, sems.at[i])
+            for i, (source, target) in enumerate(pairs)
+        ]
+
+    def start(self, *which):
+        for i in which:
+            self.copies[i].start()
+
+    def wait(self, *which):
+        for i in which:
+            self.copies[i].wait()
+
+
+def forward_kernel(count, names, *refs):
+    ref = dict(zip(names, refs, strict=True))
+    tokens, segments = ref["tokens"], ref["segments"]
+    residual, mixed_t, query_t = ref["residual"], ref["mixed_t"], ref["query_t"]
+    logs, starts, keys_values = ref["logs"], ref["starts"], ref["keys_values"]
+    keys_t, query_raw, key_raw = ref["keys_t"], ref["query_raw"], ref["key_raw"]
+    normed_t, grad_res, lefts = ref["normed_t"], ref["grad_res"], ref["lefts"]
+    ffn_grads, ffn_gain_part = ref["ffn_grads"], ref["ffn_gain_part"]
+    ring_state = ref["ring_state"]
+    all_segs, all_out, all_heads = ref["all_segs"], ref["all_out"], ref["all_heads"]
+    acc, row_sum = ref["acc"], ref["row_sum"]
+    w_gate, w_up, w_down = ref["w_gate"], ref["w_up"], ref["w_down"]
+    gate_t, up_t, grad_hidden = ref["gate_t"], ref["up_t"], ref["grad_hidden"]
+    cotangent, table = ref["cotangent"], ref["table"]
     sequences, tile = segments.shape
-    head_dim = q_gain.shape[1]
+    head_dim = ref["q_gain"].shape[0]
+    pair = 2 * head_dim
     levels = count // 2
     here = Place(count)
     me = here.ctx
-    loads = [
-        pltpu.make_async_copy(source, target, load_sems.at[i])
-        for i, (source, target) in enumerate(
-            ((w_down_in, w_down), (w_gate_in, w_gate), (w_up_in, w_up))
-        )
-    ]
-    for load in loads:
-        load.start()
-    wt_sum = WtSum(here, tile, *rest[:6])
-    ffn = Ring(count, *rest[6:9])
+    loads = Mover(
+        [
+            (ref["table_in"].at[pl.ds(pl.multiple_of(me * tile, tile), tile)], table),
+            (ref["cotangent_in"], cotangent),
+            (ref["w_down_in"], w_down),
+            (ref["w_gate_in"], w_gate),
+            (ref["w_up_in"], w_up),
+        ],
+        ref["load_sems"],
+    )
+    loads.start(0, 1, 2, 3, 4)
+    stores = Mover(
+        [
+            (all_heads.at[here.wt] if name == "heads" else ref[name], ref[name + "_out"])
+            for name in STORED
+        ],
+        ref["store_sems"],
+    )
+    wt_sum = WtSum(here, tile, *(ref[f"wt_sum{i}"] for i in range(6)))
+    ffn = Ring(count, *(ref[f"ring{i}"] for i in range(3)))
+    here.signal_near()
     all_segs[me] = jnp.zeros_like(all_segs[me])
     all_segs[me, pl.ds(0, sequences)] = segments[...]
-    all_out[here.wt] = w_out[...]
-    here.greet()
+    all_out[here.wt] = ref["w_out"][...].T
 
     def out_copy(hop, arriving=False):
         sent = (here.wt, here.wt, here.chip_wt)
         landed = (here.chip_wt, here.core_wt, here.far_wt)
-        ref = all_out.at[(landed if arriving else sent)[hop]]
+        part = all_out.at[(landed if arriving else sent)[hop]]
         device = here.chip if hop == 0 else here.core
-        return send_to(ref, ref, out_send.at[hop], out_recv.at[hop], device)
-
-    out_copy(0).start()
-    out_copy(1).start()
+        return send_to(part, part, ref["out_send"].at[hop], ref["out_recv"].at[hop], device)
 
     def rows_of(seq):
         return pl.ds(pl.multiple_of(seq * tile, tile), tile)
@@ -577,40 +581,26 @@
     def block_of(index, step):
         return lax.rem(index - 2 * step + 2 * count, count)
 
-    def up_copy(step, seq):
+    def up_copy(step, seq, sems=None):
         rows = keys_values.at[block_of(me, step), rows_of(seq)]
-        return send_to(rows, rows, up_send.at[step, seq], up_recv.at[step, seq], here.above)
-
-    def up_wait(step, seq):
-        rows = keys_values.at[block_of(me, step), rows_of(seq)]
-        earlier = step - 1
-        send_to(
-            rows, rows, up_send.at[earlier, seq], up_recv.at[earlier, seq], here.above
-        ).wait_recv()
+        index = step if sems is None else sems
+        return send_to(
+            rows, rows, ref["up_send"].at[index, seq], ref["up_recv"].at[index, seq], here.above
+        )
 
     def side_copy(step, seq, index=me):
         rows = keys_values.at[block_of(index, step), rows_of(seq)]
         return send_to(
-            rows, rows, side_send.at[step, seq], side_recv.at[step, seq], here.beside
-        )
-
-    def side_wait(step, seq):
-        side_copy(step, seq, here.beside_ctx).wait_recv()
-
-    def seg_copy(step, way, index=me):
-        ref = all_segs.at[block_of(index, step)]
+            rows, rows, ref["side_send"].at[step, seq], ref["side_recv"].at[step, seq], here.beside
+        )
+
+    def seg_copy(step, way, index=me, sems=None):
+        part = all_segs.at[block_of(index, step)]
         device = here.beside if way else here.above
-        return send_to(ref, ref, seg_send.at[step, way], seg_recv.at[step, way], device)
-
-    def seg_wait(step, way):
-        if way:
-            seg_copy(step, 1, here.beside_ctx).wait_recv()
-        else:
-            ref = all_segs.at[block_of(me, step)]
-            earlier = step - 1
-            send_to(
-                ref, ref, seg_send.at[earlier, 0], seg_recv.at[earlier, 0], here.above
-            ).wait_recv()
+        at = step if sems is None else sems
+        return send_to(
+            part, part, ref["seg_send"].at[at, way], ref["seg_recv"].at[at, way], device
+        )
 
     def goes_up(step):
         return here.has_above & (me >= 2 * step)
@@ -619,6 +609,10 @@
         block = me - 2 * step
         return (block >= 0) & (block < here.beside_ctx)
 
+    def comes_aside(step):
+        block = here.beside_ctx - 2 * step
+        return (block >= 0) & (block < me)
+
     def pass_segs(step):
         @pl.when(goes_up(step))
         def _():
@@ -637,14 +631,15 @@
         def _():
             side_copy(step, seq).start()
 
-    pass_segs(0)
-    cosine = table[:, pl.ds(0, 2 * head_dim)]
-    sine = table[:, pl.ds(2 * head_dim, 2 * head_dim)]
-    q_gain_pair = double(q_gain[...].astype(jnp.float32))
-    k_gain_pair = double(k_gain[...].astype(jnp.float32))
-    gain = attn_gain[...].astype(jnp.float32)
+    gain = as_row(ref["attn_gain"])
+    q_gain_pair = double(as_row(ref["q_gain"]))
+    k_gain_pair = double(as_row(ref["k_gain"]))
+    ffn_gain_row = as_row(ref["ffn_gain"])
+    loads.wait(0)
 
     def turn(values):
+        cosine = table[:, pl.ds(0, pair)]
+        sine = table[:, pl.ds(pair, pair)]
         return values * cosine + swap_halves(values, head_dim) * sine
 
     def project(seq, carry):
@@ -652,23 +647,33 @@
         inputs = tokens[rows, :].astype(jnp.float32)
         inverse = lax.rsqrt(jnp.mean(inputs * inputs, axis=-1, keepdims=True) + EPS)
         normed = (inputs * inverse * gain).astype(jnp.bfloat16)
-        raw_k = dot_nn(normed, w_key[...])
+        raw_k = dot_nn(normed, ref["w_key"][...])
         key_raw[rows, :] = raw_k
         unit, unused = pair_norm(raw_k, head_dim)
-        keys_values[me, rows, pl.ds(0, 2 * head_dim)] = turn(unit * k_gain_pair).astype(
+        keys_values[me, rows, pl.ds(0, pair)] = turn(unit * k_gain_pair).astype(jnp.bfloat16)
+        keys_values[me, rows, pl.ds(pair, pair)] = dot_nn(normed, ref["w_value"][...]).astype(
             jnp.bfloat16
         )
-        keys_values[me, rows, pl.ds(2 * head_dim, 2 * head_dim)] = dot_nn(
-            normed, w_value[...]
-        ).astype(jnp.bfloat16)
-        pass_rows(0, seq)
-        raw_q = dot_nn(normed, w_query[...])
+
+        @pl.when(seq == 0)
+        def _():
+            here.await_near()
+            pass_segs(0)
+
+        @pl.when(seq < 2)
+        def _():
+            pass_rows(0, seq)
+
+        @pl.when(seq == 0)
+        def _():
+            out_copy(0).start()
+            out_copy(1).start()
+
+        raw_q = dot_nn(normed, ref["w_query"][...])
         query_raw[rows, :] = raw_q
         query_t[seq] = jnp.zeros_like(query_t[seq])
         for group in range(2):
-            unit, unused = pair_norm(
-                raw_q[:, group * 2 * head_dim : (group + 1) * 2 * head_dim], head_dim
-            )
+            unit, unused = pair_norm(raw_q[:, group * pair : (group + 1) * pair], head_dim)
             turned = turn(unit * q_gain_pair) * (head_dim**-0.5)
             flipped = turned.T.astype(jnp.bfloat16)
             for member in range(2):
@@ -684,13 +689,50 @@
         return carry
 
     lax.fori_loop(0, sequences, project, 0)
+    loads.wait(1, 2)
+
+    def back_down(seq, carry):
+        rows = rows_of(seq)
+        grads = cotangent[rows, :]
+        lefts[0, :, rows] = grads.T
+        grad_hidden[rows, :] = dot_nn(grads, w_down[...]).astype(jnp.bfloat16)
+        return carry
+
+    lax.fori_loop(0, sequences, back_down, 0)
+
+    def route(seq):
+        def level(step, carry):
+            @pl.when(me >= 2 * step)
+            def _():
+                @pl.when(seq == 0)
+                def _():
+                    seg_copy(step, 0, me, step - 1).wait_recv()
+                    pass_segs(step)
+
+                up_copy(step, seq, step - 1).wait_recv()
+                pass_rows(step, seq)
+
+            return carry
+
+        lax.fori_loop(1, levels, level, 0)
+
+    route(0)
+    loads.wait(3, 4)
+
+    def flip(index, carry):
+        rows = pl.ds(pl.multiple_of(index * 128, 128), 128)
+        gate_t[:, rows] = w_gate[rows, :].T
+        up_t[:, rows] = w_up[rows, :].T
+        return carry
+
+    lax.fori_loop(0, tokens.shape[1] // 128, flip, 0)
     key_rows = lax.broadcasted_iota(jnp.int32, (tile, 4 * tile), 0)
     query_cols = lax.rem(lax.broadcasted_iota(jnp.int32, (tile, 4 * tile), 1), tile)
 
     def attend(block, seq, own):
         rows = rows_of(seq)
-        keys = keys_values[block, rows, pl.ds(0, 2 * head_dim)]
-        values = keys_values[block, rows, pl.ds(2 * head_dim, 2 * head_dim)]
+        keys = keys_values[block, rows, pl.ds(0, pair)]
+        values = keys_values[block, rows, pl.ds(pair, pair)]
         seg_query = all_segs[me, pl.ds(seq, 1)].astype(jnp.float32)
         seg_key = as_column(all_segs[block, pl.ds(seq, 1)].astype(jnp.float32))
         earlier = jnp.where(seg_key < seg_query, 1.0, 0.0)
@@ -712,70 +754,20 @@
             )
         keys_t[block, seq] = keys.T
 
-    def own_block(seq, carry):
-        attend(me, seq, True)
-        return carry
-
-    lax.fori_loop(0, sequences, own_block, 0)
-    loads[0].wait()
-
-    def back_down(seq, carry):
-        rows = rows_of(seq)
-        grads = cotangent[rows, :]
-        cot_t[:, rows] = grads.T
-        grad_hidden[rows, :] = dot_nn(grads, w_down[...]).astype(jnp.bfloat16)
-        return carry
-
-    lax.fori_loop(0, sequences, back_down, 0)
-
-    @pl.when(goes_back_aside(here, 0))
-    def _():
-        seg_wait(0, 1)
-
-        def side_block(seq, carry):
-            side_wait(0, seq)
-            attend(here.beside_ctx, seq, False)
-            return carry
-
-        lax.fori_loop(0, sequences, side_block, 0)
-
-    out_copy(0, True).wait_recv()
-    out_copy(2).start()
-
-    def level(step, carry):
-        @pl.when(me >= 2 * step)
-        def _():
-            seg_wait(step, 0)
-            pass_segs(step)
-            seg_wait(step, 1)
-
-            def line_block(seq, carry):
-                up_wait(step, seq)
-                pass_rows(step, seq)
-                attend(me - 2 * step, seq, False)
-                return carry
-
-            lax.fori_loop(0, sequences, line_block, 0)
-
-            def side_block(seq, carry):
-                side_wait(step, seq)
-                attend(here.beside_ctx - 2 * step, seq, False)
-                return carry
-
-            lax.fori_loop(0, sequences, side_block, 0)
-
-        return carry
-
-    lax.fori_loop(1, levels, level, 0)
-
     def head_copy(hop, seq, arriving=False):
         sent = (here.wt, here.wt, here.chip_wt)
         landed = (here.chip_wt, here.core_wt, here.far_wt)
-        ref = all_heads.at[(landed if arriving else sent)[hop], rows_of(seq)]
+        part = all_heads.at[(landed if arriving else sent)[hop], rows_of(seq)]
         device = here.chip if hop == 0 else here.core
-        return send_to(ref, ref, head_send.at[hop, seq], head_recv.at[hop, seq], device)
-
-    def mix(seq, carry):
+        return send_to(
+            part, part, ref["head_send"].at[hop, seq], ref["head_recv"].at[hop, seq], device
+        )
+
+    def relay(seq):
+        head_copy(0, seq, True).wait_recv()
+        head_copy(2, seq).start()
+
+    def mix(seq):
         rows = rows_of(seq)
         total = row_sum[seq]
         logs[seq] = jnp.log(total)
@@ -784,22 +776,9 @@
             part = acc[seq, group] / total[:, cols]
             mixed = jnp.concatenate([part[:, :tile], part[:, tile:]], axis=0)
             mixed_t[seq, group] = mixed
-            all_heads[here.wt, rows, pl.ds(group * 2 * head_dim, 2 * head_dim)] = mixed.T.astype(
-                jnp.bfloat16
-            )
+            all_heads[here.wt, rows, pl.ds(group * pair, pair)] = mixed.T.astype(jnp.bfloat16)
         head_copy(0, seq).start()
         head_copy(1, seq).start()
-        return carry
-
-    lax.fori_loop(0, sequences, mix, 0)
-    heads_out[...] = all_heads[here.wt]
-    out_copy(1, True).wait_recv()
-    out_copy(2, True).wait_recv()
-
-    loads[1].wait()
-    loads[2].wait()
-    ffn_gain_row = ffn_gain[...].astype(jnp.float32)
-    ffn_gain_part[...] = jnp.zeros_like(ffn_gain_part)
 
     def ffn_unit(rows):
         values = residual[rows, :]
@@ -808,13 +787,15 @@
 
     def feed(seq):
         rows = rows_of(seq)
+        head_copy(1, seq, True).wait_recv()
+        head_copy(2, seq, True).wait_recv()
         total = tokens[rows, :].astype(jnp.float32)
         for slot in range(4):
-            total = total + dot_nt(all_heads[slot, rows], all_out[slot])
+            total = total + dot_nn(all_heads[slot, rows], all_out[slot])
         residual[rows, :] = total
         unit, unused = ffn_unit(rows)
         normed = (unit * ffn_gain_row).astype(jnp.bfloat16)
-        normed_ffn_t[:, rows] = normed.T
+        lefts[1, :, rows] = normed.T
         gate = dot_nn(normed, w_gate[...])
         up = dot_nn(normed, w_up[...])
         sigmoid = jax.nn.sigmoid(gate)
@@ -825,61 +806,108 @@
         grad_up = (grads * silu).astype(jnp.bfloat16)
         ffn_grads[1, rows] = grad_gate
         ffn_grads[2, rows] = grad_up
-        grad_normed = dot_nt(grad_gate, w_gate[...]) + dot_nt(grad_up, w_up[...])
+        grad_normed = dot_nn(grad_gate, gate_t[...]) + dot_nn(grad_up, up_t[...])
         ffn_gain_part[...] += jnp.sum(grad_normed * unit, axis=0, keepdims=True)
         wt_sum.offer(seq, grad_normed)
 
-    def feed_turn(turn_, carry):
+    ffn_gain_part[...] = jnp.zeros_like(ffn_gain_part)
+
+    def sequence_turn(turn_, carry):
         @pl.when(turn_ < sequences)
         def _():
-            head_copy(0, turn_, True).wait_recv()
-            head_copy(2, turn_).start()
+            attend(me, turn_, True)
+
+            @pl.when(turn_ + 2 < sequences)
+            def _():
+                pass_rows(0, turn_ + 2)
+
+            @pl.when(comes_aside(0))
+            def _():
+                @pl.when(turn_ == 0)
+                def _():
+                    seg_copy(0, 1, here.beside_ctx).wait_recv()
+
+                side_copy(0, turn_, here.beside_ctx).wait_recv()
+                attend(here.beside_ctx, turn_, False)
+
+        @pl.when(turn_ + 1 < sequences)
+        def _():
+            route(turn_ + 1)
+
+        @pl.when(turn_ == 1)
+        def _():
+            out_copy(0, True).wait_recv()
+            out_copy(2).start()
 
         @pl.when(turn_ > 0)
         def _():
-            seq = turn_ - 1
-            head_copy(1, seq, True).wait_recv()
-            head_copy(2, seq, True).wait_recv()
-            feed(seq)
+            relay(turn_ - 1)
+
+        @pl.when(turn_ < sequences)
+        def _():
+            def level(step, carry):
+                @pl.when(me >= 2 * step)
+                def _():
+                    @pl.when(turn_ == 0)
+                    def _():
+                        seg_copy(step, 1, here.beside_ctx).wait_recv()
+
+                    attend(block_of(me, step), turn_, False)
+                    side_copy(step, turn_, here.beside_ctx).wait_recv()
+                    attend(block_of(here.beside_ctx, step), turn_, False)
+
+                return carry
+
+            lax.fori_loop(1, levels, level, 0)
+            mix(turn_)
+
+        @pl.when(turn_ == 1)
+        def _():
+            out_copy(1, True).wait_recv()
+            out_copy(2, True).wait_recv()
 
         @pl.when(turn_ > 1)
         def _():
             wt_sum.cross(turn_ - 2)
 
+        @pl.when(turn_ > 0)
+        def _():
+            feed(turn_ - 1)
+
+        @pl.when(turn_ > 2)
+        def _():
+            wt_sum.close(turn_ - 3)
+
         return carry
 
-    lax.fori_loop(0, sequences + 1, feed_turn, 0)
+    lax.fori_loop(0, sequences + 1, sequence_turn, 0)
+    for i in range(3):
+        ffn.tick(i, 0, lefts.at[min(i, 1)], ffn_grads.at[i], first=True)
+    stores.start(*range(len(STORED) - 2))
     wt_sum.cross(sequences - 1)
-    lefts = (cot_t, normed_ffn_t, normed_ffn_t)
-    for i in range(3):
-        ffn.tick(i, 0, lefts[i], ffn_grads.at[i], first=True)
-    half = tokens.shape[1] // 2
-
-    def down(seq, carry):
-        rows = rows_of(seq)
-        term = dot_nt(ffn_grads[0, rows], w_down[...])
-        mlp_part[0, rows] = term[:, :half].astype(jnp.bfloat16)
-        mlp_part[1, rows] = term[:, half:].astype(jnp.bfloat16)
-        wt_sum.close(seq)
-        return carry
-
-    lax.fori_loop(0, sequences, down, 0)
-    for i in range(3):
-        ffn.tick(i, 1, lefts[i], ffn_grads.at[i])
-
-    def back_norm(seq, carry):
+    wt_sum.close(sequences - 2)
+
+    def back_norm(seq):
         rows = rows_of(seq)
         unit, inverse = ffn_unit(rows)
         scaled = wt_sum.result(seq) * ffn_gain_row
         grads = inverse * (scaled - unit * jnp.mean(scaled * unit, axis=-1, keepdims=True))
         grad_res[rows, :] = (cotangent[rows, :].astype(jnp.float32) + grads).astype(jnp.bfloat16)
+
+    def back_turn(seq, carry):
+        back_norm(seq)
         return carry
 
-    lax.fori_loop(0, sequences, back_norm, 0)
+    lax.fori_loop(0, sequences - 1, back_turn, 0)
+    wt_sum.close(sequences - 1)
+    back_norm(sequences - 1)
+    stores.start(len(STORED) - 2)
     for i in range(3):
-        ffn.arrived(i, 2)
-        ring_state[i] = ffn.slots[i, 2]
-        ffn.finish(i, 2)
+        ffn.arrived(i, 1)
+        ring_state[i] = ffn.slots[i, 1]
+    stores.start(len(STORED) - 1)
+    for i in range(3):
+        ffn.finish(i, 1)
     wt_sum.finish(sequences)
     for hop in range(3):
         out_copy(hop).wait_send()
@@ -914,192 +942,224 @@
         return carry
 
     lax.fori_loop(0, levels, drain, 0)
-
-
-def goes_back_aside(here, step):
-    block = here.beside_ctx - 2 * step
-    return (block >= 0) & (block < here.ctx)
-
-
-def forward(*arrays):
-    tokens, segments, q_gain, w_gate = arrays[0], arrays[1], arrays[4], arrays[12]
+    stores.wait(*range(len(STORED)))
+
+
+STORED = (
+    "heads",
+    "residual",
+    "mixed_t",
+    "query_t",
+    "logs",
+    "starts",
+    "keys_values",
+    "keys_t",
+    "query_raw",
+    "key_raw",
+    "normed_t",
+    "lefts",
+    "ffn_grads",
+    "ffn_gain_part",
+    "grad_res",
+    "ring_state",
+)
+
+
+def forward(inputs):
     count = lax.axis_size("ctx")
-    sequences, tile = segments.shape
-    rows, width = tokens.shape
-    head_dim = q_gain.shape[1]
+    sequences, tile = inputs["segments"].shape
+    rows, width = inputs["tokens"].shape
+    head_dim = inputs["q_gain"].shape[0]
+    hidden = inputs["w_gate_in"].shape[1]
     pair = 2 * head_dim
     levels = count // 2
-    hidden = w_gate.shape[1]
-    vmem = pl.BlockSpec(memory_space=pltpu.VMEM)
     f32, bf16 = jnp.float32, jnp.bfloat16
-    outs = [
-        ((rows, width), f32),
-        ((rows, 2 * pair), bf16),
-        ((sequences, 2, pair, tile), f32),
-        ((sequences, pair, 4 * tile), bf16),
-        ((sequences, 1, 4 * tile), f32),
-        ((sequences, 1, tile), f32),
-        ((count, rows, 2 * pair), bf16),
-        ((count, sequences, pair, tile), bf16),
-        ((rows, 2 * pair), f32),
-        ((rows, pair), f32),
-        ((width, rows), bf16),
-        ((rows, width), bf16),
-        ((width, rows), bf16),
-        ((width, rows), bf16),
-        ((3, rows, hidden), bf16),
-        ((1, width), f32),
-        ((2, rows, width // 2), bf16),
-        ((3, width // count, hidden), bf16),
-    ]
     dma = pltpu.SemaphoreType.DMA
-    return pl.pallas_call(
-        partial(forward_kernel, count),
-        out_shape=[jax.ShapeDtypeStruct(shape, kind) for shape, kind in outs],
-        in_specs=[vmem] * 12 + [pl.BlockSpec(memory_space=pl.ANY)] * 3,
-        out_specs=[vmem] * len(outs),
-        scratch_shapes=[
-            pltpu.VMEM((count, 8, tile), jnp.int32),
-            pltpu.VMEM((4, width, 2 * pair), bf16),
-            pltpu.VMEM((4, rows, 2 * pair), bf16),
-            pltpu.VMEM((sequences, 2, head_dim, 2 * tile), f32),
-            pltpu.VMEM((sequences, 1, 4 * tile), f32),
-            dma((levels, sequences)),
-            dma((levels, sequences)),
-            dma((levels, sequences)),
-            dma((levels, sequences)),
-            dma((levels, 2)),
-            dma((levels, 2)),
-            dma((3,)),
-            dma((3,)),
-            dma((3, sequences)),
-            dma((3, sequences)),
-            pltpu.VMEM((width, hidden), bf16),
-            pltpu.VMEM((width, hidden), bf16),
-            pltpu.VMEM((width, hidden), bf16),
-            pltpu.VMEM((rows, hidden), bf16),
-            dma((3,)),
-            *wt_sum_scratch(sequences, rows, width),
-            *ring_scratch(3, 3, width // count, hidden),
-        ],
+    stored = {
+        "heads": ((rows, 2 * pair), bf16),
+        "residual": ((rows, width), f32),
+        "mixed_t": ((sequences, 2, pair, tile), f32),
+        "query_t": ((sequences, pair, 4 * tile), bf16),
+        "logs": ((sequences, 1, 4 * tile), f32),
+        "starts": ((sequences, 1, tile), f32),
+        "keys_values": ((count, rows, 2 * pair), bf16),
+        "keys_t": ((count, sequences, pair, tile), bf16),
+        "query_raw": ((rows, 2 * pair), f32),
+        "key_raw": ((rows, pair), f32),
+        "normed_t": ((width, rows), bf16),
+        "lefts": ((2, width, rows), bf16),
+        "ffn_grads": ((3, rows, hidden), bf16),
+        "ffn_gain_part": ((1, width), f32),
+        "grad_res": ((rows, width), bf16),
+        "ring_state": ((3, width // count, hidden), bf16),
+    }
+    scratch = {name: pltpu.VMEM(*spec) for name, spec in stored.items() if name != "heads"}
+    scratch |= {
+        "all_segs": pltpu.VMEM((count, 8, tile), jnp.int32),
+        "all_out": pltpu.VMEM((4, 2 * pair, width), bf16),
+        "all_heads": pltpu.VMEM((4, rows, 2 * pair), bf16),
+        "acc": pltpu.VMEM((sequences, 2, head_dim, 2 * tile), f32),
+        "row_sum": pltpu.VMEM((sequences, 1, 4 * tile), f32),
+        "table": pltpu.VMEM((tile, 2 * pair), f32),
+        "cotangent": pltpu.VMEM((rows, width), bf16),
+        "w_down": pltpu.VMEM((width, hidden), bf16),
+        "w_gate": pltpu.VMEM((width, hidden), bf16),
+        "w_up": pltpu.VMEM((width, hidden), bf16),
+        "gate_t": pltpu.VMEM((hidden, width), bf16),
+        "up_t": pltpu.VMEM((hidden, width), bf16),
+        "grad_hidden": pltpu.VMEM((rows, hidden), bf16),
+        "up_send": dma((levels, sequences)),
+        "up_recv": dma((levels, sequences)),
+        "side_send": dma((levels, sequences)),
+        "side_recv": dma((levels, sequences)),
+        "seg_send": dma((levels, 2)),
+        "seg_recv": dma((levels, 2)),
+        "out_send": dma((3,)),
+        "out_recv": dma((3,)),
+        "head_send": dma((3, sequences)),
+        "head_recv": dma((3, sequences)),
+        "load_sems": dma((5,)),
+        "store_sems": dma((len(STORED),)),
+    }
+    for i, kind in enumerate(wt_sum_scratch(sequences, rows, width)):
+        scratch[f"wt_sum{i}"] = kind
+    for i, kind in enumerate(ring_scratch(2, 3, width // count, hidden)):
+        scratch[f"ring{i}"] = kind
+    vmem, anywhere = pl.BlockSpec(memory_space=pltpu.VMEM), pl.BlockSpec(memory_space=pl.ANY)
+    names = (*inputs, *(name + "_out" for name in STORED), *scratch)
+    results = pl.pallas_call(
+        partial(forward_kernel, count, names),
+        out_shape=[jax.ShapeDtypeStruct(*stored[name]) for name in STORED],
+        in_specs=[anywhere if name.endswith("_in") else vmem for name in inputs],
+        out_specs=[anywhere] * len(STORED),
+        scratch_shapes=list(scratch.values()),
         compiler_params=pltpu.CompilerParams(
-            collective_id=2, has_side_effects=True, vmem_limit_bytes=60 * MIB
+            collective_id=2, has_side_effects=True, vmem_limit_bytes=62 * MIB
         ),
-    )(*arrays)
-
-
-def backward_kernel(count, *refs):
-    (
-        grad_res,
-        tokens,
-        table,
-        attn_gain,
-        q_gain,
-        k_gain,
-        w_query,
-        w_key,
-        w_value,
-        w_out,
-        heads,
-        mixed_t,
-        query_t,
-        logs,
-        starts,
-        keys_values,
-        keys_t,
-        query_raw,
-        key_raw,
-        normed_t,
-        cot_t,
-        normed_ffn_t,
-        ffn_grads,
-        ffn_gain_part,
-        residual,
-        mlp_part,
-        ring_state,
-    ) = refs[:27]
-    (
-        output,
-        tokens_grad,
-        down_sum,
-        gate_sum,
-        up_sum,
-        out_sum,
-        query_sum,
-        key_sum,
-        value_sum,
-        attn_gain_sum,
-        ffn_gain_sum,
-        q_gain_sum,
-        k_gain_sum,
-    ) = refs[27:40]
-    (
-        grad_res_t,
-        grad_heads_t,
-        deltas,
-        grad_query_t,
-        own_grads,
-        grad_qkv,
-        side_in,
-        side_out,
-        line_in,
-        line_out,
-        qkv_total,
-        side_send,
-        side_recv,
-        line_send,
-        line_recv,
-    ) = refs[40:55]
-    rest = refs[55:]
+    )(*inputs.values())
+    return dict(zip(STORED, results, strict=True))
+
+
+LOADED = (
+    "ring_state",
+    "lefts",
+    "ffn_grads",
+    "grad_res",
+    "w_out",
+    "mixed_t",
+    "query_t",
+    "logs",
+    "starts",
+    "keys_values",
+    "keys_t",
+    "w_down",
+    "heads",
+    "residual",
+    "table",
+    "query_raw",
+    "key_raw",
+    "w_query",
+    "w_key",
+    "w_value",
+    "tokens",
+    "normed_t",
+)
+RESULTS = (
+    "output",
+    "tokens_grad",
+    "w_down_sum",
+    "w_gate_sum",
+    "w_up_sum",
+    "w_out_sum",
+    "w_query_sum",
+    "w_key_sum",
+    "w_value_sum",
+    "attn_gain_sum",
+    "ffn_gain_sum",
+    "q_gain_sum",
+    "k_gain_sum",
+)
+
+
+def backward_kernel(count, names, *refs):
+    ref = dict(zip(names, refs, strict=True))
+    residual, mixed_t, query_t = ref["residual"], ref["mixed_t"], ref["query_t"]
+    logs, starts, keys_values = ref["logs"], ref["starts"], ref["keys_values"]
+    keys_t, query_raw, key_raw = ref["keys_t"], ref["query_raw"], ref["key_raw"]
+    normed_t, grad_res, lefts = ref["normed_t"], ref["grad_res"], ref["lefts"]
+    ffn_grads, ring_state, heads = ref["ffn_grads"], ref["ring_state"], ref["heads"]
+    tokens, table = ref["tokens"], ref["table"]
+    grad_res_t, grad_heads_t = ref["grad_res_t"], ref["grad_heads_t"]
+    deltas, grad_query_t = ref["deltas"], ref["grad_query_t"]
+    own_grads, grad_qkv = ref["own_grads"], ref["grad_qkv"]
+    side_in, side_out = ref["side_in"], ref["side_out"]
+    line_in, line_out = ref["line_in"], ref["line_out"]
+    ffn_sums, qkv_total = ref["ffn_sums"], ref["qkv_total"]
     sequences, tile = mixed_t.shape[0], mixed_t.shape[3]
-    head_dim = q_gain.shape[1]
+    head_dim = ref["q_gain"].shape[0]
     pair = 2 * head_dim
     levels = count // 2
+    last = count - 1
     here = Place(count)
     me = here.ctx
-    wt_sum = WtSum(here, tile, *rest[:6])
-    gains = GainSum(here, *rest[6:12])
-    gain_slots = rest[6]
-    ffn = Ring(count, *rest[12:15], base=2)
-    out = Ring(count, *rest[15:18])
-    qkv = Ring(count, *rest[18:21])
-    mlp_sum = WtSum(here, tile, mlp_part, *rest[21:26])
-    last = count - 1
-    here.greet_all()
-    lefts = (cot_t, normed_ffn_t, normed_ffn_t)
-    ffn_sums = (down_sum, gate_sum, up_sum)
-
-    def ffn_ticks(step, given=False, final=False):
-        for i in range(3):
-            ffn.tick(
-                i,
-                step,
-                lefts[i],
-                ffn_grads.at[i],
-                given=ring_state.at[i] if given else None,
-                result=ffn_sums[i] if final else None,
+    loads = Mover(
+        [
+            (
+                ref["table_in"].at[pl.ds(pl.multiple_of(me * tile, tile), tile)]
+                if name == "table"
+                else ref[name + "_in"],
+                ref[name],
             )
+            for name in LOADED
+        ],
+        ref["load_sems"],
+    )
+    loads.start(*range(len(LOADED)))
+    sources = {
+        "w_down_sum": ffn_sums.at[0],
+        "w_gate_sum": ffn_sums.at[1],
+        "w_up_sum": ffn_sums.at[2],
+        "w_query_sum": qkv_total.at[:, pl.ds(0, 2 * pair)],
+        "w_key_sum": qkv_total.at[:, pl.ds(2 * pair, pair)],
+        "w_value_sum": qkv_total.at[:, pl.ds(3 * pair, pair)],
+    }
+    stores = Mover(
+        [(sources[name] if name in sources else ref[name], ref[name + "_res"]) for name in RESULTS],
+        ref["store_sems"],
+    )
+    wt_sum = WtSum(here, tile, *(ref[f"wt_sum{i}"] for i in range(6)))
+    mlp_sum = WtSum(here, tile, *(ref[f"mlp_sum{i}"] for i in range(6)))
+    gains = GainSum(here, *(ref[f"gains{i}"] for i in range(6)))
+    gain_slots = ref["gains0"]
+    ffn = Ring(count, *(ref[f"ffn{i}"] for i in range(3)), base=1)
+    out = Ring(count, *(ref[f"out{i}"] for i in range(3)))
+    qkv = Ring(count, *(ref[f"qkv{i}"] for i in range(3)))
+    here.signal_all()
+    loads.wait(0, 1, 2)
+    here.await_all()
+    for i in range(3):
+        ffn.tick(i, 1, lefts.at[min(i, 1)], ffn_grads.at[i], given=ring_state.at[i])
+
+    def ffn_tick(index):
+        step, which = lax.div(index, 3), lax.rem(index, 3)
+        ffn.tick(
+            which,
+            step,
+            lefts.at[lax.min(which, 1)],
+            ffn_grads.at[which],
+            result=ffn_sums.at[which],
+            final=step == last,
+        )
 
     def rows_of(seq):
         return pl.ds(pl.multiple_of(seq * tile, tile), tile)
 
-    ffn_ticks(2, given=True)
-
-    def each(step):
-        def one(seq, carry):
-            step(seq)
-            return carry
-
-        lax.fori_loop(0, sequences, one, 0)
-
-    each(lambda seq: mlp_sum.copy(0, seq).start())
-
-    def prepare(seq, carry):
+    def prepare(seq):
         rows = rows_of(seq)
         grads = grad_res[rows, :]
         grad_res_t[:, rows] = grads.T
         grad_heads_t[seq] = jnp.zeros_like(grad_heads_t[seq])
-        low = dot_nn(grads, w_out[...]).astype(jnp.bfloat16)
+        low = dot_nn(grads, ref["w_out"][...]).astype(jnp.bfloat16)
         for group in range(2):
             flipped = low[:, group * pair : (group + 1) * pair].T
             product_t = flipped.astype(jnp.float32) * mixed_t[seq, group]
@@ -1109,11 +1169,7 @@
                 grad_heads_t[seq, pl.ds(group * head_dim, head_dim), cols] = flipped[part]
                 deltas[seq, :, cols] = jnp.sum(product_t[part], axis=0, keepdims=True)
         grad_query_t[seq] = jnp.zeros_like(grad_query_t[seq])
-        return carry
-
-    lax.fori_loop(0, sequences, prepare, 0)
-    out.tick(0, 0, grad_res_t, heads, first=True)
-    each(mlp_sum.cross)
+
     key_rows = lax.broadcasted_iota(jnp.int32, (tile, 4 * tile), 0)
     query_cols = lax.rem(lax.broadcasted_iota(jnp.int32, (tile, 4 * tile), 1), tile)
 
@@ -1146,8 +1202,8 @@
         return send_to(
             side_out.at[step, rows_of(seq)],
             side_in.at[step, rows_of(seq)],
-            side_send.at[step, seq],
-            side_recv.at[step, seq],
+            ref["side_send"].at[step, seq],
+            ref["side_recv"].at[step, seq],
             here.beside,
         )
 
@@ -1156,88 +1212,48 @@
         return send_to(
             line_out.at[earlier, rows_of(seq)],
             line_in.at[earlier, rows_of(seq)],
-            line_send.at[earlier, seq],
-            line_recv.at[earlier, seq],
+            ref["line_send"].at[earlier, seq],
+            ref["line_recv"].at[earlier, seq],
             here.below,
         )
-
-    def from_above(step, seq):
-        later = step + 1
-        return line_copy(later, seq)
 
     def block_there(step):
         block = here.beside_ctx - 2 * step
         return (block >= 0) & (block < me)
 
-    def block_comes(step):
-        return (me >= 2 * step) & (me - 2 * step < here.beside_ctx)
-
-    def send_aside(step):
+    def send_aside(step, seq):
         @pl.when(block_there(step))
         def _():
-            def one(seq, carry):
-                side_out[step, rows_of(seq)] = grads_of(
-                    here.beside_ctx - 2 * step, seq, False
-                ).astype(jnp.bfloat16)
-                side_copy(step, seq).start()
-                return carry
-
-            lax.fori_loop(0, sequences, one, 0)
-
-    def level(turn_, carry):
-        step = levels - 1 - turn_
-        send_aside(step)
-
+            side_out[step, rows_of(seq)] = grads_of(
+                here.beside_ctx - 2 * step, seq, False
+            ).astype(jnp.bfloat16)
+            side_copy(step, seq).start()
+
+    def send_down(step, seq):
         @pl.when(me >= 2 * step)
         def _():
-            def one(seq, carry):
-                rows = rows_of(seq)
-                own_grads[rows, :] = grads_of(me - 2 * step, seq, False)
-                side_copy(step, seq).wait_recv()
-                total = own_grads[rows, :] + side_in[step, rows].astype(jnp.float32)
-                own_grads[rows, :] = total
-
-                @pl.when(here.has_above)
-                def _():
-                    from_above(step, seq).wait_recv()
-                    own_grads[rows, :] += line_in[step, rows].astype(jnp.float32)
-
-                line_out[step - 1, rows] = own_grads[rows, :].astype(jnp.bfloat16)
-                line_copy(step, seq).start()
-                return carry
-
-            lax.fori_loop(0, sequences, one, 0)
-
-        ffn_ticks(3 + turn_)
-        out.tick(0, 1 + turn_, grad_res_t, heads)
-        return carry
-
-    lax.fori_loop(0, levels - 1, level, 0)
-    send_aside(0)
-    each(mlp_sum.close)
-
-    def own_block(seq, carry):
-        own_grads[rows_of(seq), :] = grads_of(me, seq, True)
-        return carry
-
-    lax.fori_loop(0, sequences, own_block, 0)
-    ffn_ticks(levels + 2)
-    out.tick(0, levels, grad_res_t, heads)
-
-    def output_rows(seq):
-        rows = rows_of(seq)
-        output[rows, :] = (residual[rows, :] + mlp_sum.result(seq)).astype(jnp.bfloat16)
-
-    each(output_rows)
-    cosine = table[:, pl.ds(0, pair)]
-    sine = table[:, pl.ds(pair, pair)]
-    q_gain_pair = double(q_gain[...].astype(jnp.float32))
-    k_gain_pair = double(k_gain[...].astype(jnp.float32))
-    gain = attn_gain[...].astype(jnp.float32)
+            rows = rows_of(seq)
+            own_grads[rows, :] = grads_of(me - 2 * step, seq, False)
+            side_copy(step, seq).wait_recv()
+            own_grads[rows, :] += side_in[step, rows].astype(jnp.float32)
+
+            @pl.when(here.has_above)
+            def _():
+                line_copy(step + 1, seq).wait_recv()
+                own_grads[rows, :] += line_in[step, rows].astype(jnp.float32)
+
+            line_out[step - 1, rows] = own_grads[rows, :].astype(jnp.bfloat16)
+            line_copy(step, seq).start()
+
+    gain = as_row(ref["attn_gain"])
+    q_gain_pair = double(as_row(ref["q_gain"]))
+    k_gain_pair = double(as_row(ref["k_gain"]))
     gain_slots[me] = jnp.zeros_like(gain_slots[me])
-    gain_slots[me, pl.ds(1, 1)] = ffn_gain_part[...]
+    gain_slots[me, pl.ds(1, 1)] = ref["ffn_gain_part"][...]
 
     def back_through(grads, raw, gain_pair, row):
+        cosine = table[:, pl.ds(0, pair)]
+        sine = table[:, pl.ds(pair, pair)]
         turned = grads * cosine - swap_halves(grads, head_dim) * sine
         unit, inverse = pair_norm(raw, head_dim)
         gain_slots[me, pl.ds(row, 1), pl.ds(0, pair)] += jnp.sum(
@@ -1253,7 +1269,7 @@
         inverse = lax.rsqrt(jnp.mean(inputs * inputs, axis=-1, keepdims=True) + EPS)
         return inputs * inverse, inverse
 
-    def project_back(seq, carry):
+    def project_back(seq):
         rows = rows_of(seq)
         for group in range(2):
             grads = grad_query_t[seq, group] * (head_dim**-0.5)
@@ -1261,14 +1277,14 @@
             cols = pl.ds(group * pair, pair)
             grad_qkv[rows, cols] = back_through(grads, query_raw[rows, cols], q_gain_pair, 2)
 
-        @pl.when(block_comes(0))
+        @pl.when(me < here.beside_ctx)
         def _():
             side_copy(0, seq).wait_recv()
             own_grads[rows, :] += side_in[0, rows].astype(jnp.float32)
 
         @pl.when(here.has_above)
         def _():
-            from_above(0, seq).wait_recv()
+            line_copy(1, seq).wait_recv()
             own_grads[rows, :] += line_in[0, rows].astype(jnp.float32)
 
         grad_qkv[rows, pl.ds(2 * pair, pair)] = back_through(
@@ -1278,73 +1294,133 @@
             jnp.bfloat16
         )
         grads = (
-            dot_nt(grad_qkv[rows, pl.ds(0, 2 * pair)], w_query[...])
-            + dot_nt(grad_qkv[rows, pl.ds(2 * pair, pair)], w_key[...])
-            + dot_nt(grad_qkv[rows, pl.ds(3 * pair, pair)], w_value[...])
-        )
-        unit, inverse = token_unit(rows)
+            dot_nt(grad_qkv[rows, pl.ds(0, 2 * pair)], ref["w_query"][...])
+            + dot_nt(grad_qkv[rows, pl.ds(2 * pair, pair)], ref["w_key"][...])
+            + dot_nt(grad_qkv[rows, pl.ds(3 * pair, pair)], ref["w_value"][...])
+        )
+        unit, unused = token_unit(rows)
         gain_slots[me, pl.ds(0, 1)] += jnp.sum(grads * unit, axis=0, keepdims=True)
         wt_sum.offer(seq, grads)
-        return carry
-
-    lax.fori_loop(0, sequences, project_back, 0)
-    gains.start()
-    qkv.tick(0, 0, normed_t, grad_qkv, first=True)
-
-    def crossing(seq, carry):
-        wt_sum.cross(seq)
-        return carry
-
-    lax.fori_loop(0, sequences, crossing, 0)
-
-    def tail(step, carry):
-        qkv.tick(0, step, normed_t, grad_qkv)
-
-        @pl.when(step + levels < last)
-        def _():
-            out.tick(0, step + levels, grad_res_t, heads)
-
-        return carry
-
-    ffn_ticks(last, final=True)
-    lax.fori_loop(1, last - 1, tail, 0)
-    out.tick(0, last, grad_res_t, heads, result=out_sum)
-
-    def closing(seq, carry):
-        wt_sum.close(seq)
-        return carry
-
-    lax.fori_loop(0, sequences, closing, 0)
-    qkv.tick(0, last - 1, normed_t, grad_qkv)
-
-    def token_rows(seq, carry):
+
+    def output_rows(seq):
+        rows = rows_of(seq)
+        ref["output"][rows, :] = (residual[rows, :] + mlp_sum.result(seq)).astype(jnp.bfloat16)
+
+    def token_rows(seq):
         rows = rows_of(seq)
         unit, inverse = token_unit(rows)
         scaled = wt_sum.result(seq) * gain
         grads = inverse * (scaled - unit * jnp.mean(scaled * unit, axis=-1, keepdims=True))
-        tokens_grad[rows, :] = (grad_res[rows, :].astype(jnp.float32) + grads).astype(
+        ref["tokens_grad"][rows, :] = (grad_res[rows, :].astype(jnp.float32) + grads).astype(
             jnp.bfloat16
         )
+
+    loads.wait(*range(3, len(LOADED)))
+
+    def sequence_turn(turn_, carry):
+        @pl.when(turn_ + 1 < sequences)
+        def _():
+            prepare(turn_ + 1)
+
+            def aside(index, carry):
+                send_aside(levels - 1 - index, turn_ + 1)
+                return carry
+
+            lax.fori_loop(0, levels, aside, 0)
+
+        @pl.when((turn_ >= 0) & (turn_ < sequences))
+        def _():
+            def down(index, carry):
+                send_down(levels - 1 - index, turn_)
+                return carry
+
+            lax.fori_loop(0, levels - 1, down, 0)
+            rows = rows_of(turn_)
+            own_grads[rows, :] = grads_of(me, turn_, True)
+            mlp_sum.offer(turn_, dot_nt(ffn_grads[0, rows], ref["w_down"][...]))
+
+        ffn_tick(turn_ + 7)
+
+        @pl.when((turn_ >= 1) & (turn_ <= sequences))
+        def _():
+            mlp_sum.cross(turn_ - 1)
+
+        @pl.when(turn_ == sequences)
+        def _():
+            out.tick(0, 0, grad_res_t, heads, first=True)
+
+        @pl.when(turn_ == sequences + 1)
+        def _():
+            out.tick(0, 1, grad_res_t, heads)
+
+        @pl.when(turn_ >= 2)
+        def _():
+            project_back(turn_ - 2)
+            mlp_sum.close(turn_ - 2)
+
+        @pl.when(turn_ >= 3)
+        def _():
+            wt_sum.cross(turn_ - 3)
+            output_rows(turn_ - 3)
+
         return carry
 
-    lax.fori_loop(0, sequences, token_rows, 0)
+    turns = sequences + 3
+    lax.fori_loop(-1, turns - 1, sequence_turn, 0)
+    qkv.tick(0, 0, normed_t, grad_qkv, first=True)
+    gains.start()
+    wt_sum.cross(sequences - 1)
+    output_rows(sequences - 1)
+    stores.start(0)
+    left_over = 3 * count - 6 - turns
+    each = -(-left_over // (last - 1))
+
+    def tail(step, carry):
+        for i in range(each):
+            index = 6 + turns + each * (step - 1) + i
+
+            @pl.when(index < 3 * count)
+            def _():
+                ffn_tick(index)
+
+        qkv.tick(0, step, normed_t, grad_qkv)
+
+        @pl.when(step < last)
+        def _():
+            out.tick(
+                0, step + 1, grad_res_t, heads, result=ref["w_out_sum"], final=step + 1 == last
+            )
+
+        @pl.when(step <= sequences)
+        def _():
+            wt_sum.close(step - 1)
+
+        @pl.when((step >= 2) & (step <= sequences + 1))
+        def _():
+            token_rows(step - 2)
+
+        return carry
+
+    middle = min(4, last)
+    lax.fori_loop(1, middle, tail, 0)
     total = gains.total()
-    attn_gain_sum[...] = total[0:1]
-    ffn_gain_sum[...] = total[1:2]
+    ref["attn_gain_sum"][...] = total[0:1]
+    ref["ffn_gain_sum"][...] = total[1:2]
     folded = total[:, :pair]
     folded = folded + pltpu.roll(folded, head_dim, 1)
-    q_gain_sum[...] = folded[2:3, :head_dim]
-    k_gain_sum[...] = folded[3:4, :head_dim]
+    ref["q_gain_sum"][...] = folded[2:3]
+    ref["k_gain_sum"][...] = folded[3:4]
+    stores.start(9, 10, 11, 12)
+    lax.fori_loop(middle, last, tail, 0)
+    stores.start(1, 2, 3, 4, 5)
     qkv.tick(0, last, normed_t, grad_qkv, result=qkv_total)
-    query_sum[...] = qkv_total[:, pl.ds(0, 2 * pair)]
-    key_sum[...] = qkv_total[:, pl.ds(2 * pair, pair)]
-    value_sum[...] = qkv_total[:, pl.ds(3 * pair, pair)]
+    stores.start(6, 7, 8)
     wt_sum.finish(sequences)
+    mlp_sum.finish(sequences)
     for i in range(3):
         ffn.finish(i, last)
     out.finish(0, last)
     qkv.finish(0, last)
-    mlp_sum.finish(sequences)
 
     def drain(step, carry):
         @pl.when(block_there(step))
@@ -1366,73 +1442,103 @@
         return carry
 
     lax.fori_loop(0, levels, drain, 0)
-
-
-def backward(*arrays):
-    (grad_res, tokens, table, attn_gain, q_gain) = arrays[:5]
-    mixed_t, cot_t, ffn_grads = arrays[11], arrays[20], arrays[22]
+    stores.wait(*range(len(RESULTS)))
+
+
+def backward(inputs):
     count = lax.axis_size("ctx")
-    sequences, tile = mixed_t.shape[0], mixed_t.shape[3]
-    rows, width = tokens.shape
-    head_dim = q_gain.shape[1]
+    sequences, tile = inputs["mixed_t_in"].shape[0], inputs["mixed_t_in"].shape[3]
+    rows, width = inputs["tokens_in"].shape
+    head_dim = inputs["q_gain"].shape[0]
+    hidden = inputs["ffn_grads_in"].shape[2]
     pair = 2 * head_dim
     levels = count // 2
     block = width // count
-    hidden = ffn_grads.shape[2]
-    vmem = pl.BlockSpec(memory_space=pltpu.VMEM)
     f32, bf16 = jnp.float32, jnp.bfloat16
-    outs = [
-        ((rows, width), bf16),
-        ((rows, width), bf16),
-        ((block, hidden), f32),
-        ((block, hidden), f32),
-        ((block, hidden), f32),
-        ((block, 2 * pair), f32),
-        ((block, 2 * pair), f32),
-        ((block, pair), f32),
-        ((block, pair), f32),
-        ((1, width), f32),
-        ((1, width), f32),
-        ((1, head_dim), f32),
-        ((1, head_dim), f32),
-    ]
     dma = pltpu.SemaphoreType.DMA
-    return pl.pallas_call(
-        partial(backward_kernel, count),
-        out_shape=[jax.ShapeDtypeStruct(shape, kind) for shape, kind in outs],
-        in_specs=[vmem] * len(arrays),
-        out_specs=[vmem] * len(outs),
-        scratch_shapes=[
-            pltpu.VMEM((width, rows), bf16),
-            pltpu.VMEM((sequences, pair, 4 * tile), bf16),
-            pltpu.VMEM((sequences, 1, 4 * tile), f32),
-            pltpu.VMEM((sequences, 2, head_dim, 2 * tile), f32),
-            pltpu.VMEM((rows, 2 * pair), f32),
-            pltpu.VMEM((rows, 4 * pair), bf16),
-            pltpu.VMEM((levels, rows, 2 * pair), bf16),
-            pltpu.VMEM((levels, rows, 2 * pair), bf16),
-            pltpu.VMEM((levels - 1, rows, 2 * pair), bf16),
-            pltpu.VMEM((levels - 1, rows, 2 * pair), bf16),
-            pltpu.VMEM((block, 4 * pair), f32),
-            dma((levels, sequences)),
-            dma((levels, sequences)),
-            dma((levels - 1, sequences)),
-            dma((levels - 1, sequences)),
-            *wt_sum_scratch(sequences, rows, width),
-            pltpu.VMEM((count, 8, width), f32),
-            pltpu.VMEM((2, 2, 8, width), f32),
-            dma((count - 1,)),
-            dma((count - 1,)),
-            dma((2,)),
-            dma((2,)),
-            *ring_scratch(count - 2, 3, block, hidden),
-            *ring_scratch(count, 1, block, 2 * pair),
-            *ring_scratch(count, 1, block, 4 * pair),
-            *wt_sum_scratch(sequences, rows, width)[1:],
-        ],
+    results = {
+        "output": ((rows, width), bf16),
+        "tokens_grad": ((rows, width), bf16),
+        "w_down_sum": ((block, hidden), f32),
+        "w_gate_sum": ((block, hidden), f32),
+        "w_up_sum": ((block, hidden), f32),
+        "w_out_sum": ((block, 2 * pair), f32),
+        "w_query_sum": ((block, 2 * pair), f32),
+        "w_key_sum": ((block, pair), f32),
+        "w_value_sum": ((block, pair), f32),
+        "attn_gain_sum": ((1, width), f32),
+        "ffn_gain_sum": ((1, width), f32),
+        "q_gain_sum": ((1, pair), f32),
+        "k_gain_sum": ((1, pair), f32),
+    }
+    staged = ("output", "tokens_grad", "w_out_sum") + RESULTS[9:]
+    scratch = {name: pltpu.VMEM(*results[name]) for name in staged}
+    for name in LOADED:
+        kind = inputs[name + "_in"]
+        shape = (tile, kind.shape[1]) if name == "table" else kind.shape
+        scratch[name] = pltpu.VMEM(shape, kind.dtype)
+    scratch |= {
+        "grad_res_t": pltpu.VMEM((width, rows), bf16),
+        "grad_heads_t": pltpu.VMEM((sequences, pair, 4 * tile), bf16),
+        "deltas": pltpu.VMEM((sequences, 1, 4 * tile), f32),
+        "grad_query_t": pltpu.VMEM((sequences, 2, head_dim, 2 * tile), f32),
+        "own_grads": pltpu.VMEM((rows, 2 * pair), f32),
+        "grad_qkv": pltpu.VMEM((rows, 4 * pair), bf16),
+        "side_in": pltpu.VMEM((levels, rows, 2 * pair), bf16),
+        "side_out": pltpu.VMEM((levels, rows, 2 * pair), bf16),
+        "line_in": pltpu.VMEM((levels - 1, rows, 2 * pair), bf16),
+        "line_out": pltpu.VMEM((levels - 1, rows, 2 * pair), bf16),
+        "ffn_sums": pltpu.VMEM((3, block, hidden), f32),
+        "qkv_total": pltpu.VMEM((block, 4 * pair), f32),
+        "side_send": dma((levels, sequences)),
+        "side_recv": dma((levels, sequences)),
+        "line_send": dma((levels - 1, sequences)),
+        "line_recv": dma((levels - 1, sequences)),
+        "load_sems": dma((len(LOADED),)),
+        "store_sems": dma((len(RESULTS),)),
+        "gains0": pltpu.VMEM((count, 8, width), f32),
+        "gains1": pltpu.VMEM((2, 2, 8, width), f32),
+        "gains2": dma((count - 1,)),
+        "gains3": dma((count - 1,)),
+        "gains4": dma((2,)),
+        "gains5": dma((2,)),
+    }
+    for label, kinds in (
+        ("wt_sum", wt_sum_scratch(sequences, rows, width)),
+        ("mlp_sum", wt_sum_scratch(sequences, rows, width)),
+        ("ffn", ring_scratch(count - 1, 3, block, hidden)),
+        ("out", ring_scratch(count, 1, block, 2 * pair)),
+        ("qkv", ring_scratch(count, 1, block, 4 * pair)),
+    ):
+        scratch |= {f"{label}{i}": kind for i, kind in enumerate(kinds)}
+    vmem, anywhere = pl.BlockSpec(memory_space=pltpu.VMEM), pl.BlockSpec(memory_space=pl.ANY)
+    names = (*inputs, *(name + "_res" for name in RESULTS), *scratch)
+    arrays = pl.pallas_call(
+        partial(backward_kernel, count, names),
+        out_shape=[jax.ShapeDtypeStruct(*results[name]) for name in RESULTS],
+        in_specs=[anywhere if name.endswith("_in") else vmem for name in inputs],
+        out_specs=[anywhere] * len(RESULTS),
+        scratch_shapes=list(scratch.values()),
         compiler_params=pltpu.CompilerParams(
             collective_id=3, has_side_effects=True, vmem_limit_bytes=62 * MIB
         ),
+    )(*inputs.values())
+    return dict(zip(RESULTS, arrays, strict=True))
+
+
+def hand_over_kernel(count, *refs):
+    for source, target in zip(refs[:count], refs[count:], strict=True):
+        target[...] = source[...]
+
+
+def hand_over(arrays):
+    vmem = pl.BlockSpec(memory_space=pltpu.VMEM)
+    return pl.pallas_call(
+        partial(hand_over_kernel, len(arrays)),
+        out_shape=[jax.ShapeDtypeStruct(array.shape, array.dtype) for array in arrays],
+        in_specs=[vmem] * len(arrays),
+        out_specs=[vmem] * len(arrays),
+        compiler_params=pltpu.CompilerParams(vmem_limit_bytes=32 * MIB),
     )(*arrays)
 
 
@@ -1689,102 +1795,55 @@
     sequences, seq_rows, model_width = tokens.shape
     count, head_dim = lax.axis_size("ctx"), q_gain.shape[0]
     token_rows = tokens.reshape(sequences * seq_rows, model_width)
-    table = lax.dynamic_slice_in_dim(
-        jnp.asarray(rotary_table(count * seq_rows, head_dim)),
-        lax.axis_index("ctx") * seq_rows,
-        seq_rows,
-        0,
-    )
-    gains = (attn_gain[None], q_gain[None], k_gain[None])
-    (
-        residual,
-        heads,
-        mixed_t,
-        query_t,
-        logs,
-        starts,
-        keys_values,
-        keys_t,
-        query_raw,
-        key_raw,
-        normed_t,
-        grad_residual,
-        cot_t,
-        normed_ffn_t,
-        ffn_grads,
-        ffn_gain_part,
-        mlp_part,
-        ring_state,
-    ) = forward(
-        token_rows,
-        segments,
-        table,
-        *gains,
-        w_query,
-        key_matrix,
-        value_matrix,
-        w_out,
-        cotangent.reshape(token_rows.shape),
-        ffn_gain[None],
-        w_gate,
-        w_up,
-        w_down,
-    )
-    (
-        output_rows,
-        tokens_grad,
-        w_down_grad,
-        w_gate_grad,
-        w_up_grad,
-        w_out_grad,
-        w_query_grad,
-        w_key_grad,
-        w_value_grad,
-        attn_gain_grad,
-        ffn_gain_grad,
-        q_gain_grad,
-        k_gain_grad,
-    ) = backward(
-        grad_residual,
-        token_rows,
-        table,
-        *gains,
-        w_query,
-        key_matrix,
-        value_matrix,
-        w_out,
-        heads,
-        mixed_t,
-        query_t,
-        logs,
-        starts,
-        keys_values,
-        keys_t,
-        query_raw,
-        key_raw,
-        normed_t,
-        cot_t,
-        normed_ffn_t,
-        ffn_grads,
-        ffn_gain_part,
-        residual,
-        mlp_part,
-        ring_state,
-    )
+    table = jnp.asarray(rotary_table(count * seq_rows, head_dim))
+    gains = {"attn_gain": attn_gain, "q_gain": q_gain, "k_gain": k_gain}
+    kept = forward(
+        {
+            "tokens": token_rows,
+            "segments": segments,
+            **gains,
+            "ffn_gain": ffn_gain,
+            "w_query": w_query,
+            "w_key": key_matrix,
+            "w_value": value_matrix,
+            "w_out": w_out,
+            "table_in": table,
+            "cotangent_in": cotangent.reshape(token_rows.shape),
+            "w_down_in": w_down,
+            "w_gate_in": w_gate,
+            "w_up_in": w_up,
+        }
+    )
+    ffn_gain_part = kept.pop("ffn_gain_part")
+    sums = backward(
+        {
+            **gains,
+            "ffn_gain_part": ffn_gain_part,
+            **{name + "_in": array for name, array in kept.items()},
+            "tokens_in": token_rows,
+            "table_in": table,
+            "w_query_in": w_query,
+            "w_key_in": key_matrix,
+            "w_value_in": value_matrix,
+            "w_out_in": w_out,
+            "w_down_in": w_down,
+        }
+    )
+    done = dict(zip(RESULTS, hand_over([sums[name] for name in RESULTS]), strict=True))
     return (
-        output_rows.reshape(tokens.shape),
-        tokens_grad.reshape(tokens.shape),
-        attn_gain_grad[0],
-        w_query_grad,
-        w_key_grad,
-        w_value_grad,
-        q_gain_grad[0],
-        k_gain_grad[0],
-        w_out_grad,
-        ffn_gain_grad[0],
-        w_gate_grad,
-        w_up_grad,
-        w_down_grad,
+        done["output"].reshape(tokens.shape),
+        done["tokens_grad"].reshape(tokens.shape),
+        done["attn_gain_sum"][0],
+        done["w_query_sum"],
+        done["w_key_sum"],
+        done["w_value_sum"],
+        done["q_gain_sum"][0, :head_dim],
+        done["k_gain_sum"][0, :head_dim],
+        done["w_out_sum"],
+        done["ffn_gain_sum"][0],
+        done["w_gate_sum"],
+        done["w_up_sum"],
+        done["w_down_sum"],
     )
 
 

time: 242 us -> 207 us (0.86)
  Pallas kernels: 226 us -> 193 us
  local copies, waits for them, and re-layouts: 15.1 us -> 12.4 us
    pallas_call x2 -> x3, Pallas kernels: 226 us -> 193 us  [the longest x1 134 us: backward(): pl.pallas_call(partial(backward_kernel, count, names), out_shape=[jax.Sha...]
    broadcast_in_dim x2 -> x0, local copies, waits for them, and re-layouts: 2.56 us -> none  [the longest x1 1.28 us: on_device(): gains = (attn_gain[None], q_gain[None], k_gain[None])]
    unnamed x37 -> x26, local copies, waits for them, and re-layouts: 11 us -> 11.9 us
where the time goes in v5:
time: 207 us; the launch traced here: 206 us
  Pallas kernels  193 us (93%)
  local copies, waits for them, and re-layouts  12.4 us (6%)
    pallas_call x1, Pallas kernels, backward(): pl.pallas_call(partial(backward_kernel, count, names), out_shape=[jax.Sha...  134 us
    pallas_call x1, Pallas kernels, forward(): pl.pallas_call(partial(forward_kernel, count, names), out_shape=[jax.Shap...  55.9 us
    unnamed x26, local copies, waits for them, and re-layouts  11.9 us

profile of v5, /device:TPU:0, one launch (start us, length us, event | category | flops | bytes accessed | tf_op | source)
XLA Modules:
  0.0 205.9 jit_solution(2569723776089349483)
XLA Ops:
  0.6 55.9 %shard_map.246 = (bf16[640,256]{1,0:T(8,128)(2,1)}, f32[640,1024]{1,0:T(8,128)}, f32[5,2,128,128]{3,2,1,0:T(8,128)}, bf16[5,128,512]{2,1,0:T(8,128)(2,1)}, f32[5...) custom-call(bf16[640,1024]{1,0:T(8,128)(2,1)} %bitcast.10, ...), custom_call_target="tpu_custom_call" | custom-call | tf_op jit(solution)/shard_map/pallas_call | solution.py:1030
  56.5 134.4 %shard_map.247 = (bf16[640,1024]{1,0:T(8,128)(2,1)}, bf16[640,1024]{1,0:T(8,128)(2,1)}, f32[128,1152]{1,0:T(8,128)}, f32[128,1152]{1,0:T(8,128)}, f32[128,1152]{...) custom-call(bf16[1024]{0:T(1024)(128)(2,1)} %refs_0_.1, ...), custom_call_target="tpu_custom_call" | custom-call | tf_op jit(solution)/shard_map/pallas_call | solution.py:1516
  190.9 0.0 copy-start
  191.0 1.3 copy-done
  192.3 0.0 copy-start.1
  192.3 1.3 copy-done.1
  193.6 0.0 copy-start.2
  193.6 1.1 copy-done.2
  194.6 0.0 copy-start.3
  194.6 1.1 copy-done.3
  195.7 0.0 copy-start.4
  195.7 1.1 copy-done.4
  196.8 0.0 copy-start.5
  196.8 0.9 copy-done.5
  197.7 0.0 copy-start.6
  197.7 0.9 copy-done.6
  198.6 0.0 copy-start.7
  198.6 0.8 copy-done.7
  199.4 0.0 copy-start.8
  199.4 0.8 copy-done.8
  200.3 0.0 copy-start.9
  200.3 0.7 copy-done.9
  200.9 0.0 copy-start.10
  200.9 0.7 copy-done.10
  201.6 0.0 copy-start.11
  201.6 0.7 copy-done.11
  202.3 0.0 copy-start.12
  202.3 0.6 copy-done.12
  202.9 2.5 %shard_map.248 = (bf16[640,1024]{1,0:T(8,128)(2,1)}, bf16[640,1024]{1,0:T(8,128)(2,1)}, f32[128,1152]{1,0:T(8,128)}, f32[128,1152]{1,0:T(8,128)}, f32[128,1152]{...) custom-call(bf16[640,1024]{1,0:T(8,128)(2,1)S(1)} %copy-done, ...), custom_call_target="tpu_custom_call" | custom-call | tf_op jit(solution)/shard_map/pallas_call | solution.py:1536
  205.4 0.5 slice_bitcast_fusion
Async XLA Ops:
  190.9 1.3 copy-start
  192.3 1.3 copy-start.1
  193.6 1.1 copy-start.2
  194.6 1.1 copy-start.3
  195.7 1.1 copy-start.4
  196.8 0.9 copy-start.5
  197.7 0.9 copy-start.6
  198.6 0.8 copy-start.7
  199.4 0.8 copy-start.8
  200.3 0.7 copy-start.9
  200.9 0.7 copy-start.10
  201.6 0.7 copy-start.11
  202.3 0.6 copy-start.12

commit v6 on v5

--- a/solution.py
+++ b/solution.py
@@ -343,19 +343,6 @@
             pltpu.get_barrier_semaphore(), inc=1, device_id=peer, device_id_type=MESH
         )
 
-    def signal_near(self):
-        for peer in (self.beside, self.core, self.chip):
-            self.signal(peer)
-        for there, peer in ((self.has_above, self.above), (self.has_below, self.below)):
-
-            @pl.when(there)
-            def _():
-                self.signal(peer)
-
-    def await_near(self):
-        edges = self.has_above.astype(jnp.int32) + self.has_below.astype(jnp.int32)
-        pl.semaphore_wait(pltpu.get_barrier_semaphore(), 3 + edges)
-
     def signal_all(self):
         for shift in range(1, self.count):
             self.signal((lax.rem(self.ctx + shift, self.count), self.wt))
@@ -378,20 +365,24 @@
 
 
 class WtSum:
-    def __init__(self, here, tile, part, got, far, full, send_sems, recv_sems):
-        self.here, self.tile = here, tile
+    def __init__(self, here, tile, part, got, far, full, send_sems, recv_sems, before=None):
+        self.here, self.tile, self.before = here, tile, before
         self.part, self.got, self.far, self.full = part, got, far, full
         self.send_sems, self.recv_sems = send_sems, recv_sems
         self.mine, self.theirs = here.core_bit, 1 - here.core_bit
+        self.half = got.shape[1]
 
     def rows(self, seq):
         return pl.ds(pl.multiple_of(seq * self.tile, self.tile), self.tile)
+
+    def cols(self, half):
+        return pl.ds(pl.multiple_of(half * self.half, self.half), self.half)
 
     def copy(self, hop, seq, arriving=False):
         rows = self.rows(seq)
         half = self.theirs if arriving else self.mine
         source = (
-            self.part.at[self.theirs, rows],
+            self.part.at[rows, self.cols(self.theirs)],
             self.got.at[rows],
             self.full.at[half, rows],
         )[hop]
@@ -402,25 +393,24 @@
         )
 
     def offer(self, seq, value):
-        rows = self.rows(seq)
-        half = value.shape[1] // 2
-        self.part[0, rows] = value[:, :half].astype(jnp.bfloat16)
-        self.part[1, rows] = value[:, half:].astype(jnp.bfloat16)
+        self.part[self.rows(seq), pl.ds(0, 2 * self.half)] = value.astype(jnp.bfloat16)
         self.copy(0, seq).start()
 
     def cross(self, seq):
         rows = self.rows(seq)
         self.copy(0, seq).wait_recv()
-        total = self.part[self.mine, rows].astype(jnp.float32) + self.got[rows].astype(
-            jnp.float32
-        )
+        total = self.part[rows, self.cols(self.mine)].astype(jnp.float32) + self.got[
+            rows
+        ].astype(jnp.float32)
         self.got[rows] = total.astype(jnp.bfloat16)
         self.copy(1, seq).start()
 
     def close(self, seq):
         rows = self.rows(seq)
-        self.copy(1, seq).wait_recv()
+        self.copy(1, seq).wait()
         total = self.got[rows].astype(jnp.float32) + self.far[rows].astype(jnp.float32)
+        if self.before is not None:
+            self.before.copy(2, seq).wait_send()
         self.full[self.mine, rows] = total.astype(jnp.bfloat16)
         self.copy(2, seq).start()
 
@@ -431,25 +421,13 @@
             jnp.float32
         )
 
-    def finish(self, sequences):
+    def finish(self, sequences, hops=(0, 2)):
         def sent(seq, carry):
-            for hop in range(3):
+            for hop in hops:
                 self.copy(hop, seq).wait_send()
             return carry
 
         lax.fori_loop(0, sequences, sent, 0)
-
-
-def wt_sum_scratch(sequences, rows, width):
-    half = width // 2
-    return [
-        pltpu.VMEM((2, rows, half), jnp.bfloat16),
-        pltpu.VMEM((rows, half), jnp.bfloat16),
-        pltpu.VMEM((rows, half), jnp.bfloat16),
-        pltpu.VMEM((2, rows, half), jnp.bfloat16),
-        pltpu.SemaphoreType.DMA((3, sequences)),
-        pltpu.SemaphoreType.DMA((3, sequences)),
-    ]
 
 
 def ring_scratch(count, arrays, rows, width):
@@ -523,15 +501,33 @@
             self.copies[i].wait()
 
 
-def forward_kernel(count, names, *refs):
+TURN_TICKS = 1
+VMEM_LIMIT = 63 * MIB
+RESULTS = (
+    "output",
+    "tokens_grad",
+    "w_down_sum",
+    "w_gate_sum",
+    "w_up_sum",
+    "w_out_sum",
+    "w_query_sum",
+    "w_key_sum",
+    "w_value_sum",
+    "attn_gain_sum",
+    "ffn_gain_sum",
+    "q_gain_sum",
+    "k_gain_sum",
+)
+
+
+def layer_kernel(count, names, *refs):
     ref = dict(zip(names, refs, strict=True))
     tokens, segments = ref["tokens"], ref["segments"]
     residual, mixed_t, query_t = ref["residual"], ref["mixed_t"], ref["query_t"]
     logs, starts, keys_values = ref["logs"], ref["starts"], ref["keys_values"]
-    keys_t, query_raw, key_raw = ref["keys_t"], ref["query_raw"], ref["key_raw"]
-    normed_t, grad_res, lefts = ref["normed_t"], ref["grad_res"], ref["lefts"]
+    query_raw, key_raw = ref["query_raw"], ref["key_raw"]
+    grad_res, lefts = ref["grad_res"], ref["lefts"]
     ffn_grads, ffn_gain_part = ref["ffn_grads"], ref["ffn_gain_part"]
-    ring_state = ref["ring_state"]
     all_segs, all_out, all_heads = ref["all_segs"], ref["all_out"], ref["all_heads"]
     acc, row_sum = ref["acc"], ref["row_sum"]
     w_gate, w_up, w_down = ref["w_gate"], ref["w_up"], ref["w_down"]
@@ -550,20 +546,15 @@
             (ref["w_down_in"], w_down),
             (ref["w_gate_in"], w_gate),
             (ref["w_up_in"], w_up),
+            (ref["tokens_in"], tokens),
         ],
         ref["load_sems"],
     )
-    loads.start(0, 1, 2, 3, 4)
-    stores = Mover(
-        [
-            (all_heads.at[here.wt] if name == "heads" else ref[name], ref[name + "_out"])
-            for name in STORED
-        ],
-        ref["store_sems"],
-    )
-    wt_sum = WtSum(here, tile, *(ref[f"wt_sum{i}"] for i in range(6)))
-    ffn = Ring(count, *(ref[f"ring{i}"] for i in range(3)))
-    here.signal_near()
+    loads.start(5, 0, 1, 2, 3, 4)
+    shared = [ref[name] for name in ("sum_got", "sum_far", "sum_full")]
+    ffn_sum = WtSum(here, tile, ref["ffn_part"], *shared, ref["ffn_send"], ref["ffn_recv"])
+    ffn = Ring(count, *(ref[f"ffn{i}"] for i in range(3)))
+    here.signal_all()
     all_segs[me] = jnp.zeros_like(all_segs[me])
     all_segs[me, pl.ds(0, sequences)] = segments[...]
     all_out[here.wt] = ref["w_out"][...].T
@@ -635,7 +626,7 @@
     q_gain_pair = double(as_row(ref["q_gain"]))
     k_gain_pair = double(as_row(ref["k_gain"]))
     ffn_gain_row = as_row(ref["ffn_gain"])
-    loads.wait(0)
+    loads.wait(0, 5)
 
     def turn(values):
         cosine = table[:, pl.ds(0, pair)]
@@ -657,7 +648,7 @@
 
         @pl.when(seq == 0)
         def _():
-            here.await_near()
+            here.await_all()
             pass_segs(0)
 
         @pl.when(seq < 2)
@@ -682,7 +673,6 @@
                     pl.ds(group * head_dim, head_dim),
                     pl.ds((2 * group + member) * tile, tile),
                 ] = flipped[member * head_dim : (member + 1) * head_dim]
-        normed_t[:, rows] = normed.T
         acc[seq] = jnp.zeros_like(acc[seq])
         row_sum[seq] = jnp.zeros_like(row_sum[seq])
         starts[seq] = jnp.zeros_like(starts[seq])
@@ -726,33 +716,35 @@
         return carry
 
     lax.fori_loop(0, tokens.shape[1] // 128, flip, 0)
-    key_rows = lax.broadcasted_iota(jnp.int32, (tile, 4 * tile), 0)
-    query_cols = lax.rem(lax.broadcasted_iota(jnp.int32, (tile, 4 * tile), 1), tile)
-
-    def attend(block, seq, own):
+    key_rows = lax.broadcasted_iota(jnp.int32, (tile, tile), 0)
+    query_cols = lax.broadcasted_iota(jnp.int32, (tile, tile), 1)
+
+    def attend(blocks, seq):
         rows = rows_of(seq)
-        keys = keys_values[block, rows, pl.ds(0, pair)]
-        values = keys_values[block, rows, pl.ds(pair, pair)]
         seg_query = all_segs[me, pl.ds(seq, 1)].astype(jnp.float32)
-        seg_key = as_column(all_segs[block, pl.ds(seq, 1)].astype(jnp.float32))
-        earlier = jnp.where(seg_key < seg_query, 1.0, 0.0)
-        starts[seq] += jnp.sum(earlier, axis=0, keepdims=True)
-        seg_wide = jnp.concatenate([seg_query] * 4, axis=1)
-        if own:
-            allowed = (seg_key == seg_wide) & (key_rows <= query_cols)
-        else:
-            allowed = seg_key >= seg_wide
-        scores = dot_nn(keys, query_t[seq])
-        weights = jnp.where(allowed, jnp.exp(scores), 0.0)
+        masks, values_t = [], []
+        for block in blocks:
+            seg_key = as_column(all_segs[block, pl.ds(seq, 1)].astype(jnp.float32))
+            earlier = jnp.where(seg_key < seg_query, 1.0, 0.0)
+            starts[seq] += jnp.sum(earlier, axis=0, keepdims=True)
+            if block is me:
+                same = (seg_key == seg_query) & (key_rows <= query_cols)
+                masks.append(jnp.where(same, 1.0, 0.0))
+            else:
+                masks.append(1.0 - earlier)
+            values_t.append(keys_values[block, rows, pl.ds(pair, pair)].T)
+        keys = [keys_values[block, rows, pl.ds(0, pair)] for block in blocks]
+        mask = jnp.concatenate(masks, axis=0)
+        scores = dot_nn(jnp.concatenate(keys, axis=0), query_t[seq])
+        weights = jnp.exp(scores) * jnp.concatenate([mask] * 4, axis=1)
         row_sum[seq] += jnp.sum(weights, axis=0, keepdims=True)
         low = weights.astype(jnp.bfloat16)
-        values_t = values.T
+        value_rows = jnp.concatenate(values_t, axis=1)
         for group in range(2):
             acc[seq, group] += dot_nn(
-                values_t[group * head_dim : (group + 1) * head_dim],
+                value_rows[group * head_dim : (group + 1) * head_dim],
                 low[:, group * 2 * tile : (group + 1) * 2 * tile],
             )
-        keys_t[block, seq] = keys.T
 
     def head_copy(hop, seq, arriving=False):
         sent = (here.wt, here.wt, here.chip_wt)
@@ -798,7 +790,7 @@
         lefts[1, :, rows] = normed.T
         gate = dot_nn(normed, w_gate[...])
         up = dot_nn(normed, w_up[...])
-        sigmoid = jax.nn.sigmoid(gate)
+        sigmoid = 0.5 * jnp.tanh(0.5 * gate) + 0.5
         silu = gate * sigmoid
         ffn_grads[0, rows] = (silu * up).astype(jnp.bfloat16)
         grads = grad_hidden[rows, :].astype(jnp.float32)
@@ -808,15 +800,13 @@
         ffn_grads[2, rows] = grad_up
         grad_normed = dot_nn(grad_gate, gate_t[...]) + dot_nn(grad_up, up_t[...])
         ffn_gain_part[...] += jnp.sum(grad_normed * unit, axis=0, keepdims=True)
-        wt_sum.offer(seq, grad_normed)
+        ffn_sum.offer(seq, grad_normed)
 
     ffn_gain_part[...] = jnp.zeros_like(ffn_gain_part)
 
     def sequence_turn(turn_, carry):
         @pl.when(turn_ < sequences)
         def _():
-            attend(me, turn_, True)
-
             @pl.when(turn_ + 2 < sequences)
             def _():
                 pass_rows(0, turn_ + 2)
@@ -828,7 +818,11 @@
                     seg_copy(0, 1, here.beside_ctx).wait_recv()
 
                 side_copy(0, turn_, here.beside_ctx).wait_recv()
-                attend(here.beside_ctx, turn_, False)
+                attend([me, here.beside_ctx], turn_)
+
+            @pl.when(jnp.logical_not(comes_aside(0)))
+            def _():
+                attend([me], turn_)
 
         @pl.when(turn_ + 1 < sequences)
         def _():
@@ -852,9 +846,8 @@
                     def _():
                         seg_copy(step, 1, here.beside_ctx).wait_recv()
 
-                    attend(block_of(me, step), turn_, False)
                     side_copy(step, turn_, here.beside_ctx).wait_recv()
-                    attend(block_of(here.beside_ctx, step), turn_, False)
+                    attend([block_of(me, step), block_of(here.beside_ctx, step)], turn_)
 
                 return carry
 
@@ -868,7 +861,7 @@
 
         @pl.when(turn_ > 1)
         def _():
-            wt_sum.cross(turn_ - 2)
+            ffn_sum.cross(turn_ - 2)
 
         @pl.when(turn_ > 0)
         def _():
@@ -876,246 +869,31 @@
 
         @pl.when(turn_ > 2)
         def _():
-            wt_sum.close(turn_ - 3)
+            ffn_sum.close(turn_ - 3)
 
         return carry
 
     lax.fori_loop(0, sequences + 1, sequence_turn, 0)
     for i in range(3):
         ffn.tick(i, 0, lefts.at[min(i, 1)], ffn_grads.at[i], first=True)
-    stores.start(*range(len(STORED) - 2))
-    wt_sum.cross(sequences - 1)
-    wt_sum.close(sequences - 2)
-
-    def back_norm(seq):
-        rows = rows_of(seq)
-        unit, inverse = ffn_unit(rows)
-        scaled = wt_sum.result(seq) * ffn_gain_row
-        grads = inverse * (scaled - unit * jnp.mean(scaled * unit, axis=-1, keepdims=True))
-        grad_res[rows, :] = (cotangent[rows, :].astype(jnp.float32) + grads).astype(jnp.bfloat16)
-
-    def back_turn(seq, carry):
-        back_norm(seq)
-        return carry
-
-    lax.fori_loop(0, sequences - 1, back_turn, 0)
-    wt_sum.close(sequences - 1)
-    back_norm(sequences - 1)
-    stores.start(len(STORED) - 2)
-    for i in range(3):
-        ffn.arrived(i, 1)
-        ring_state[i] = ffn.slots[i, 1]
-    stores.start(len(STORED) - 1)
-    for i in range(3):
-        ffn.finish(i, 1)
-    wt_sum.finish(sequences)
-    for hop in range(3):
-        out_copy(hop).wait_send()
-
-        def sent(seq, carry):
-            head_copy(hop, seq).wait_send()
-            return carry
-
-        lax.fori_loop(0, sequences, sent, 0)
-
-    def drain(step, carry):
-        @pl.when(goes_up(step))
-        def _():
-            seg_copy(step, 0).wait_send()
-
-            def sent(seq, carry):
-                up_copy(step, seq).wait_send()
-                return carry
-
-            lax.fori_loop(0, sequences, sent, 0)
-
-        @pl.when(goes_aside(step))
-        def _():
-            seg_copy(step, 1).wait_send()
-
-            def sent(seq, carry):
-                side_copy(step, seq).wait_send()
-                return carry
-
-            lax.fori_loop(0, sequences, sent, 0)
-
-        return carry
-
-    lax.fori_loop(0, levels, drain, 0)
-    stores.wait(*range(len(STORED)))
-
-
-STORED = (
-    "heads",
-    "residual",
-    "mixed_t",
-    "query_t",
-    "logs",
-    "starts",
-    "keys_values",
-    "keys_t",
-    "query_raw",
-    "key_raw",
-    "normed_t",
-    "lefts",
-    "ffn_grads",
-    "ffn_gain_part",
-    "grad_res",
-    "ring_state",
-)
-
-
-def forward(inputs):
-    count = lax.axis_size("ctx")
-    sequences, tile = inputs["segments"].shape
-    rows, width = inputs["tokens"].shape
-    head_dim = inputs["q_gain"].shape[0]
-    hidden = inputs["w_gate_in"].shape[1]
-    pair = 2 * head_dim
-    levels = count // 2
-    f32, bf16 = jnp.float32, jnp.bfloat16
-    dma = pltpu.SemaphoreType.DMA
-    stored = {
-        "heads": ((rows, 2 * pair), bf16),
-        "residual": ((rows, width), f32),
-        "mixed_t": ((sequences, 2, pair, tile), f32),
-        "query_t": ((sequences, pair, 4 * tile), bf16),
-        "logs": ((sequences, 1, 4 * tile), f32),
-        "starts": ((sequences, 1, tile), f32),
-        "keys_values": ((count, rows, 2 * pair), bf16),
-        "keys_t": ((count, sequences, pair, tile), bf16),
-        "query_raw": ((rows, 2 * pair), f32),
-        "key_raw": ((rows, pair), f32),
-        "normed_t": ((width, rows), bf16),
-        "lefts": ((2, width, rows), bf16),
-        "ffn_grads": ((3, rows, hidden), bf16),
-        "ffn_gain_part": ((1, width), f32),
-        "grad_res": ((rows, width), bf16),
-        "ring_state": ((3, width // count, hidden), bf16),
-    }
-    scratch = {name: pltpu.VMEM(*spec) for name, spec in stored.items() if name != "heads"}
-    scratch |= {
-        "all_segs": pltpu.VMEM((count, 8, tile), jnp.int32),
-        "all_out": pltpu.VMEM((4, 2 * pair, width), bf16),
-        "all_heads": pltpu.VMEM((4, rows, 2 * pair), bf16),
-        "acc": pltpu.VMEM((sequences, 2, head_dim, 2 * tile), f32),
-        "row_sum": pltpu.VMEM((sequences, 1, 4 * tile), f32),
-        "table": pltpu.VMEM((tile, 2 * pair), f32),
-        "cotangent": pltpu.VMEM((rows, width), bf16),
-        "w_down": pltpu.VMEM((width, hidden), bf16),
-        "w_gate": pltpu.VMEM((width, hidden), bf16),
-        "w_up": pltpu.VMEM((width, hidden), bf16),
-        "gate_t": pltpu.VMEM((hidden, width), bf16),
-        "up_t": pltpu.VMEM((hidden, width), bf16),
-        "grad_hidden": pltpu.VMEM((rows, hidden), bf16),
-        "up_send": dma((levels, sequences)),
-        "up_recv": dma((levels, sequences)),
-        "side_send": dma((levels, sequences)),
-        "side_recv": dma((levels, sequences)),
-        "seg_send": dma((levels, 2)),
-        "seg_recv": dma((levels, 2)),
-        "out_send": dma((3,)),
-        "out_recv": dma((3,)),
-        "head_send": dma((3, sequences)),
-        "head_recv": dma((3, sequences)),
-        "load_sems": dma((5,)),
-        "store_sems": dma((len(STORED),)),
-    }
-    for i, kind in enumerate(wt_sum_scratch(sequences, rows, width)):
-        scratch[f"wt_sum{i}"] = kind
-    for i, kind in enumerate(ring_scratch(2, 3, width // count, hidden)):
-        scratch[f"ring{i}"] = kind
-    vmem, anywhere = pl.BlockSpec(memory_space=pltpu.VMEM), pl.BlockSpec(memory_space=pl.ANY)
-    names = (*inputs, *(name + "_out" for name in STORED), *scratch)
-    results = pl.pallas_call(
-        partial(forward_kernel, count, names),
-        out_shape=[jax.ShapeDtypeStruct(*stored[name]) for name in STORED],
-        in_specs=[anywhere if name.endswith("_in") else vmem for name in inputs],
-        out_specs=[anywhere] * len(STORED),
-        scratch_shapes=list(scratch.values()),
-        compiler_params=pltpu.CompilerParams(
-            collective_id=2, has_side_effects=True, vmem_limit_bytes=62 * MIB
-        ),
-    )(*inputs.values())
-    return dict(zip(STORED, results, strict=True))
-
-
-LOADED = (
-    "ring_state",
-    "lefts",
-    "ffn_grads",
-    "grad_res",
-    "w_out",
-    "mixed_t",
-    "query_t",
-    "logs",
-    "starts",
-    "keys_values",
-    "keys_t",
-    "w_down",
-    "heads",
-    "residual",
-    "table",
-    "query_raw",
-    "key_raw",
-    "w_query",
-    "w_key",
-    "w_value",
-    "tokens",
-    "normed_t",
-)
-RESULTS = (
-    "output",
-    "tokens_grad",
-    "w_down_sum",
-    "w_gate_sum",
-    "w_up_sum",
-    "w_out_sum",
-    "w_query_sum",
-    "w_key_sum",
-    "w_value_sum",
-    "attn_gain_sum",
-    "ffn_gain_sum",
-    "q_gain_sum",
-    "k_gain_sum",
-)
-
-
-def backward_kernel(count, names, *refs):
-    ref = dict(zip(names, refs, strict=True))
-    residual, mixed_t, query_t = ref["residual"], ref["mixed_t"], ref["query_t"]
-    logs, starts, keys_values = ref["logs"], ref["starts"], ref["keys_values"]
-    keys_t, query_raw, key_raw = ref["keys_t"], ref["query_raw"], ref["key_raw"]
-    normed_t, grad_res, lefts = ref["normed_t"], ref["grad_res"], ref["lefts"]
-    ffn_grads, ring_state, heads = ref["ffn_grads"], ref["ring_state"], ref["heads"]
-    tokens, table = ref["tokens"], ref["table"]
-    grad_res_t, grad_heads_t = ref["grad_res_t"], ref["grad_heads_t"]
-    deltas, grad_query_t = ref["deltas"], ref["grad_query_t"]
-    own_grads, grad_qkv = ref["own_grads"], ref["grad_qkv"]
+    rows_all, width = tokens.shape
+    last = count - 1
+    deltas, own_grads = ref["deltas"], ref["own_grads"]
     side_in, side_out = ref["side_in"], ref["side_out"]
     line_in, line_out = ref["line_in"], ref["line_out"]
     ffn_sums, qkv_total = ref["ffn_sums"], ref["qkv_total"]
-    sequences, tile = mixed_t.shape[0], mixed_t.shape[3]
-    head_dim = ref["q_gain"].shape[0]
-    pair = 2 * head_dim
-    levels = count // 2
-    last = count - 1
-    here = Place(count)
-    me = here.ctx
-    loads = Mover(
-        [
-            (
-                ref["table_in"].at[pl.ds(pl.multiple_of(me * tile, tile), tile)]
-                if name == "table"
-                else ref[name + "_in"],
-                ref[name],
-            )
-            for name in LOADED
-        ],
-        ref["load_sems"],
-    )
-    loads.start(*range(len(LOADED)))
+    grad_query_t = acc
+    grad_res_t = w_gate.at[:, pl.ds(0, rows_all)]
+    grad_heads_t = w_gate
+    query_n = gate_t.at[pl.ds(0, 4 * tile)]
+    grad_heads_n = gate_t.at[pl.ds(4 * tile, 4 * tile)]
+    grad_qkv = w_up.at[pl.ds(0, rows_all), pl.ds(0, 4 * pair)]
+    normed_t = w_up.at[:, pl.ds(4 * pair, rows_all)]
+    qkv_t = up_t.at[pl.ds(rows_all, 4 * pair)]
+    heads = all_heads.at[here.wt]
     sources = {
+        "output": cotangent,
+        "tokens_grad": tokens,
         "w_down_sum": ffn_sums.at[0],
         "w_gate_sum": ffn_sums.at[1],
         "w_up_sum": ffn_sums.at[2],
@@ -1127,18 +905,19 @@
         [(sources[name] if name in sources else ref[name], ref[name + "_res"]) for name in RESULTS],
         ref["store_sems"],
     )
-    wt_sum = WtSum(here, tile, *(ref[f"wt_sum{i}"] for i in range(6)))
-    mlp_sum = WtSum(here, tile, *(ref[f"mlp_sum{i}"] for i in range(6)))
+    wt_sum = WtSum(here, tile, up_t, *shared, ref["wt_send"], ref["wt_recv"], ffn_sum)
+    mlp_sum = WtSum(here, tile, grad_hidden, *(ref[f"mlp_sum{i}"] for i in range(5)))
     gains = GainSum(here, *(ref[f"gains{i}"] for i in range(6)))
     gain_slots = ref["gains0"]
-    ffn = Ring(count, *(ref[f"ffn{i}"] for i in range(3)), base=1)
     out = Ring(count, *(ref[f"out{i}"] for i in range(3)))
     qkv = Ring(count, *(ref[f"qkv{i}"] for i in range(3)))
-    here.signal_all()
-    loads.wait(0, 1, 2)
-    here.await_all()
-    for i in range(3):
-        ffn.tick(i, 1, lefts.at[min(i, 1)], ffn_grads.at[i], given=ring_state.at[i])
+
+    def heads_at(seq):
+        start = pl.multiple_of(seq * pair, pair)
+        return (pl.ds(start, pair), pl.ds(rows_all, 4 * tile))
+
+    def seq_cols(seq):
+        return (slice(None), pl.ds(pl.multiple_of(seq * tile, tile), tile))
 
     def ffn_tick(index):
         step, which = lax.div(index, 3), lax.rem(index, 3)
@@ -1151,14 +930,22 @@
             final=step == last,
         )
 
-    def rows_of(seq):
-        return pl.ds(pl.multiple_of(seq * tile, tile), tile)
+    def token_unit(rows):
+        inputs = tokens[rows, :].astype(jnp.float32)
+        inverse = lax.rsqrt(jnp.mean(inputs * inputs, axis=-1, keepdims=True) + EPS)
+        return inputs * inverse, inverse
 
     def prepare(seq):
         rows = rows_of(seq)
-        grads = grad_res[rows, :]
+        unit, inverse = ffn_unit(rows)
+        scaled = ffn_sum.result(seq) * ffn_gain_row
+        back = inverse * (scaled - unit * jnp.mean(scaled * unit, axis=-1, keepdims=True))
+        grads = (cotangent[rows, :].astype(jnp.float32) + back).astype(jnp.bfloat16)
+        grad_res[rows, :] = grads
         grad_res_t[:, rows] = grads.T
-        grad_heads_t[seq] = jnp.zeros_like(grad_heads_t[seq])
+        unit, unused = token_unit(rows)
+        normed_t[:, rows] = (unit * gain).astype(jnp.bfloat16).T
+        grad_heads_t[heads_at(seq)] = jnp.zeros((pair, 4 * tile), jnp.bfloat16)
         low = dot_nn(grads, ref["w_out"][...]).astype(jnp.bfloat16)
         for group in range(2):
             flipped = low[:, group * pair : (group + 1) * pair].T
@@ -1166,44 +953,49 @@
             for member in range(2):
                 part = slice(member * head_dim, (member + 1) * head_dim)
                 cols = pl.ds((2 * group + member) * tile, tile)
-                grad_heads_t[seq, pl.ds(group * head_dim, head_dim), cols] = flipped[part]
+                into = pl.ds(pl.multiple_of(seq * pair + group * head_dim, head_dim), head_dim)
+                spot = pl.ds(rows_all + (2 * group + member) * tile, tile)
+                grad_heads_t[into, spot] = flipped[part]
                 deltas[seq, :, cols] = jnp.sum(product_t[part], axis=0, keepdims=True)
+        grad_heads_n[seq_cols(seq)] = grad_heads_t[heads_at(seq)].T
+        query_n[seq_cols(seq)] = query_t[seq].T
         grad_query_t[seq] = jnp.zeros_like(grad_query_t[seq])
 
-    key_rows = lax.broadcasted_iota(jnp.int32, (tile, 4 * tile), 0)
-    query_cols = lax.rem(lax.broadcasted_iota(jnp.int32, (tile, 4 * tile), 1), tile)
-
-    def grads_of(block, seq, own):
+    def grads_of(blocks, seq):
         rows = rows_of(seq)
-        keys = keys_values[block, rows, pl.ds(0, pair)]
-        values = keys_values[block, rows, pl.ds(pair, pair)]
-        places = (key_rows + block * tile).astype(jnp.float32)
-        start = starts[seq]
-        allowed = places >= jnp.concatenate([start] * 4, axis=1)
-        if own:
-            allowed = allowed & (key_rows <= query_cols)
-        queries = query_t[seq]
-        grad_heads = grad_heads_t[seq]
-        scores = dot_nn(keys, queries)
-        probs = jnp.where(allowed, jnp.exp(scores - logs[seq]), 0.0)
-        grad_probs = dot_nn(values, grad_heads)
+        keys = [keys_values[block, rows, pl.ds(0, pair)] for block in blocks]
+        values = [keys_values[block, rows, pl.ds(pair, pair)] for block in blocks]
+        masks = []
+        for block in blocks:
+            allowed = key_rows.astype(jnp.float32) >= starts[seq] - (block * tile).astype(
+                jnp.float32
+            )
+            if block is me:
+                allowed = allowed & (key_rows <= query_cols)
+            masks.append(jnp.where(allowed, 1.0, 0.0))
+        mask = jnp.concatenate(masks, axis=0)
+        grad_heads = grad_heads_t[heads_at(seq)]
+        scores = dot_nn(jnp.concatenate(keys, axis=0), query_t[seq])
+        probs = jnp.exp(scores - logs[seq]) * jnp.concatenate([mask] * 4, axis=1)
+        grad_probs = dot_nn(jnp.concatenate(values, axis=0), grad_heads)
         grad_scores = (probs * (grad_probs - deltas[seq])).astype(jnp.bfloat16)
-        flipped = keys_t[block, seq]
+        flipped = jnp.concatenate([part.T for part in keys], axis=1)
         for group in range(2):
             cols = slice(group * 2 * tile, (group + 1) * 2 * tile)
             grad_query_t[seq, group] += dot_nn(
                 flipped[group * head_dim : (group + 1) * head_dim], grad_scores[:, cols]
             )
-        grad_keys = dot_nt(grad_scores, queries)
-        grad_values = dot_nt(probs.astype(jnp.bfloat16), grad_heads)
-        return jnp.concatenate([grad_keys, grad_values], axis=1)
-
-    def side_copy(step, seq):
+        grad_keys = dot_nn(grad_scores, query_n[seq_cols(seq)])
+        grad_values = dot_nn(probs.astype(jnp.bfloat16), grad_heads_n[seq_cols(seq)])
+        both = jnp.concatenate([grad_keys, grad_values], axis=1)
+        return [both[i * tile : (i + 1) * tile] for i in range(len(blocks))]
+
+    def side_grad_copy(step, seq):
         return send_to(
             side_out.at[step, rows_of(seq)],
             side_in.at[step, rows_of(seq)],
-            ref["side_send"].at[step, seq],
-            ref["side_recv"].at[step, seq],
+            ref["side_grad_send"].at[step, seq],
+            ref["side_grad_recv"].at[step, seq],
             here.beside,
         )
 
@@ -1217,39 +1009,60 @@
             here.below,
         )
 
-    def block_there(step):
-        block = here.beside_ctx - 2 * step
-        return (block >= 0) & (block < me)
-
-    def send_aside(step, seq):
-        @pl.when(block_there(step))
-        def _():
-            side_out[step, rows_of(seq)] = grads_of(
-                here.beside_ctx - 2 * step, seq, False
-            ).astype(jnp.bfloat16)
-            side_copy(step, seq).start()
+    def find_grads(seq):
+        rows = rows_of(seq)
+
+        def level(index, carry):
+            step = levels - 1 - index
+
+            @pl.when(me >= 2 * step)
+            def _():
+                line, side = grads_of(
+                    [block_of(me, step), block_of(here.beside_ctx, step)], seq
+                )
+                side_out[step, rows] = side.astype(jnp.bfloat16)
+                side_grad_copy(step, seq).start()
+                line_out[step - 1, rows] = line.astype(jnp.bfloat16)
+
+            return carry
+
+        lax.fori_loop(0, levels - 1, level, 0)
+
+        @pl.when(comes_aside(0))
+        def _():
+            own, side = grads_of([me, here.beside_ctx], seq)
+            side_out[0, rows] = side.astype(jnp.bfloat16)
+            side_grad_copy(0, seq).start()
+            own_grads[rows, :] = own
+
+        @pl.when(jnp.logical_not(comes_aside(0)))
+        def _():
+            own_grads[rows, :] = grads_of([me], seq)[0]
 
     def send_down(step, seq):
         @pl.when(me >= 2 * step)
         def _():
             rows = rows_of(seq)
-            own_grads[rows, :] = grads_of(me - 2 * step, seq, False)
-            side_copy(step, seq).wait_recv()
-            own_grads[rows, :] += side_in[step, rows].astype(jnp.float32)
+            side_grad_copy(step, seq).wait_recv()
+            total = line_out[step - 1, rows].astype(jnp.float32) + side_in[step, rows].astype(
+                jnp.float32
+            )
 
             @pl.when(here.has_above)
             def _():
                 line_copy(step + 1, seq).wait_recv()
-                own_grads[rows, :] += line_in[step, rows].astype(jnp.float32)
-
-            line_out[step - 1, rows] = own_grads[rows, :].astype(jnp.bfloat16)
+                line_out[step - 1, rows] = (
+                    total + line_in[step, rows].astype(jnp.float32)
+                ).astype(jnp.bfloat16)
+
+            @pl.when(jnp.logical_not(here.has_above))
+            def _():
+                line_out[step - 1, rows] = total.astype(jnp.bfloat16)
+
             line_copy(step, seq).start()
 
-    gain = as_row(ref["attn_gain"])
-    q_gain_pair = double(as_row(ref["q_gain"]))
-    k_gain_pair = double(as_row(ref["k_gain"]))
     gain_slots[me] = jnp.zeros_like(gain_slots[me])
-    gain_slots[me, pl.ds(1, 1)] = ref["ffn_gain_part"][...]
+    gain_slots[me, pl.ds(1, 1)] = ffn_gain_part[...]
 
     def back_through(grads, raw, gain_pair, row):
         cosine = table[:, pl.ds(0, pair)]
@@ -1264,11 +1077,6 @@
             jnp.bfloat16
         )
 
-    def token_unit(rows):
-        inputs = tokens[rows, :].astype(jnp.float32)
-        inverse = lax.rsqrt(jnp.mean(inputs * inputs, axis=-1, keepdims=True) + EPS)
-        return inputs * inverse, inverse
-
     def project_back(seq):
         rows = rows_of(seq)
         for group in range(2):
@@ -1279,7 +1087,7 @@
 
         @pl.when(me < here.beside_ctx)
         def _():
-            side_copy(0, seq).wait_recv()
+            side_grad_copy(0, seq).wait_recv()
             own_grads[rows, :] += side_in[0, rows].astype(jnp.float32)
 
         @pl.when(here.has_above)
@@ -1293,40 +1101,38 @@
         grad_qkv[rows, pl.ds(3 * pair, pair)] = own_grads[rows, pl.ds(pair, pair)].astype(
             jnp.bfloat16
         )
-        grads = (
-            dot_nt(grad_qkv[rows, pl.ds(0, 2 * pair)], ref["w_query"][...])
-            + dot_nt(grad_qkv[rows, pl.ds(2 * pair, pair)], ref["w_key"][...])
-            + dot_nt(grad_qkv[rows, pl.ds(3 * pair, pair)], ref["w_value"][...])
-        )
+        grads = dot_nn(grad_qkv[rows, :], qkv_t[...])
         unit, unused = token_unit(rows)
         gain_slots[me, pl.ds(0, 1)] += jnp.sum(grads * unit, axis=0, keepdims=True)
         wt_sum.offer(seq, grads)
 
     def output_rows(seq):
         rows = rows_of(seq)
-        ref["output"][rows, :] = (residual[rows, :] + mlp_sum.result(seq)).astype(jnp.bfloat16)
+        cotangent[rows, :] = (residual[rows, :] + mlp_sum.result(seq)).astype(jnp.bfloat16)
 
     def token_rows(seq):
         rows = rows_of(seq)
         unit, inverse = token_unit(rows)
         scaled = wt_sum.result(seq) * gain
         grads = inverse * (scaled - unit * jnp.mean(scaled * unit, axis=-1, keepdims=True))
-        ref["tokens_grad"][rows, :] = (grad_res[rows, :].astype(jnp.float32) + grads).astype(
+        tokens[rows, :] = (grad_res[rows, :].astype(jnp.float32) + grads).astype(
             jnp.bfloat16
         )
 
-    loads.wait(*range(3, len(LOADED)))
-
-    def sequence_turn(turn_, carry):
+    qkv_t[pl.ds(0, 2 * pair), :] = ref["w_query"][...].T
+    qkv_t[pl.ds(2 * pair, pair), :] = ref["w_key"][...].T
+    qkv_t[pl.ds(3 * pair, pair), :] = ref["w_value"][...].T
+    ffn_sum.cross(sequences - 1)
+
+    def grad_turn(turn_, carry):
         @pl.when(turn_ + 1 < sequences)
         def _():
             prepare(turn_ + 1)
-
-            def aside(index, carry):
-                send_aside(levels - 1 - index, turn_ + 1)
-                return carry
-
-            lax.fori_loop(0, levels, aside, 0)
+            find_grads(turn_ + 1)
+
+        @pl.when((turn_ == 0) | (turn_ == 1))
+        def _():
+            ffn_sum.close(sequences - 2 + turn_)
 
         @pl.when((turn_ >= 0) & (turn_ < sequences))
         def _():
@@ -1335,11 +1141,10 @@
                 return carry
 
             lax.fori_loop(0, levels - 1, down, 0)
-            rows = rows_of(turn_)
-            own_grads[rows, :] = grads_of(me, turn_, True)
-            mlp_sum.offer(turn_, dot_nt(ffn_grads[0, rows], ref["w_down"][...]))
-
-        ffn_tick(turn_ + 7)
+            mlp_sum.offer(turn_, dot_nt(ffn_grads[0, rows_of(turn_)], w_down[...]))
+
+        for i in range(TURN_TICKS):
+            ffn_tick(3 + TURN_TICKS * (turn_ + 1) + i)
 
         @pl.when((turn_ >= 1) & (turn_ <= sequences))
         def _():
@@ -1366,18 +1171,19 @@
         return carry
 
     turns = sequences + 3
-    lax.fori_loop(-1, turns - 1, sequence_turn, 0)
+    lax.fori_loop(-1, turns - 1, grad_turn, 0)
     qkv.tick(0, 0, normed_t, grad_qkv, first=True)
     gains.start()
     wt_sum.cross(sequences - 1)
     output_rows(sequences - 1)
     stores.start(0)
-    left_over = 3 * count - 6 - turns
+    done = 3 + TURN_TICKS * turns
+    left_over = 3 * count - done
     each = -(-left_over // (last - 1))
 
     def tail(step, carry):
         for i in range(each):
-            index = 6 + turns + each * (step - 1) + i
+            index = done + each * (step - 1) + i
 
             @pl.when(index < 3 * count)
             def _():
@@ -1415,29 +1221,47 @@
     stores.start(1, 2, 3, 4, 5)
     qkv.tick(0, last, normed_t, grad_qkv, result=qkv_total)
     stores.start(6, 7, 8)
+    ffn_sum.finish(sequences, (0,))
     wt_sum.finish(sequences)
     mlp_sum.finish(sequences)
     for i in range(3):
         ffn.finish(i, last)
     out.finish(0, last)
     qkv.finish(0, last)
+    for hop in range(3):
+        out_copy(hop).wait_send()
+
+        def sent(seq, carry):
+            head_copy(hop, seq).wait_send()
+            return carry
+
+        lax.fori_loop(0, sequences, sent, 0)
+
+    def each_seq(step):
+        def one(seq, carry):
+            step(seq)
+            return carry
+
+        lax.fori_loop(0, sequences, one, 0)
 
     def drain(step, carry):
-        @pl.when(block_there(step))
-        def _():
-            def sent(seq, carry):
-                side_copy(step, seq).wait_send()
-                return carry
-
-            lax.fori_loop(0, sequences, sent, 0)
+        @pl.when(goes_up(step))
+        def _():
+            seg_copy(step, 0).wait_send()
+            each_seq(lambda seq: up_copy(step, seq).wait_send())
+
+        @pl.when(goes_aside(step))
+        def _():
+            seg_copy(step, 1).wait_send()
+            each_seq(lambda seq: side_copy(step, seq).wait_send())
+
+        @pl.when(comes_aside(step))
+        def _():
+            each_seq(lambda seq: side_grad_copy(step, seq).wait_send())
 
         @pl.when((step > 0) & (me >= 2 * step))
         def _():
-            def sent(seq, carry):
-                line_copy(step, seq).wait_send()
-                return carry
-
-            lax.fori_loop(0, sequences, sent, 0)
+            each_seq(lambda seq: line_copy(step, seq).wait_send())
 
         return carry
 
@@ -1445,12 +1269,12 @@
     stores.wait(*range(len(RESULTS)))
 
 
-def backward(inputs):
+def layer(inputs):
     count = lax.axis_size("ctx")
-    sequences, tile = inputs["mixed_t_in"].shape[0], inputs["mixed_t_in"].shape[3]
+    sequences, tile = inputs["segments"].shape
     rows, width = inputs["tokens_in"].shape
     head_dim = inputs["q_gain"].shape[0]
-    hidden = inputs["ffn_grads_in"].shape[2]
+    hidden = inputs["w_gate_in"].shape[1]
     pair = 2 * head_dim
     levels = count // 2
     block = width // count
@@ -1471,42 +1295,85 @@
         "q_gain_sum": ((1, pair), f32),
         "k_gain_sum": ((1, pair), f32),
     }
-    staged = ("output", "tokens_grad", "w_out_sum") + RESULTS[9:]
+    staged = ("w_out_sum",) + RESULTS[9:]
     scratch = {name: pltpu.VMEM(*results[name]) for name in staged}
-    for name in LOADED:
-        kind = inputs[name + "_in"]
-        shape = (tile, kind.shape[1]) if name == "table" else kind.shape
-        scratch[name] = pltpu.VMEM(shape, kind.dtype)
-    scratch |= {
-        "grad_res_t": pltpu.VMEM((width, rows), bf16),
-        "grad_heads_t": pltpu.VMEM((sequences, pair, 4 * tile), bf16),
-        "deltas": pltpu.VMEM((sequences, 1, 4 * tile), f32),
-        "grad_query_t": pltpu.VMEM((sequences, 2, head_dim, 2 * tile), f32),
-        "own_grads": pltpu.VMEM((rows, 2 * pair), f32),
-        "grad_qkv": pltpu.VMEM((rows, 4 * pair), bf16),
-        "side_in": pltpu.VMEM((levels, rows, 2 * pair), bf16),
-        "side_out": pltpu.VMEM((levels, rows, 2 * pair), bf16),
-        "line_in": pltpu.VMEM((levels - 1, rows, 2 * pair), bf16),
-        "line_out": pltpu.VMEM((levels - 1, rows, 2 * pair), bf16),
-        "ffn_sums": pltpu.VMEM((3, block, hidden), f32),
-        "qkv_total": pltpu.VMEM((block, 4 * pair), f32),
-        "side_send": dma((levels, sequences)),
-        "side_recv": dma((levels, sequences)),
-        "line_send": dma((levels - 1, sequences)),
-        "line_recv": dma((levels - 1, sequences)),
-        "load_sems": dma((len(LOADED),)),
-        "store_sems": dma((len(RESULTS),)),
-        "gains0": pltpu.VMEM((count, 8, width), f32),
-        "gains1": pltpu.VMEM((2, 2, 8, width), f32),
-        "gains2": dma((count - 1,)),
-        "gains3": dma((count - 1,)),
-        "gains4": dma((2,)),
-        "gains5": dma((2,)),
+    buffers = {
+        "tokens": ((rows, width), bf16),
+        "residual": ((rows, width), f32),
+        "mixed_t": ((sequences, 2, pair, tile), f32),
+        "query_t": ((sequences, pair, 4 * tile), bf16),
+        "logs": ((sequences, 1, 4 * tile), f32),
+        "starts": ((sequences, 1, tile), f32),
+        "keys_values": ((count, rows, 2 * pair), bf16),
+        "query_raw": ((rows, 2 * pair), f32),
+        "key_raw": ((rows, pair), f32),
+        "lefts": ((2, width, rows), bf16),
+        "ffn_grads": ((3, rows, hidden), bf16),
+        "ffn_gain_part": ((1, width), f32),
+        "grad_res": ((rows, width), bf16),
+        "all_segs": ((count, 8, tile), jnp.int32),
+        "all_out": ((4, 2 * pair, width), bf16),
+        "all_heads": ((4, rows, 2 * pair), bf16),
+        "acc": ((sequences, 2, head_dim, 2 * tile), f32),
+        "row_sum": ((sequences, 1, 4 * tile), f32),
+        "table": ((tile, 2 * pair), f32),
+        "cotangent": ((rows, width), bf16),
+        "w_down": ((width, hidden), bf16),
+        "w_gate": ((width, hidden), bf16),
+        "w_up": ((width, hidden), bf16),
+        "gate_t": ((hidden, width), bf16),
+        "up_t": ((hidden, width), bf16),
+        "grad_hidden": ((rows, hidden), bf16),
+        "ffn_part": ((rows, width), bf16),
+        "sum_got": ((rows, width // 2), bf16),
+        "sum_far": ((rows, width // 2), bf16),
+        "sum_full": ((2, rows, width // 2), bf16),
+        "mlp_sum0": ((rows, width // 2), bf16),
+        "mlp_sum1": ((rows, width // 2), bf16),
+        "mlp_sum2": ((2, rows, width // 2), bf16),
+        "deltas": ((sequences, 1, 4 * tile), f32),
+        "own_grads": ((rows, 2 * pair), f32),
+        "side_in": ((levels, rows, 2 * pair), bf16),
+        "side_out": ((levels, rows, 2 * pair), bf16),
+        "line_in": ((levels - 1, rows, 2 * pair), bf16),
+        "line_out": ((levels - 1, rows, 2 * pair), bf16),
+        "ffn_sums": ((3, block, hidden), f32),
+        "qkv_total": ((block, 4 * pair), f32),
+        "gains0": ((count, 8, width), f32),
+        "gains1": ((2, 2, 8, width), f32),
     }
+    scratch |= {name: pltpu.VMEM(*spec) for name, spec in buffers.items()}
+    semaphores = {
+        "load_sems": (6,),
+        "store_sems": (len(RESULTS),),
+        "up_send": (levels, sequences),
+        "up_recv": (levels, sequences),
+        "side_send": (levels, sequences),
+        "side_recv": (levels, sequences),
+        "seg_send": (levels, 2),
+        "seg_recv": (levels, 2),
+        "out_send": (3,),
+        "out_recv": (3,),
+        "head_send": (3, sequences),
+        "head_recv": (3, sequences),
+        "ffn_send": (3, sequences),
+        "ffn_recv": (3, sequences),
+        "wt_send": (3, sequences),
+        "wt_recv": (3, sequences),
+        "mlp_sum3": (3, sequences),
+        "mlp_sum4": (3, sequences),
+        "side_grad_send": (levels, sequences),
+        "side_grad_recv": (levels, sequences),
+        "line_send": (levels - 1, sequences),
+        "line_recv": (levels - 1, sequences),
+        "gains2": (count - 1,),
+        "gains3": (count - 1,),
+        "gains4": (2,),
+        "gains5": (2,),
+    }
+    scratch |= {name: dma(shape) for name, shape in semaphores.items()}
     for label, kinds in (
-        ("wt_sum", wt_sum_scratch(sequences, rows, width)),
-        ("mlp_sum", wt_sum_scratch(sequences, rows, width)),
-        ("ffn", ring_scratch(count - 1, 3, block, hidden)),
+        ("ffn", ring_scratch(count, 3, block, hidden)),
         ("out", ring_scratch(count, 1, block, 2 * pair)),
         ("qkv", ring_scratch(count, 1, block, 4 * pair)),
     ):
@@ -1514,31 +1381,39 @@
     vmem, anywhere = pl.BlockSpec(memory_space=pltpu.VMEM), pl.BlockSpec(memory_space=pl.ANY)
     names = (*inputs, *(name + "_res" for name in RESULTS), *scratch)
     arrays = pl.pallas_call(
-        partial(backward_kernel, count, names),
+        partial(layer_kernel, count, names),
         out_shape=[jax.ShapeDtypeStruct(*results[name]) for name in RESULTS],
         in_specs=[anywhere if name.endswith("_in") else vmem for name in inputs],
         out_specs=[anywhere] * len(RESULTS),
         scratch_shapes=list(scratch.values()),
         compiler_params=pltpu.CompilerParams(
-            collective_id=3, has_side_effects=True, vmem_limit_bytes=62 * MIB
+            collective_id=2, has_side_effects=True, vmem_limit_bytes=VMEM_LIMIT
         ),
     )(*inputs.values())
     return dict(zip(RESULTS, arrays, strict=True))
 
 
 def hand_over_kernel(count, *refs):
-    for source, target in zip(refs[:count], refs[count:], strict=True):
-        target[...] = source[...]
+    sources, targets, staged = refs[:count], refs[count : 2 * count], refs[2 * count : 3 * count]
+    loads = Mover(list(zip(sources, staged, strict=True)), refs[3 * count])
+    stores = Mover(list(zip(staged, targets, strict=True)), refs[3 * count + 1])
+    loads.start(*range(count))
+    for i in range(count):
+        loads.wait(i)
+        stores.start(i)
+    stores.wait(*range(count))
 
 
 def hand_over(arrays):
-    vmem = pl.BlockSpec(memory_space=pltpu.VMEM)
+    anywhere = pl.BlockSpec(memory_space=pl.ANY)
+    dma = pltpu.SemaphoreType.DMA((len(arrays),))
     return pl.pallas_call(
         partial(hand_over_kernel, len(arrays)),
         out_shape=[jax.ShapeDtypeStruct(array.shape, array.dtype) for array in arrays],
-        in_specs=[vmem] * len(arrays),
-        out_specs=[vmem] * len(arrays),
-        compiler_params=pltpu.CompilerParams(vmem_limit_bytes=32 * MIB),
+        in_specs=[anywhere] * len(arrays),
+        out_specs=[anywhere] * len(arrays),
+        scratch_shapes=[pltpu.VMEM(array.shape, array.dtype) for array in arrays] + [dma, dma],
+        compiler_params=pltpu.CompilerParams(vmem_limit_bytes=60 * MIB),
     )(*arrays)
 
 
@@ -1550,7 +1425,7 @@
     return np.concatenate([cosine] * 4 + [-sine, sine] * 2, axis=1).astype(np.float32)
 
 
-def kernels_fit(tokens, w_query, key_matrix, q_gain):
+def kernels_fit(tokens, w_query, key_matrix, q_gain, w_gate):
     sequences, tile, width = tokens.shape
     count, head_dim = lax.axis_size("ctx"), q_gain.shape[0]
     return (
@@ -1564,6 +1439,9 @@
         and w_query.shape[1] == 4 * head_dim
         and key_matrix.shape[1] == 2 * head_dim
         and width % (128 * count) == 0
+        and w_gate.shape[1] >= max(width, sequences * tile + 512)
+        and w_gate.shape[1] <= 1152
+        and width <= 1024
     )
 
 
@@ -1775,7 +1653,7 @@
     w_down,
     cotangent,
 ):
-    if not kernels_fit(tokens, w_query, key_matrix, q_gain):
+    if not kernels_fit(tokens, w_query, key_matrix, q_gain, w_gate):
         return on_device_plain(
             tokens,
             segments,
@@ -1797,9 +1675,8 @@
     token_rows = tokens.reshape(sequences * seq_rows, model_width)
     table = jnp.asarray(rotary_table(count * seq_rows, head_dim))
     gains = {"attn_gain": attn_gain, "q_gain": q_gain, "k_gain": k_gain}
-    kept = forward(
+    sums = layer(
         {
-            "tokens": token_rows,
             "segments": segments,
             **gains,
             "ffn_gain": ffn_gain,
@@ -1807,26 +1684,12 @@
             "w_key": key_matrix,
             "w_value": value_matrix,
             "w_out": w_out,
+            "tokens_in": token_rows,
             "table_in": table,
             "cotangent_in": cotangent.reshape(token_rows.shape),
             "w_down_in": w_down,
             "w_gate_in": w_gate,
             "w_up_in": w_up,
-        }
-    )
-    ffn_gain_part = kept.pop("ffn_gain_part")
-    sums = backward(
-        {
-            **gains,
-            "ffn_gain_part": ffn_gain_part,
-            **{name + "_in": array for name, array in kept.items()},
-            "tokens_in": token_rows,
-            "table_in": table,
-            "w_query_in": w_query,
-            "w_key_in": key_matrix,
-            "w_value_in": value_matrix,
-            "w_out_in": w_out,
-            "w_down_in": w_down,
         }
     )
     done = dict(zip(RESULTS, hand_over([sums[name] for name in RESULTS]), strict=True))

time: 207 us -> 189 us (0.913)
  local copies, waits for them, and re-layouts: 12.4 us -> 1.18 us
  Pallas kernels: 193 us -> 187 us
    unnamed x26 -> x0, local copies, waits for them, and re-layouts: 11.9 us -> none
    pallas_call x2 -> x1, Pallas kernels: 190 us -> 183 us  [layer(): pl.pallas_call(partial(layer_kernel, count, names), out_shape=[jax.ShapeD...]
where the time goes in v6:
time: 189 us
  Pallas kernels  187 us (99%)
    pallas_call x1, Pallas kernels, layer(): pl.pallas_call(partial(layer_kernel, count, names), out_shape=[jax.ShapeD...  183 us

profile of v6, /device:TPU:0, one launch (start us, length us, event | category | flops | bytes accessed | tf_op | source)
XLA Modules:
  0.0 189.1 jit_solution(5339557525486118421)
XLA Ops:
  0.7 183.5 %shard_map.246 = (bf16[640,1024]{1,0:T(8,128)(2,1)}, bf16[640,1024]{1,0:T(8,128)(2,1)}, f32[128,1152]{1,0:T(8,128)}, f32[128,1152]{1,0:T(8,128)}, f32[128,1152]{...) custom-call(s32[5,128]{1,0:T(8,128)} %refs_0_.1, ...), custom_call_target="tpu_custom_call" | custom-call | tf_op jit(solution)/shard_map/pallas_call | solution.py:1383
  184.1 3.7 %shard_map.247 = (bf16[640,1024]{1,0:T(8,128)(2,1)}, bf16[640,1024]{1,0:T(8,128)(2,1)}, f32[128,1152]{1,0:T(8,128)}, f32[128,1152]{1,0:T(8,128)}, f32[128,1152]{...) custom-call(bf16[640,1024]{1,0:T(8,128)(2,1)} %get-tuple-element.39., ...), custom_call_target="tpu_custom_call" | custom-call | tf_op jit(solution)/shard_map/pallas_call | solution.py:1410
  187.9 1.2 slice_bitcast_fusion

commit v7 on v6

--- a/solution.py
+++ b/solution.py
@@ -337,6 +337,7 @@
         self.far_wt = lax.rem(self.core_wt + 2, 4)
         self.core = (self.ctx, self.core_wt)
         self.chip = (self.ctx, self.chip_wt)
+        self.far = (self.ctx, self.far_wt)
 
     def signal(self, peer):
         pl.semaphore_signal(
@@ -348,9 +349,10 @@
             self.signal((lax.rem(self.ctx + shift, self.count), self.wt))
         self.signal(self.core)
         self.signal(self.chip)
+        self.signal(self.far)
 
     def await_all(self):
-        pl.semaphore_wait(pltpu.get_barrier_semaphore(), self.count + 1)
+        pl.semaphore_wait(pltpu.get_barrier_semaphore(), self.count + 2)
 
 
 def send_to(source, target, send_sem, recv_sem, device):
@@ -501,7 +503,8 @@
             self.copies[i].wait()
 
 
-TURN_TICKS = 1
+TICKS = (1, 1, 5)
+REACH = 2
 VMEM_LIMIT = 63 * MIB
 RESULTS = (
     "output",
@@ -572,11 +575,12 @@
     def block_of(index, step):
         return lax.rem(index - 2 * step + 2 * count, count)
 
-    def up_copy(step, seq, sems=None):
-        rows = keys_values.at[block_of(me, step), rows_of(seq)]
-        index = step if sems is None else sems
+    def up_copy(step, seq, arriving=False, forward=False):
+        block = block_of(me, step) if arriving else block_of(me, step - 1) if forward else me
+        rows = keys_values.at[block, rows_of(seq)]
+        device = (lax.rem(me + (2 if forward else 2 * step), count), here.wt)
         return send_to(
-            rows, rows, ref["up_send"].at[index, seq], ref["up_recv"].at[index, seq], here.above
+            rows, rows, ref["up_send"].at[step, seq], ref["up_recv"].at[step, seq], device
         )
 
     def side_copy(step, seq, index=me):
@@ -585,16 +589,21 @@
             rows, rows, ref["side_send"].at[step, seq], ref["side_recv"].at[step, seq], here.beside
         )
 
-    def seg_copy(step, way, index=me, sems=None):
+    def seg_up_copy(step, arriving=False):
+        part = all_segs.at[block_of(me, step) if arriving else me]
+        device = (lax.rem(me + 2 * step, count), here.wt)
+        return send_to(
+            part, part, ref["seg_send"].at[step, 0], ref["seg_recv"].at[step, 0], device
+        )
+
+    def seg_side_copy(step, index=me):
         part = all_segs.at[block_of(index, step)]
-        device = here.beside if way else here.above
-        at = step if sems is None else sems
         return send_to(
-            part, part, ref["seg_send"].at[at, way], ref["seg_recv"].at[at, way], device
+            part, part, ref["seg_send"].at[step, 1], ref["seg_recv"].at[step, 1], here.beside
         )
 
     def goes_up(step):
-        return here.has_above & (me >= 2 * step)
+        return me + 2 * step < count
 
     def goes_aside(step):
         block = me - 2 * step
@@ -604,23 +613,30 @@
         block = here.beside_ctx - 2 * step
         return (block >= 0) & (block < me)
 
-    def pass_segs(step):
-        @pl.when(goes_up(step))
-        def _():
-            seg_copy(step, 0).start()
-
-        @pl.when(goes_aside(step))
-        def _():
-            seg_copy(step, 1).start()
-
-    def pass_rows(step, seq):
-        @pl.when(goes_up(step))
-        def _():
-            up_copy(step, seq).start()
-
-        @pl.when(goes_aside(step))
-        def _():
-            side_copy(step, seq).start()
+    def pass_segs():
+        for step in range(1, levels):
+
+            @pl.when(goes_up(step))
+            def _():
+                seg_up_copy(step).start()
+
+        @pl.when(goes_aside(0))
+        def _():
+            seg_side_copy(0).start()
+
+    def forwards(step):
+        return (step > REACH) & (me >= 2 * (step - 1)) & here.has_above
+
+    def pass_rows(seq):
+        @pl.when(goes_aside(0))
+        def _():
+            side_copy(0, seq).start()
+
+        for step in range(1, min(REACH + 1, levels)):
+
+            @pl.when(goes_up(step))
+            def _():
+                up_copy(step, seq).start()
 
     gain = as_row(ref["attn_gain"])
     q_gain_pair = double(as_row(ref["q_gain"]))
@@ -649,11 +665,11 @@
         @pl.when(seq == 0)
         def _():
             here.await_all()
-            pass_segs(0)
-
-        @pl.when(seq < 2)
-        def _():
-            pass_rows(0, seq)
+            pass_segs()
+
+        @pl.when(seq == 0)
+        def _():
+            pass_rows(seq)
 
         @pl.when(seq == 0)
         def _():
@@ -678,7 +694,32 @@
         starts[seq] = jnp.zeros_like(starts[seq])
         return carry
 
+    def route_level(step, seq):
+        @pl.when(me >= 2 * step)
+        def _():
+            @pl.when(seq == 0)
+            def _():
+                seg_up_copy(step, True).wait_recv()
+                seg_side_copy(step).start()
+
+            up_copy(step, seq, True).wait_recv()
+            side_copy(step, seq).start()
+
+            @pl.when(forwards(step + 1))
+            def _():
+                up_copy(step + 1, seq, forward=True).start()
+
+    def route(seq):
+        def level(step, carry):
+            route_level(step, seq)
+            return carry
+
+        lax.fori_loop(1, levels, level, 0)
+
     lax.fori_loop(0, sequences, project, 0)
+    pass_rows(1)
+    for step in range(1, min(REACH + 1, levels)):
+        route_level(step, 0)
     loads.wait(1, 2)
 
     def back_down(seq, carry):
@@ -689,24 +730,9 @@
         return carry
 
     lax.fori_loop(0, sequences, back_down, 0)
-
-    def route(seq):
-        def level(step, carry):
-            @pl.when(me >= 2 * step)
-            def _():
-                @pl.when(seq == 0)
-                def _():
-                    seg_copy(step, 0, me, step - 1).wait_recv()
-                    pass_segs(step)
-
-                up_copy(step, seq, step - 1).wait_recv()
-                pass_rows(step, seq)
-
-            return carry
-
-        lax.fori_loop(1, levels, level, 0)
-
-    route(0)
+    for step in range(REACH + 1, levels):
+        route_level(step, 0)
+
     loads.wait(3, 4)
 
     def flip(index, carry):
@@ -746,6 +772,12 @@
                 low[:, group * 2 * tile : (group + 1) * 2 * tile],
             )
 
+    def attend_own(seq, carry):
+        attend([me], seq)
+        return carry
+
+    lax.fori_loop(0, sequences, attend_own, 0)
+
     def head_copy(hop, seq, arriving=False):
         sent = (here.wt, here.wt, here.chip_wt)
         landed = (here.chip_wt, here.core_wt, here.far_wt)
@@ -755,9 +787,18 @@
             part, part, ref["head_send"].at[hop, seq], ref["head_recv"].at[hop, seq], device
         )
 
+    def far_copy(seq):
+        part = all_heads.at[here.wt, rows_of(seq)]
+        return send_to(
+            part, part, ref["head_send"].at[2, seq], ref["head_recv"].at[2, seq], here.far
+        )
+
     def relay(seq):
         head_copy(0, seq, True).wait_recv()
-        head_copy(2, seq).start()
+
+        @pl.when(seq < sequences - 1)
+        def _():
+            head_copy(2, seq).start()
 
     def mix(seq):
         rows = rows_of(seq)
@@ -771,6 +812,10 @@
             all_heads[here.wt, rows, pl.ds(group * pair, pair)] = mixed.T.astype(jnp.bfloat16)
         head_copy(0, seq).start()
         head_copy(1, seq).start()
+
+        @pl.when(seq == sequences - 1)
+        def _():
+            far_copy(seq).start()
 
     def ffn_unit(rows):
         values = residual[rows, :]
@@ -809,31 +854,28 @@
         def _():
             @pl.when(turn_ + 2 < sequences)
             def _():
-                pass_rows(0, turn_ + 2)
+                pass_rows(turn_ + 2)
 
             @pl.when(comes_aside(0))
             def _():
                 @pl.when(turn_ == 0)
                 def _():
-                    seg_copy(0, 1, here.beside_ctx).wait_recv()
+                    seg_side_copy(0, here.beside_ctx).wait_recv()
 
                 side_copy(0, turn_, here.beside_ctx).wait_recv()
-                attend([me, here.beside_ctx], turn_)
-
-            @pl.when(jnp.logical_not(comes_aside(0)))
-            def _():
-                attend([me], turn_)
+                attend([here.beside_ctx], turn_)
 
         @pl.when(turn_ + 1 < sequences)
         def _():
-            route(turn_ + 1)
+            for step in range(1, min(REACH + 1, levels)):
+                route_level(step, turn_ + 1)
 
         @pl.when(turn_ == 1)
         def _():
             out_copy(0, True).wait_recv()
             out_copy(2).start()
 
-        @pl.when(turn_ > 0)
+        @pl.when((turn_ > 0) & (turn_ <= sequences))
         def _():
             relay(turn_ - 1)
 
@@ -844,7 +886,7 @@
                 def _():
                     @pl.when(turn_ == 0)
                     def _():
-                        seg_copy(step, 1, here.beside_ctx).wait_recv()
+                        seg_side_copy(step, here.beside_ctx).wait_recv()
 
                     side_copy(step, turn_, here.beside_ctx).wait_recv()
                     attend([block_of(me, step), block_of(here.beside_ctx, step)], turn_)
@@ -853,6 +895,11 @@
 
             lax.fori_loop(1, levels, level, 0)
             mix(turn_)
+
+        @pl.when(turn_ + 1 < sequences)
+        def _():
+            for step in range(REACH + 1, levels):
+                route_level(step, turn_ + 1)
 
         @pl.when(turn_ == 1)
         def _():
@@ -1124,62 +1171,74 @@
     qkv_t[pl.ds(3 * pair, pair), :] = ref["w_value"][...].T
     ffn_sum.cross(sequences - 1)
 
+    few, more, early = TICKS
+
+    def ticks_before(turn_):
+        return 3 + few * lax.min(turn_, early) + more * lax.max(turn_ - early, 0)
+
     def grad_turn(turn_, carry):
-        @pl.when(turn_ + 1 < sequences)
-        def _():
-            prepare(turn_ + 1)
-            find_grads(turn_ + 1)
-
-        @pl.when((turn_ == 0) | (turn_ == 1))
-        def _():
-            ffn_sum.close(sequences - 2 + turn_)
-
-        @pl.when((turn_ >= 0) & (turn_ < sequences))
+        @pl.when(turn_ < sequences)
+        def _():
+            prepare(turn_)
+            find_grads(turn_)
+
+        @pl.when((turn_ == 1) | (turn_ == 2))
+        def _():
+            ffn_sum.close(sequences - 3 + turn_)
+
+        @pl.when((turn_ >= 2) & (turn_ < sequences + 2))
         def _():
             def down(index, carry):
-                send_down(levels - 1 - index, turn_)
+                send_down(levels - 1 - index, turn_ - 2)
                 return carry
 
             lax.fori_loop(0, levels - 1, down, 0)
-            mlp_sum.offer(turn_, dot_nt(ffn_grads[0, rows_of(turn_)], w_down[...]))
-
-        for i in range(TURN_TICKS):
-            ffn_tick(3 + TURN_TICKS * (turn_ + 1) + i)
+
+        for i in range(max(few, more)):
+
+            @pl.when(ticks_before(turn_) + i < ticks_before(turn_ + 1))
+            def _():
+                ffn_tick(ticks_before(turn_) + i)
 
         @pl.when((turn_ >= 1) & (turn_ <= sequences))
         def _():
-            mlp_sum.cross(turn_ - 1)
-
-        @pl.when(turn_ == sequences)
-        def _():
-            out.tick(0, 0, grad_res_t, heads, first=True)
-
-        @pl.when(turn_ == sequences + 1)
-        def _():
-            out.tick(0, 1, grad_res_t, heads)
-
-        @pl.when(turn_ >= 2)
-        def _():
-            project_back(turn_ - 2)
-            mlp_sum.close(turn_ - 2)
-
-        @pl.when(turn_ >= 3)
-        def _():
-            wt_sum.cross(turn_ - 3)
-            output_rows(turn_ - 3)
+            seq = turn_ - 1
+            mlp_sum.offer(seq, dot_nt(ffn_grads[0, rows_of(seq)], w_down[...]))
+
+        @pl.when((turn_ >= 2) & (turn_ <= sequences + 1))
+        def _():
+            mlp_sum.cross(turn_ - 2)
+
+        @pl.when((turn_ >= 3) & (turn_ <= sequences + 2))
+        def _():
+            mlp_sum.close(turn_ - 3)
+
+        @pl.when(turn_ >= 4)
+        def _():
+            output_rows(turn_ - 4)
+            project_back(turn_ - 4)
+
+        @pl.when(turn_ >= 5)
+        def _():
+            wt_sum.cross(turn_ - 5)
+
+        for i in range(4):
+
+            @pl.when(turn_ == sequences + i)
+            def _():
+                out.tick(0, i, grad_res_t, heads, first=i == 0)
 
         return carry
 
-    turns = sequences + 3
-    lax.fori_loop(-1, turns - 1, grad_turn, 0)
+    turns = sequences + 4
+    lax.fori_loop(0, turns, grad_turn, 0)
     qkv.tick(0, 0, normed_t, grad_qkv, first=True)
     gains.start()
     wt_sum.cross(sequences - 1)
-    output_rows(sequences - 1)
     stores.start(0)
-    done = 3 + TURN_TICKS * turns
+    done = 3 + few * early + more * (turns - early)
     left_over = 3 * count - done
-    each = -(-left_over // (last - 1))
+    each = -(-left_over // last)
 
     def tail(step, carry):
         for i in range(each):
@@ -1189,12 +1248,12 @@
             def _():
                 ffn_tick(index)
 
-        qkv.tick(0, step, normed_t, grad_qkv)
-
-        @pl.when(step < last)
+        qkv.tick(0, step, normed_t, grad_qkv, result=qkv_total, final=step == last)
+
+        @pl.when(step + 3 <= last)
         def _():
             out.tick(
-                0, step + 1, grad_res_t, heads, result=ref["w_out_sum"], final=step + 1 == last
+                0, step + 3, grad_res_t, heads, result=ref["w_out_sum"], final=step + 3 == last
             )
 
         @pl.when(step <= sequences)
@@ -1217,10 +1276,8 @@
     ref["q_gain_sum"][...] = folded[2:3]
     ref["k_gain_sum"][...] = folded[3:4]
     stores.start(9, 10, 11, 12)
-    lax.fori_loop(middle, last, tail, 0)
-    stores.start(1, 2, 3, 4, 5)
-    qkv.tick(0, last, normed_t, grad_qkv, result=qkv_total)
-    stores.start(6, 7, 8)
+    lax.fori_loop(middle, last + 1, tail, 0)
+    stores.start(1, 2, 3, 4, 5, 6, 7, 8)
     ffn_sum.finish(sequences, (0,))
     wt_sum.finish(sequences)
     mlp_sum.finish(sequences)
@@ -1245,14 +1302,17 @@
         lax.fori_loop(0, sequences, one, 0)
 
     def drain(step, carry):
-        @pl.when(goes_up(step))
-        def _():
-            seg_copy(step, 0).wait_send()
+        @pl.when((step > 0) & goes_up(step))
+        def _():
+            seg_up_copy(step).wait_send()
+
+        @pl.when(((step > 0) & (step <= REACH) & goes_up(step)) | forwards(step))
+        def _():
             each_seq(lambda seq: up_copy(step, seq).wait_send())
 
         @pl.when(goes_aside(step))
         def _():
-            seg_copy(step, 1).wait_send()
+            seg_side_copy(step).wait_send()
             each_seq(lambda seq: side_copy(step, seq).wait_send())
 
         @pl.when(comes_aside(step))

time: 189 us -> 181 us (0.958)
  Pallas kernels: 187 us -> 179 us
    pallas_call x1, Pallas kernels: 183 us -> 175 us  [layer(): pl.pallas_call(partial(layer_kernel, count, names), out_shape=[jax.ShapeD...]
where the time goes in v7:
time: 181 us
  Pallas kernels  179 us (99%)
    pallas_call x1, Pallas kernels, layer(): pl.pallas_call(partial(layer_kernel, count, names), out_shape=[jax.ShapeD...  175 us
    pallas_call x1, Pallas kernels, hand_over(): pl.pallas_call(partial(hand_over_kernel, len(arrays)), out_shape=[jax.Sha...  3.74 us

profile of v7, /device:TPU:0, one launch (start us, length us, event | category | flops | bytes accessed | tf_op | source)
XLA Modules:
  0.0 180.7 jit_solution(10388644223853523849)
XLA Ops:
  0.7 175.1 %shard_map.246 = (bf16[640,1024]{1,0:T(8,128)(2,1)}, bf16[640,1024]{1,0:T(8,128)(2,1)}, f32[128,1152]{1,0:T(8,128)}, f32[128,1152]{1,0:T(8,128)}, f32[128,1152]{...) custom-call(s32[5,128]{1,0:T(8,128)} %refs_0_.1, ...), custom_call_target="tpu_custom_call" | custom-call | tf_op jit(solution)/shard_map/pallas_call | solution.py:1443
  175.7 3.7 %shard_map.247 = (bf16[640,1024]{1,0:T(8,128)(2,1)}, bf16[640,1024]{1,0:T(8,128)(2,1)}, f32[128,1152]{1,0:T(8,128)}, f32[128,1152]{1,0:T(8,128)}, f32[128,1152]{...) custom-call(bf16[640,1024]{1,0:T(8,128)(2,1)} %get-tuple-element.39., ...), custom_call_target="tpu_custom_call" | custom-call | tf_op jit(solution)/shard_map/pallas_call | solution.py:1470
  179.5 1.2 slice_bitcast_fusion

commit v8 on v7

--- a/solution.py
+++ b/solution.py
@@ -331,6 +331,8 @@
         self.above = (lax.rem(self.ctx + 2, count), self.wt)
         self.below = (lax.rem(self.ctx + count - 2, count), self.wt)
         self.has_above = self.ctx + 2 < count
+        self.top = self.ctx >= count - 2
+        self.serves = (self.ctx >= count - 4) & (self.ctx < count - 2)
         self.has_below = self.ctx >= 2
         self.core_wt = self.wt + 1 - 2 * self.core_bit
         self.chip_wt = lax.rem(self.wt + 2, 4)
@@ -469,22 +471,29 @@
         for shift in range(1, self.here.count):
             self.copy(shift).start()
 
-    def total(self):
+    def sum_ctx(self):
         for shift in range(1, self.here.count):
             self.copy(shift, True).wait_recv()
         total = self.slots[0]
         for index in range(1, self.here.count):
             total = total + self.slots[index]
-        for hop in range(2):
-            self.beside[hop, 0] = total
-            self.pair_copy(hop).start()
-            self.pair_copy(hop).wait_recv()
-            total = total + self.beside[hop, 1]
+        self.beside[0, 0] = total
+        self.pair_copy(0).start()
+
+    def sum_cores(self):
+        self.pair_copy(0).wait_recv()
+        self.beside[1, 0] = self.beside[0, 0] + self.beside[0, 1]
+        self.pair_copy(1).start()
+
+    def sum_chips(self):
+        self.pair_copy(1).wait_recv()
+        return self.beside[1, 0] + self.beside[1, 1]
+
+    def finish(self):
         for shift in range(1, self.here.count):
             self.copy(shift).wait_send()
         for hop in range(2):
             self.pair_copy(hop).wait_send()
-        return total
 
 
 class Mover:
@@ -562,6 +571,15 @@
     all_segs[me, pl.ds(0, sequences)] = segments[...]
     all_out[here.wt] = ref["w_out"][...].T
 
+    rows_all, width = tokens.shape
+    grad_heads_t = w_gate
+
+    heads_small = gate_t.at[pl.ds(4 * tile, 2 * pair), pl.ds(2 * pair, sequences * tile)]
+
+    def heads_at(seq):
+        start = pl.multiple_of(seq * pair, pair)
+        return (pl.ds(start, pair), pl.ds(rows_all, 4 * tile))
+
     def out_copy(hop, arriving=False):
         sent = (here.wt, here.wt, here.chip_wt)
         landed = (here.chip_wt, here.core_wt, here.far_wt)
@@ -643,6 +661,22 @@
     k_gain_pair = double(as_row(ref["k_gain"]))
     ffn_gain_row = as_row(ref["ffn_gain"])
     loads.wait(0, 5)
+
+    def share_copy(what, seq):
+        source = (
+            query_t.at[seq],
+            ref["stats_out"].at[seq],
+            heads_small.at[:, pl.ds(pl.multiple_of(seq * tile, tile), tile)],
+            ref["deltas"].at[seq],
+        )[what]
+        target = (
+            ref["upper_query_t"],
+            ref["stats_in"],
+            ref["upper_heads"],
+            ref["upper_deltas"],
+        )[what].at[seq]
+        sems = ref["share_send"].at[what, seq], ref["share_recv"].at[what, seq]
+        return send_to(source, target, *sems, here.below)
 
     def turn(values):
         cosine = table[:, pl.ds(0, pair)]
@@ -689,6 +723,11 @@
                     pl.ds(group * head_dim, head_dim),
                     pl.ds((2 * group + member) * tile, tile),
                 ] = flipped[member * head_dim : (member + 1) * head_dim]
+
+        @pl.when(here.top)
+        def _():
+            share_copy(0, seq).start()
+
         acc[seq] = jnp.zeros_like(acc[seq])
         row_sum[seq] = jnp.zeros_like(row_sum[seq])
         starts[seq] = jnp.zeros_like(starts[seq])
@@ -813,6 +852,14 @@
         head_copy(0, seq).start()
         head_copy(1, seq).start()
 
+        @pl.when(here.top)
+        def _():
+            stats_out = ref["stats_out"]
+            stats_out[seq] = jnp.zeros_like(stats_out[seq])
+            stats_out[seq, pl.ds(0, 1)] = logs[seq]
+            stats_out[seq, pl.ds(1, 1), pl.ds(0, tile)] = starts[seq]
+            share_copy(1, seq).start()
+
         @pl.when(seq == sequences - 1)
         def _():
             far_copy(seq).start()
@@ -923,7 +970,6 @@
     lax.fori_loop(0, sequences + 1, sequence_turn, 0)
     for i in range(3):
         ffn.tick(i, 0, lefts.at[min(i, 1)], ffn_grads.at[i], first=True)
-    rows_all, width = tokens.shape
     last = count - 1
     deltas, own_grads = ref["deltas"], ref["own_grads"]
     side_in, side_out = ref["side_in"], ref["side_out"]
@@ -931,9 +977,11 @@
     ffn_sums, qkv_total = ref["ffn_sums"], ref["qkv_total"]
     grad_query_t = acc
     grad_res_t = w_gate.at[:, pl.ds(0, rows_all)]
-    grad_heads_t = w_gate
-    query_n = gate_t.at[pl.ds(0, 4 * tile)]
-    grad_heads_n = gate_t.at[pl.ds(4 * tile, 4 * tile)]
+    query_n = gate_t.at[pl.ds(0, 4 * tile), pl.ds(0, pair)]
+    grad_heads_n = gate_t.at[pl.ds(4 * tile, 4 * tile), pl.ds(0, pair)]
+    upper_query_n = gate_t.at[pl.ds(0, 4 * tile), pl.ds(pair, pair)]
+    upper_heads_t = gate_t.at[pl.ds(0, pair), pl.ds(2 * pair, 4 * tile)]
+    upper_heads_n = gate_t.at[pl.ds(4 * tile, 4 * tile), pl.ds(pair, pair)]
     grad_qkv = w_up.at[pl.ds(0, rows_all), pl.ds(0, 4 * pair)]
     normed_t = w_up.at[:, pl.ds(4 * pair, rows_all)]
     qkv_t = up_t.at[pl.ds(rows_all, 4 * pair)]
@@ -959,13 +1007,6 @@
     out = Ring(count, *(ref[f"out{i}"] for i in range(3)))
     qkv = Ring(count, *(ref[f"qkv{i}"] for i in range(3)))
 
-    def heads_at(seq):
-        start = pl.multiple_of(seq * pair, pair)
-        return (pl.ds(start, pair), pl.ds(rows_all, 4 * tile))
-
-    def seq_cols(seq):
-        return (slice(None), pl.ds(pl.multiple_of(seq * tile, tile), tile))
-
     def ffn_tick(index):
         step, which = lax.div(index, 3), lax.rem(index, 3)
         ffn.tick(
@@ -996,6 +1037,8 @@
         low = dot_nn(grads, ref["w_out"][...]).astype(jnp.bfloat16)
         for group in range(2):
             flipped = low[:, group * pair : (group + 1) * pair].T
+            small = pl.ds(pl.multiple_of(seq * tile, tile), tile)
+            heads_small[pl.ds(group * pair, pair), small] = flipped
             product_t = flipped.astype(jnp.float32) * mixed_t[seq, group]
             for member in range(2):
                 part = slice(member * head_dim, (member + 1) * head_dim)
@@ -1004,38 +1047,51 @@
                 spot = pl.ds(rows_all + (2 * group + member) * tile, tile)
                 grad_heads_t[into, spot] = flipped[part]
                 deltas[seq, :, cols] = jnp.sum(product_t[part], axis=0, keepdims=True)
-        grad_heads_n[seq_cols(seq)] = grad_heads_t[heads_at(seq)].T
-        query_n[seq_cols(seq)] = query_t[seq].T
         grad_query_t[seq] = jnp.zeros_like(grad_query_t[seq])
 
-    def grads_of(blocks, seq):
+        @pl.when(here.top)
+        def _():
+            share_copy(2, seq).start()
+            share_copy(3, seq).start()
+
+    def grads_of(blocks, seq, upper=False):
         rows = rows_of(seq)
         keys = [keys_values[block, rows, pl.ds(0, pair)] for block in blocks]
         values = [keys_values[block, rows, pl.ds(pair, pair)] for block in blocks]
+        if upper:
+            stats = ref["stats_in"]
+            log, start = stats[seq, pl.ds(0, 1)], stats[seq, pl.ds(1, 1), pl.ds(0, tile)]
+            delta = ref["upper_deltas"][seq]
+            queries, grad_heads = ref["upper_query_t"][seq], upper_heads_t[...]
+            query_rows, grad_rows = upper_query_n, upper_heads_n
+        else:
+            log, start, delta = logs[seq], starts[seq], deltas[seq]
+            queries, grad_heads = query_t[seq], grad_heads_t[heads_at(seq)]
+            query_rows, grad_rows = query_n, grad_heads_n
         masks = []
         for block in blocks:
-            allowed = key_rows.astype(jnp.float32) >= starts[seq] - (block * tile).astype(
-                jnp.float32
-            )
-            if block is me:
+            allowed = key_rows.astype(jnp.float32) >= start - (block * tile).astype(jnp.float32)
+            if block is me and not upper:
                 allowed = allowed & (key_rows <= query_cols)
             masks.append(jnp.where(allowed, 1.0, 0.0))
         mask = jnp.concatenate(masks, axis=0)
-        grad_heads = grad_heads_t[heads_at(seq)]
-        scores = dot_nn(jnp.concatenate(keys, axis=0), query_t[seq])
-        probs = jnp.exp(scores - logs[seq]) * jnp.concatenate([mask] * 4, axis=1)
+        scores = dot_nn(jnp.concatenate(keys, axis=0), queries)
+        probs = jnp.exp(scores - log) * jnp.concatenate([mask] * 4, axis=1)
         grad_probs = dot_nn(jnp.concatenate(values, axis=0), grad_heads)
-        grad_scores = (probs * (grad_probs - deltas[seq])).astype(jnp.bfloat16)
+        grad_scores = (probs * (grad_probs - delta)).astype(jnp.bfloat16)
         flipped = jnp.concatenate([part.T for part in keys], axis=1)
         for group in range(2):
             cols = slice(group * 2 * tile, (group + 1) * 2 * tile)
-            grad_query_t[seq, group] += dot_nn(
+            grads = dot_nn(
                 flipped[group * head_dim : (group + 1) * head_dim], grad_scores[:, cols]
             )
-        grad_keys = dot_nn(grad_scores, query_n[seq_cols(seq)])
-        grad_values = dot_nn(probs.astype(jnp.bfloat16), grad_heads_n[seq_cols(seq)])
-        both = jnp.concatenate([grad_keys, grad_values], axis=1)
-        return [both[i * tile : (i + 1) * tile] for i in range(len(blocks))]
+            if upper:
+                ref["upper_grad"][group] += grads
+            else:
+                grad_query_t[seq, group] += grads
+        grad_keys = dot_nn(grad_scores, query_rows[...])
+        grad_values = dot_nn(probs.astype(jnp.bfloat16), grad_rows[...])
+        return jnp.concatenate([grad_keys, grad_values], axis=1)
 
     def side_grad_copy(step, seq):
         return send_to(
@@ -1056,38 +1112,87 @@
             here.below,
         )
 
+    two = ref["two_grads"]
+
+    def hands_down(step):
+        return (me >= 2 * step) & (here.has_above | (step == 1))
+
+    def upper_grad_copy(seq):
+        return send_to(
+            ref["upper_grad_out"].at[seq],
+            ref["upper_grad_in"].at[seq],
+            ref["upper_send"].at[seq],
+            ref["upper_recv"].at[seq],
+            here.above,
+        )
+
+    def send_side(step, seq):
+        side_out[step, rows_of(seq)] = two[pl.ds(tile, tile)].astype(jnp.bfloat16)
+        side_grad_copy(step, seq).start()
+
     def find_grads(seq):
         rows = rows_of(seq)
+        query_n[...] = query_t[seq].T
+        grad_heads_n[...] = grad_heads_t[heads_at(seq)].T
+
+        @pl.when(here.serves)
+        def _():
+            for what in range(4):
+                share_copy(what, seq).wait_recv()
+            upper_heads_t[...] = jnp.zeros_like(upper_heads_t)
+            for group in range(2):
+                for member in range(2):
+                    part = ref["upper_heads"][
+                        seq, pl.ds(group * pair + member * head_dim, head_dim)
+                    ]
+                    cols = pl.ds((2 * group + member) * tile, tile)
+                    upper_heads_t[pl.ds(group * head_dim, head_dim), cols] = part
+            upper_query_n[...] = ref["upper_query_t"][seq].T
+            upper_heads_n[...] = upper_heads_t[...].T
+            ref["upper_grad"][...] = jnp.zeros_like(ref["upper_grad"])
 
         def level(index, carry):
-            step = levels - 1 - index
-
-            @pl.when(me >= 2 * step)
+            step = levels - 2 - index
+
+            @pl.when(hands_down(step))
             def _():
-                line, side = grads_of(
-                    [block_of(me, step), block_of(here.beside_ctx, step)], seq
-                )
-                side_out[step, rows] = side.astype(jnp.bfloat16)
-                side_grad_copy(step, seq).start()
-                line_out[step - 1, rows] = line.astype(jnp.bfloat16)
+                blocks = [block_of(me, step), block_of(here.beside_ctx, step)]
+                two[...] = grads_of(blocks, seq)
+
+                @pl.when(here.serves)
+                def _():
+                    two[...] += grads_of(blocks, seq, True)
+
+                send_side(step, seq)
+                line_out[step - 1, rows] = two[pl.ds(0, tile)].astype(jnp.bfloat16)
 
             return carry
 
-        lax.fori_loop(0, levels - 1, level, 0)
+        lax.fori_loop(0, levels - 2, level, 0)
 
         @pl.when(comes_aside(0))
         def _():
-            own, side = grads_of([me, here.beside_ctx], seq)
-            side_out[0, rows] = side.astype(jnp.bfloat16)
-            side_grad_copy(0, seq).start()
-            own_grads[rows, :] = own
+            two[...] = grads_of([me, here.beside_ctx], seq)
 
         @pl.when(jnp.logical_not(comes_aside(0)))
         def _():
-            own_grads[rows, :] = grads_of([me], seq)[0]
+            two[pl.ds(0, tile)] = grads_of([me], seq)
+
+        @pl.when(here.serves)
+        def _():
+            ref["upper_grad_out"][seq] = ref["upper_grad"][...].astype(jnp.bfloat16)
+            upper_grad_copy(seq).start()
+
+        @pl.when(comes_aside(0))
+        def _():
+            send_side(0, seq)
+
+        own_grads[rows, :] = two[pl.ds(0, tile)]
+
+    gets_line = me < count - 4
 
     def send_down(step, seq):
-        @pl.when(me >= 2 * step)
+        @pl.when(hands_down(step))
         def _():
             rows = rows_of(seq)
             side_grad_copy(step, seq).wait_recv()
@@ -1095,14 +1200,14 @@
                 jnp.float32
             )
 
-            @pl.when(here.has_above)
+            @pl.when(gets_line)
             def _():
                 line_copy(step + 1, seq).wait_recv()
                 line_out[step - 1, rows] = (
                     total + line_in[step, rows].astype(jnp.float32)
                 ).astype(jnp.bfloat16)
 
-            @pl.when(jnp.logical_not(here.has_above))
+            @pl.when(jnp.logical_not(gets_line))
             def _():
                 line_out[step - 1, rows] = total.astype(jnp.bfloat16)
 
@@ -1126,6 +1231,12 @@
 
     def project_back(seq):
         rows = rows_of(seq)
+
+        @pl.when(here.top)
+        def _():
+            upper_grad_copy(seq).wait_recv()
+            grad_query_t[seq] += ref["upper_grad_in"][seq].astype(jnp.float32)
+
         for group in range(2):
             grads = grad_query_t[seq, group] * (head_dim**-0.5)
             grads = jnp.concatenate([grads[:, :tile], grads[:, tile:]], axis=0).T
@@ -1166,11 +1277,6 @@
             jnp.bfloat16
         )
 
-    qkv_t[pl.ds(0, 2 * pair), :] = ref["w_query"][...].T
-    qkv_t[pl.ds(2 * pair, pair), :] = ref["w_key"][...].T
-    qkv_t[pl.ds(3 * pair, pair), :] = ref["w_value"][...].T
-    ffn_sum.cross(sequences - 1)
-
     few, more, early = TICKS
 
     def ticks_before(turn_):
@@ -1180,19 +1286,29 @@
         @pl.when(turn_ < sequences)
         def _():
             prepare(turn_)
-            find_grads(turn_)
+
+        @pl.when((turn_ >= 1) & (turn_ <= sequences))
+        def _():
+            find_grads(turn_ - 1)
+
+        @pl.when(turn_ == 0)
+        def _():
+            ffn_sum.cross(sequences - 1)
+            qkv_t[pl.ds(0, 2 * pair), :] = ref["w_query"][...].T
+            qkv_t[pl.ds(2 * pair, pair), :] = ref["w_key"][...].T
+            qkv_t[pl.ds(3 * pair, pair), :] = ref["w_value"][...].T
 
         @pl.when((turn_ == 1) | (turn_ == 2))
         def _():
             ffn_sum.close(sequences - 3 + turn_)
 
-        @pl.when((turn_ >= 2) & (turn_ < sequences + 2))
+        @pl.when((turn_ >= 3) & (turn_ < sequences + 3))
         def _():
             def down(index, carry):
-                send_down(levels - 1 - index, turn_ - 2)
+                send_down(levels - 2 - index, turn_ - 3)
                 return carry
 
-            lax.fori_loop(0, levels - 1, down, 0)
+            lax.fori_loop(0, levels - 2, down, 0)
 
         for i in range(max(few, more)):
 
@@ -1213,14 +1329,14 @@
         def _():
             mlp_sum.close(turn_ - 3)
 
-        @pl.when(turn_ >= 4)
-        def _():
-            output_rows(turn_ - 4)
-            project_back(turn_ - 4)
-
         @pl.when(turn_ >= 5)
         def _():
-            wt_sum.cross(turn_ - 5)
+            output_rows(turn_ - 5)
+            project_back(turn_ - 5)
+
+        @pl.when(turn_ >= 6)
+        def _():
+            wt_sum.cross(turn_ - 6)
 
         for i in range(4):
 
@@ -1230,7 +1346,7 @@
 
         return carry
 
-    turns = sequences + 4
+    turns = sequences + 5
     lax.fori_loop(0, turns, grad_turn, 0)
     qkv.tick(0, 0, normed_t, grad_qkv, first=True)
     gains.start()
@@ -1238,9 +1354,31 @@
     stores.start(0)
     done = 3 + few * early + more * (turns - early)
     left_over = 3 * count - done
-    each = -(-left_over // last)
+    each = -(-left_over // (last - 1))
 
     def tail(step, carry):
+        @pl.when(step == 2)
+        def _():
+            gains.sum_ctx()
+
+        @pl.when(step == 3)
+        def _():
+            gains.sum_cores()
+
+        @pl.when(step == 4)
+        def _():
+            total = gains.sum_chips()
+            ref["attn_gain_sum"][...] = total[0:1]
+            ref["ffn_gain_sum"][...] = total[1:2]
+            folded = total[:, :pair]
+            folded = folded + pltpu.roll(folded, head_dim, 1)
+            ref["q_gain_sum"][...] = folded[2:3]
+            ref["k_gain_sum"][...] = folded[3:4]
+
+        @pl.when(step == last)
+        def _():
+            stores.start(1, 2, 3, 4, 5, 9, 10, 11, 12)
+
         for i in range(each):
             index = done + each * (step - 1) + i
 
@@ -1266,18 +1404,9 @@
 
         return carry
 
-    middle = min(4, last)
-    lax.fori_loop(1, middle, tail, 0)
-    total = gains.total()
-    ref["attn_gain_sum"][...] = total[0:1]
-    ref["ffn_gain_sum"][...] = total[1:2]
-    folded = total[:, :pair]
-    folded = folded + pltpu.roll(folded, head_dim, 1)
-    ref["q_gain_sum"][...] = folded[2:3]
-    ref["k_gain_sum"][...] = folded[3:4]
-    stores.start(9, 10, 11, 12)
-    lax.fori_loop(middle, last + 1, tail, 0)
-    stores.start(1, 2, 3, 4, 5, 6, 7, 8)
+    lax.fori_loop(1, count, tail, 0)
+    stores.start(6, 7, 8)
+    gains.finish()
     ffn_sum.finish(sequences, (0,))
     wt_sum.finish(sequences)
     mlp_sum.finish(sequences)
@@ -1313,19 +1442,33 @@
         @pl.when(goes_aside(step))
         def _():
             seg_side_copy(step).wait_send()
+
+        @pl.when(goes_aside(step))
+        def _():
             each_seq(lambda seq: side_copy(step, seq).wait_send())
 
-        @pl.when(comes_aside(step))
+        @pl.when((step > 0) & (step < levels - 1) & hands_down(step))
         def _():
             each_seq(lambda seq: side_grad_copy(step, seq).wait_send())
-
-        @pl.when((step > 0) & (me >= 2 * step))
-        def _():
             each_seq(lambda seq: line_copy(step, seq).wait_send())
 
         return carry
 
     lax.fori_loop(0, levels, drain, 0)
+
+    @pl.when(comes_aside(0))
+    def _():
+        each_seq(lambda seq: side_grad_copy(0, seq).wait_send())
+
+    @pl.when(here.top)
+    def _():
+        for what in range(4):
+            each_seq(lambda seq: share_copy(what, seq).wait_send())
+
+    @pl.when(here.serves)
+    def _():
+        each_seq(lambda seq: upper_grad_copy(seq).wait_send())
+
     stores.wait(*range(len(RESULTS)))
 
 
@@ -1393,10 +1536,19 @@
         "mlp_sum2": ((2, rows, width // 2), bf16),
         "deltas": ((sequences, 1, 4 * tile), f32),
         "own_grads": ((rows, 2 * pair), f32),
-        "side_in": ((levels, rows, 2 * pair), bf16),
-        "side_out": ((levels, rows, 2 * pair), bf16),
-        "line_in": ((levels - 1, rows, 2 * pair), bf16),
-        "line_out": ((levels - 1, rows, 2 * pair), bf16),
+        "side_in": ((levels - 1, rows, 2 * pair), bf16),
+        "side_out": ((levels - 1, rows, 2 * pair), bf16),
+        "line_in": ((levels - 2, rows, 2 * pair), bf16),
+        "line_out": ((levels - 2, rows, 2 * pair), bf16),
+        "two_grads": ((2 * tile, 2 * pair), f32),
+        "upper_query_t": ((sequences, pair, 4 * tile), bf16),
+        "upper_heads": ((sequences, 2 * pair, tile), bf16),
+        "upper_deltas": ((sequences, 1, 4 * tile), f32),
+        "stats_out": ((sequences, 8, 4 * tile), f32),
+        "stats_in": ((sequences, 8, 4 * tile), f32),
+        "upper_grad": ((2, head_dim, 2 * tile), f32),
+        "upper_grad_out": ((sequences, 2, head_dim, 2 * tile), bf16),
+        "upper_grad_in": ((sequences, 2, head_dim, 2 * tile), bf16),
         "ffn_sums": ((3, block, hidden), f32),
         "qkv_total": ((block, 4 * pair), f32),
         "gains0": ((count, 8, width), f32),
@@ -1422,10 +1574,14 @@
         "wt_recv": (3, sequences),
         "mlp_sum3": (3, sequences),
         "mlp_sum4": (3, sequences),
-        "side_grad_send": (levels, sequences),
-        "side_grad_recv": (levels, sequences),
-        "line_send": (levels - 1, sequences),
-        "line_recv": (levels - 1, sequences),
+        "side_grad_send": (levels - 1, sequences),
+        "side_grad_recv": (levels - 1, sequences),
+        "share_send": (4, sequences),
+        "share_recv": (4, sequences),
+        "upper_send": (sequences,),
+        "upper_recv": (sequences,),
+        "line_send": (levels - 2, sequences),
+        "line_recv": (levels - 2, sequences),
         "gains2": (count - 1,),
         "gains3": (count - 1,),
         "gains4": (2,),
@@ -1491,9 +1647,9 @@
     return (
         lax.axis_size("wt") == 4
         and count % 2 == 0
-        and count >= 4
+        and count >= 6
         and tile == 128
-        and sequences <= 8
+        and sequences <= 5
         and sequences * count <= 40
         and head_dim == 64
         and w_query.shape[1] == 4 * head_dim

time: 181 us -> 178 us (0.983)
  Pallas kernels: 179 us -> 176 us
    pallas_call x1, Pallas kernels: 175 us -> 173 us  [layer(): pl.pallas_call(partial(layer_kernel, count, names), out_shape=[jax.ShapeD...]
where the time goes in v8:
time: 178 us
  Pallas kernels  176 us (99%)
    pallas_call x1, Pallas kernels, layer(): pl.pallas_call(partial(layer_kernel, count, names), out_shape=[jax.ShapeD...  173 us
    pallas_call x1, Pallas kernels, hand_over(): pl.pallas_call(partial(hand_over_kernel, len(arrays)), out_shape=[jax.Sha...  3.74 us

profile of v8, /device:TPU:0, one launch (start us, length us, event | category | flops | bytes accessed | tf_op | source)
XLA Modules:
  0.0 178.2 jit_solution(15920911025523973745)
XLA Ops:
  0.7 172.6 %shard_map.246 = (bf16[640,1024]{1,0:T(8,128)(2,1)}, bf16[640,1024]{1,0:T(8,128)(2,1)}, f32[128,1152]{1,0:T(8,128)}, f32[128,1152]{1,0:T(8,128)}, f32[128,1152]{...) custom-call(s32[5,128]{1,0:T(8,128)} %refs_0_.1, ...), custom_call_target="tpu_custom_call" | custom-call | tf_op jit(solution)/shard_map/pallas_call | solution.py:1599
  173.2 3.7 %shard_map.247 = (bf16[640,1024]{1,0:T(8,128)(2,1)}, bf16[640,1024]{1,0:T(8,128)(2,1)}, f32[128,1152]{1,0:T(8,128)}, f32[128,1152]{1,0:T(8,128)}, f32[128,1152]{...) custom-call(bf16[640,1024]{1,0:T(8,128)(2,1)} %get-tuple-element.39., ...), custom_call_target="tpu_custom_call" | custom-call | tf_op jit(solution)/shard_map/pallas_call | solution.py:1626
  177.0 1.2 slice_bitcast_fusion

commit v9 on v8

--- a/solution.py
+++ b/solution.py
@@ -1609,20 +1609,32 @@
     return dict(zip(RESULTS, arrays, strict=True))
 
 
+def pieces_of(shape):
+    return max(shape[0] // 128, 1) if shape[0] % 128 == 0 else 1
+
+
 def hand_over_kernel(count, *refs):
     sources, targets, staged = refs[:count], refs[count : 2 * count], refs[2 * count : 3 * count]
-    loads = Mover(list(zip(sources, staged, strict=True)), refs[3 * count])
-    stores = Mover(list(zip(staged, targets, strict=True)), refs[3 * count + 1])
-    loads.start(*range(count))
-    for i in range(count):
+    ways_in, ways_out = [], []
+    for source, target, stage in zip(sources, targets, staged, strict=True):
+        parts = pieces_of(source.shape)
+        size = source.shape[0] // parts
+        for part in range(parts):
+            rows = pl.ds(part * size, size)
+            ways_in.append((source.at[rows], stage.at[rows]))
+            ways_out.append((stage.at[rows], target.at[rows]))
+    loads, stores = Mover(ways_in, refs[3 * count]), Mover(ways_out, refs[3 * count + 1])
+    every = range(len(ways_in))
+    loads.start(*every)
+    for i in every:
         loads.wait(i)
         stores.start(i)
-    stores.wait(*range(count))
+    stores.wait(*every)
 
 
 def hand_over(arrays):
     anywhere = pl.BlockSpec(memory_space=pl.ANY)
-    dma = pltpu.SemaphoreType.DMA((len(arrays),))
+    dma = pltpu.SemaphoreType.DMA((sum(pieces_of(array.shape) for array in arrays),))
     return pl.pallas_call(
         partial(hand_over_kernel, len(arrays)),
         out_shape=[jax.ShapeDtypeStruct(array.shape, array.dtype) for array in arrays],

time: 178 us -> 179 us (level)
  no operation moved by 1% of the time
where the time goes in v9:
time: 179 us
  Pallas kernels  177 us (99%)
    pallas_call x1, Pallas kernels, layer(): pl.pallas_call(partial(layer_kernel, count, names), out_shape=[jax.ShapeD...  173 us
    pallas_call x1, Pallas kernels, hand_over(): pl.pallas_call(partial(hand_over_kernel, len(arrays)), out_shape=[jax.Sha...  4.44 us

profile of v9, /device:TPU:0, one launch (start us, length us, event | category | flops | bytes accessed | tf_op | source)
XLA Modules:
  0.0 178.9 jit_solution(6815705119193294491)
XLA Ops:
  0.7 172.6 %shard_map.246 = (bf16[640,1024]{1,0:T(8,128)(2,1)}, bf16[640,1024]{1,0:T(8,128)(2,1)}, f32[128,1152]{1,0:T(8,128)}, f32[128,1152]{1,0:T(8,128)}, f32[128,1152]{...) custom-call(s32[5,128]{1,0:T(8,128)} %refs_0_.1, ...), custom_call_target="tpu_custom_call" | custom-call | tf_op jit(solution)/shard_map/pallas_call | solution.py:1599
  173.2 4.4 %shard_map.247 = (bf16[640,1024]{1,0:T(8,128)(2,1)}, bf16[640,1024]{1,0:T(8,128)(2,1)}, f32[128,1152]{1,0:T(8,128)}, f32[128,1152]{1,0:T(8,128)}, f32[128,1152]{...) custom-call(bf16[640,1024]{1,0:T(8,128)(2,1)} %get-tuple-element.39., ...), custom_call_target="tpu_custom_call" | custom-call | tf_op jit(solution)/shard_map/pallas_call | solution.py:1638
  177.7 1.2 slice_bitcast_fusion
